TPU v7x, 256 devices: a whole 4x4x8 slice. The times are simulated.
256 devices in a mesh: gz: 64 (over y_hi, z, x), gy: 4 (over y_lo, core).
Axes of the slice: x: 4, y: 4 (y_hi: 2, y_lo: 2; y = y_hi * 2 + y_lo), z: 8, core: 2. Of those that a mesh axis runs over, the one named last changes fastest.
Arguments:
- volume: float32 [256, 64, 2048], P('gz', 'gy'), may hold values from -10 to 10
- measured: float32 [64, 256, 2048], P('gz', None, 'gy'), may hold values from -48 to 48
- row_norm: float32 [64, 256, 2048], P('gz', None, 'gy'), may hold values from 4 to 40
- col_norm: float32 [256, 64, 2048], P('gz', 'gy'), may hold values from 8 to 800
- ray_weight: float32 [64, 64], P(None, 'gy'), may hold values from 0.5 to 1.5
- tiles: bfloat16 [16, 128, 128], replicated, may hold values from -0.5 to 0.5
- tile_kind: int32 [64, 16], replicated, may hold values from 0 to 15
- tile_band: int32 [64, 16], replicated, may hold values from 0 to 15, as said below
- band_start: int32 [64, 64], replicated, may hold values from 0 to 252, as said below
Outputs:
- smoothed: float32 [256, 64, 2048], P('gz', 'gy')
- residual: float32 [64, 256, 2048], P('gz', None, 'gy')
Inputs may be any that keep to these rules, and one draw needn't show every extreme that they name: Plane k of slab s lands on detector row band_start + k; each entry lies within 2 rows of s * 4; slab 0 starts at row 0 and the last slab ends at the last row. `tile_band`: each entry lies within 2 of its x tile's own index; x tile 0 maps to detector tile 0 and the last x tile to the last detector tile.
All inputs are finite; a program needn't handle non-finite values.
Results may differ from a plain program's by a relative error of at most 0.0015.
Values may be sent and summed in bfloat16 or wider, within the bound.
No kernel may reach another device: no remote copies, remote signals or barrier semaphores. Data moves between devices by JAX's collectives and lax.ppermute only.
A program may use at most 192 MiB of HBM per device.

v0:
```python
import math

import jax
import jax.numpy as jnp
from jax import lax
from jax.sharding import PartitionSpec as P

PASSES = 3


EPS_TV = 0.01
EPS_NORM = 1e-06
RELAX = 1.0
TV_ALPHA = 0.2


def extended_2(value, sides, width):
    for axis, dim in sides:
        devices, length = (lax.axis_size(axis), value.shape[dim])
        up = [(i, (i + 1) % devices) for i in range(devices - 1)]
        down = [(j, i) for i, j in up]
        last = lax.slice_in_dim(value, length - width, length, axis=dim)
        leading = lax.slice_in_dim(value, 0, width, axis=dim)
        before = lax.ppermute(last, axis, up)
        after = lax.ppermute(leading, axis, down)
        value = jnp.concatenate([before, value, after], axis=dim)
    return value


def per_device(
    volume, measured, row_norm, col_norm, ray_weight, tiles, tile_kind, tile_band, band_start
):
    planes, rows_here, width = volume.shape
    tile_size = tiles.shape[1]
    xtiles = width // tile_size
    angle_count = tile_kind.shape[0]
    group = math.gcd(angle_count, 8)
    groups = angle_count // group
    slab_count = lax.axis_size("gz")
    slab_index = lax.axis_index("gz")
    block_count = lax.axis_size("gy")
    block_index = lax.axis_index("gy")
    detector_tiles = jnp.arange(xtiles, dtype=jnp.int32)
    ray_part = jnp.einsum(
        "ay,zyx->azx", ray_weight, volume, precision=lax.Precision.HIGHEST
    ).astype(jnp.bfloat16)
    kind_groups = tile_kind.reshape(groups, group, xtiles)
    band_groups = tile_band.reshape(groups, group, xtiles)

    def project(inputs):
        ray_sums, tile_kinds, band_tiles = inputs
        chosen = jnp.take(tiles, tile_kinds, axis=0)
        products = jnp.einsum(
            "gzjc,gjcd->gzjd",
            ray_sums.reshape(group, planes, xtiles, tile_size),
            chosen,
            preferred_element_type=jnp.float32,
        )
        onehot = (band_tiles[:, :, None] == detector_tiles[None, None, :]).astype(jnp.float32)
        placed = jnp.einsum("gzjd,gjt->gztd", products, onehot, precision=lax.Precision.HIGHEST)
        return placed.reshape(group, planes, width)

    partial_proj = lax.map(
        project, (ray_part.reshape(groups, group, planes, width), kind_groups, band_groups)
    )
    partial_proj = partial_proj.reshape(angle_count, planes, width)
    owner_rows = lax.all_to_all(partial_proj, "gz", split_axis=0, concat_axis=1, tiled=True)
    owner_cols = lax.psum_scatter(owner_rows, "gy", scatter_dimension=2, tiled=True)
    total_rows = planes * slab_count
    starts = lax.dynamic_index_in_dim(band_start, slab_index, 0, keepdims=False)
    row_ids = jnp.arange(total_rows, dtype=jnp.int32)
    landing = jnp.take(starts, row_ids // planes) + row_ids % planes
    placement = (row_ids[:, None] == landing[None, :]).astype(jnp.float32)
    projection = jnp.dot(placement, owner_cols[0], precision=lax.Precision.HIGHEST)
    residual = (measured[0] - projection) / row_norm[0]
    band_resid = jnp.dot(placement.T, residual, precision=lax.Precision.HIGHEST).astype(
        jnp.bfloat16
    )
    slab_rows = lax.all_to_all(band_resid[None], "gz", split_axis=1, concat_axis=0, tiled=True)
    full_rows = lax.all_gather(slab_rows, "gy", axis=2, tiled=True)

    def back_project(inputs):
        band_rows, tile_kinds, band_tiles = inputs
        chosen = jnp.take(tiles, tile_kinds, axis=0)
        shaped = band_rows.reshape(group, planes, xtiles, tile_size)
        picked = jnp.take_along_axis(shaped, band_tiles[:, None, :, None], axis=2)
        spread = jnp.einsum("gzjc,gjdc->gzjd", picked, chosen, preferred_element_type=jnp.float32)
        return spread.reshape(group, planes, width)

    back_rows = lax.map(
        back_project, (full_rows.reshape(groups, group, planes, width), kind_groups, band_groups)
    )
    back_rows = back_rows.reshape(angle_count, planes, width)
    smeared = jnp.einsum("ay,azx->zyx", ray_weight, back_rows, precision=lax.Precision.HIGHEST)
    updated = volume + RELAX * smeared / col_norm
    change = updated - volume
    moved = jnp.sqrt(lax.psum(jnp.sum(change * change), ("gz", "gy")))
    step_size = TV_ALPHA * moved
    volume_now = updated
    for sweep in range(PASSES):
        extended = extended_2(volume_now, (("gz", 0), ("gy", 1)), 1)
        extended = jnp.pad(extended, ((0, 0), (0, 0), (1, 1)))
        z_cells = slab_index * planes + jnp.arange(planes + 2 * 1, dtype=jnp.int32) - 1
        y_cells = block_index * rows_here + jnp.arange(rows_here + 2 * 1, dtype=jnp.int32) - 1
        x_cells = jnp.arange(width + 2 * 1, dtype=jnp.int32) - 1
        z_inside = ((z_cells >= 0) & (z_cells < slab_count * planes)).astype(jnp.float32)
        y_inside = ((y_cells >= 0) & (y_cells < block_count * rows_here)).astype(jnp.float32)
        x_inside = ((x_cells >= 0) & (x_cells < width)).astype(jnp.float32)
        inside = z_inside[:, None, None] * y_inside[None, :, None] * x_inside[None, None, :]
        lower = extended[:-1, :-1, :-1]
        diff_z = extended[1:, :-1, :-1] - lower
        diff_y = extended[:-1, 1:, :-1] - lower
        diff_x = extended[:-1, :-1, 1:] - lower
        magnitude = jnp.sqrt(diff_z * diff_z + diff_y * diff_y + diff_x * diff_x + EPS_TV)
        inside_q = inside[:-1, :-1, :-1]
        flux_z = diff_z / magnitude * inside_q
        flux_y = diff_y / magnitude * inside_q
        flux_x = diff_x / magnitude * inside_q
        gradient = -(flux_z + flux_y + flux_x)[1:, 1:, 1:]
        gradient = gradient + flux_z[:-1, 1:, 1:]
        gradient = gradient + flux_y[1:, :-1, 1:]
        gradient = gradient + flux_x[1:, 1:, :-1]
        own_sum = jnp.sum(gradient * gradient)
        grad_total = jnp.sqrt(lax.psum(own_sum, ("gz", "gy")) + EPS_NORM)
        factor = step_size / grad_total
        smoothed = (extended[1:-1, 1:-1, 1:-1] - factor * gradient) * inside[1:-1, 1:-1, 1:-1]
        volume_now, inside = (smoothed, inside[1:-1, 1:-1, 1:-1])
    return (volume_now, residual[None])


def solution(mesh):
    placed = (
        P("gz", "gy", None),
        P("gz", None, "gy"),
        P("gz", None, "gy"),
        P("gz", "gy", None),
        P(None, "gy"),
        P(),
        P(),
        P(),
        P(),
    )
    return jax.shard_map(
        per_device,
        mesh=mesh,
        in_specs=placed,
        out_specs=(P("gz", "gy", None), P("gz", None, "gy")),
        check_vma=False,
    )
```

profile of v0, /device:TPU:1, one launch (start us, length us, event | category | flops | bytes accessed | tf_op | source)
XLA Modules:
  0.0 634.3 jit_solution(15205065706096711680)
XLA Ops:
  8.8 3.9 fusion.32
  13.7 63.6 %while.22 = (s32[]{:T(128)}, f32[8,8,4,2048]{3,2,1,0:T(4,128)S(1)}, s32[8,8,16]{2,1,0:T(8,128)S(1)}, s32[8,8,16]{2,1,0:T(8,128)S(1)}, bf16[16,128,128]{2,1,0:T(8...) while((s32[]{:T(128)}, f32[8,8,4,2048]{3,2,1,0:T(4,128)S(1)}, ...), condition=%wide.region_1.3_spmd.clone, body=%wide.region_0.2_spmd.clone.sunk | while | flops 31461120 | bytes 14820189 | solution.py:63
  77.3 64.1 %all_to_all.24 = f32[64,4,2048]{2,1,0:T(4,128)} all-to-all(f32[64,4,2048]{2,1,0:T(4,128)S(1)} %bitcast.111), channel_id=1, replica_groups=mesh['gz'=64,'gy'=4] {'gz'}, dimensions={0} | all-to-all | bytes 4194304 | tf_op jit(solution)/shard_map/all_to_all | solution.py:67
  146.4 27.5 %reduce-scatter.2.cloned.1.call-done = f32[1,256,512]{2,1,0:T(8,128)} async-done(((f32[1,256,2048]{2,1,0:T(8,128)}), f32[1,256,512]{2,1,0:T(8,128)}) %reduce-scatter.2.cloned.1.call-update) | async-done | bytes 524304 | tf_op jit(solution)/shard_map/reduce_scatter | solution.py:68
  180.0 24.5 %all_to_all.25 = bf16[64,2,1024]{2,1,0:T(2,128)(2,1)S(1)} all-to-all(bf16[64,2,1024]{2,1,0:T(2,128)(2,1)S(1)} %reshape.302), channel_id=1, replica_groups=mesh['gz'=64,'gy'=4] {'gz'}, dimensions={0} | all-to-all | bytes 524288 | tf_op jit(solution)/shard_map/all_to_all | solution.py:79
  207.1 19.3 %all-gather.2.cloned.1.call-done = bf16[64,4,2048]{2,1,0:T(4,128)(2,1)} async-done(((bf16[64,4,512]{2,1,0:T(4,128)(2,1)}), bf16[64,4,2048]{2,1,0:T(4,128)(2,1)}) %all-gather.2.cloned.1.call-update) | async-done | bytes 1048592 | tf_op jit(solution)/shard_map/all_gather | solution.py:80
  226.9 78.1 %while.21 = (s32[]{:T(128)}, f32[8,8,4,2048]{3,2,1,0:T(4,128)S(1)}, s32[8,8,16]{2,1,0:T(8,128)S(1)}, bf16[16,128,128]{2,1,0:T(8,128)(2,1)S(1)}, s32[8,8,16]{2,1,...) while((s32[]{:T(128)}, f32[8,8,4,2048]{3,2,1,0:T(4,128)S(1)}, s32[8,8,16]{2,1,0:T(8,128)S(1)}, ...), condition=%wide.region_4.6_spmd, body=%wide.region_3.5_spmd.sunk | while | flops 18943488 | bytes 13513565 | solution.py:90
  232.1 4.6 fusion.70
  241.8 4.6 fusion.70
  251.6 4.6 fusion.70
  261.4 4.6 fusion.70
  271.1 4.6 fusion.70
  280.9 4.6 fusion.70
  290.6 4.6 fusion.70
  300.4 4.6 fusion.70
  306.3 4.6 multiply_reduce_fusion.3
  310.9 3.6 collective-permute-start
  317.3 3.8 collective-permute-done.1
  321.1 4.3 collective-permute-start.2
  334.2 81.2 %all-reduce.3 = (f32[]{:T(128)}, f32[]{:T(128)}) all-reduce(f32[]{:T(128)} %get-tuple-element.173, f32[]{:T(128)} %get-tuple-element.150), channel_id=1, replica_groups=mesh['gz'=64,'gy'=4] {'gz','gy'}, use_global_device_ids=true, to_apply=%region_6.8 | all-reduce | flops 2 | bytes 16 | tf_op jit(solution)/shard_map/psum | solution.py:97
  422.4 3.6 collective-permute-done.5
  438.3 82.6 %psum.30 = f32[]{:T(128)} all-reduce(f32[]{:T(128)} %get-tuple-element.146), channel_id=1, replica_groups=mesh['gz'=64,'gy'=4] {'gz','gy'}, use_global_device_ids=true, to_apply=%region_10.12 | all-reduce | flops 1 | bytes 8 | tf_op jit(solution)/shard_map/psum | solution.py:124
  527.2 3.6 collective-permute-done.9
  543.1 82.6 %psum.31 = f32[]{:T(128)} all-reduce(f32[]{:T(128)} %get-tuple-element.142), channel_id=1, replica_groups=mesh['gz'=64,'gy'=4] {'gz','gy'}, use_global_device_ids=true, to_apply=%region_12.14 | all-reduce | flops 1 | bytes 8 | tf_op jit(solution)/shard_map/psum | solution.py:124
  (228 shorter events, 170.4 us)
Async XLA Ops:
  7.2 137.3 %copy-start = (s32[64,64]{1,0:T(8,128)S(1)}, s32[64,64]{1,0:T(8,128)}, u32[]{:S(2)}) copy-start(s32[64,64]{1,0:T(8,128)} %param.23) | copy-start | bytes 49156
  7.2 166.7 %reduce-scatter.2.cloned.1.call-start = ((), (), s32[]{:S(2)}) async-start(), calls=%async_computation.3 | async-start | bytes 2621440 | tf_op jit(solution)/shard_map/reduce_scatter | solution.py:68
  12.7 1.0 copy-start.1
  144.4 29.5 %copy-start.5 = (f32[1,256,512]{2,1,0:T(8,128)S(1)}, f32[1,256,512]{2,1,0:T(8,128)}, u32[]{:S(2)}) copy-start(f32[1,256,512]{2,1,0:T(8,128)} %param.17) | copy-start | bytes 1572868
  144.4 29.5 %copy-start.6 = (f32[1,256,512]{2,1,0:T(8,128)S(1)}, f32[1,256,512]{2,1,0:T(8,128)}, u32[]{:S(2)}) copy-start(f32[1,256,512]{2,1,0:T(8,128)} %param.16) | copy-start | bytes 1572868
  144.4 82.0 %all-gather.2.cloned.1.call-start = ((), (), s32[]{:S(2)}) async-start(), calls=%async_computation.4 | async-start | bytes 1310720 | tf_op jit(solution)/shard_map/all_gather | solution.py:80
  175.4 0.8 copy-start.4
  226.9 79.5 %copy-start.3 = (f32[4,16,2048]{2,1,0:T(8,128)S(1)}, f32[4,16,2048]{2,1,0:T(8,128)}, u32[]{:S(2)}) copy-start(f32[4,16,2048]{2,1,0:T(8,128)} %param.15) | copy-start | bytes 1572868
  226.9 79.4 %copy-start.7 = (f32[64,16]{0,1:T(8,128)S(1)}, f32[64,16]{0,1:T(8,128)}, u32[]{:S(2)}) copy-start(f32[64,16]{0,1:T(8,128)} %param.19) | copy-start | bytes 12292
  305.0 1.4 copy-start.2
  310.9 6.4 %collective-permute-start = (f32[1,16,2048]{2,1,0:T(8,128)S(1)}, f32[1,16,2048]{2,1,0:T(8,128)S(1)}, u32[]{:S(2)}, u32[]{:S(2)}) collective-permute-start(f32[1,16,2048]{2,1,0:T(8,128)S(1)} %get-tuple-element.171), channel_id=1, source_target_pairs={{0,4},{4,8},{8,12},{12,16},{16,20},{20,24},{24,28},{28,32},{32,36}... | collective-permute-start | bytes 393224 | tf_op jit(solution)/shard_map/ppermute | solution.py:24
  314.6 6.5 %collective-permute-start.1 = (f32[1,16,2048]{2,1,0:T(8,128)S(1)}, f32[1,16,2048]{2,1,0:T(8,128)S(1)}, u32[]{:S(2)}, u32[]{:S(2)}) collective-permute-start(f32[1,16,2048]{2,1,0:T(8,128)S(1)} %get-tuple-element.172), channel_id=1, source_target_pairs={{4,0},{8,4},{12,8},{16,12},{20,16},{24,20},{28,24},{32,28},{36,32}... | collective-permute-start | bytes 393224 | tf_op jit(solution)/shard_map/ppermute | solution.py:25
  321.1 6.4 %collective-permute-start.2 = (f32[6,1,2048]{2,1,0:T(1,128)S(1)}, f32[6,1,2048]{2,1,0:T(1,128)S(1)}, u32[]{:S(2)}, u32[]{:S(2)}) collective-permute-start(f32[6,1,2048]{2,1,0:T(1,128)S(1)} %get-tuple-element.165), channel_id=1, source_target_pairs={{0,1},{1,2},{2,3},{4,5},{5,6},{6,7},{8,9},{9,10},{10,11},{12,13},{... | collective-permute-start | bytes 147464 | tf_op jit(solution)/shard_map/ppermute | solution.py:24
  325.5 5.4 collective-permute-start.3
  417.1 5.3 collective-permute-start.4
  420.3 5.7 collective-permute-start.5
  426.0 5.7 collective-permute-start.6
  429.6 5.4 collective-permute-start.7
  522.0 5.3 collective-permute-start.8
  525.1 5.7 collective-permute-start.9
  530.9 5.5 collective-permute-start.10
  534.4 5.4 collective-permute-start.11
Sparse Core Ops, SparseCore 0:
  144.5 29.3 reduce-scatter.1
  207.2 19.1 all-gather.1
where the time goes:
time: 636 us; the launch traced here: 634 us
  blocking collectives  335 us (53%)
  local copies, waits for them, and re-layouts  87.7 us (14%)
  matrix products  77 us (12%)
  waiting for transfers between devices  70.8 us (11%)
  starting transfers between devices  31.2 us (5%)
  between operations  17.3 us (3%)
  other arithmetic  14.7 us (2%)
    psum x2, blocking collectives, per_device(): grad_total = jnp.sqrt(lax.psum(own_sum, ('gz', 'gy')) + EPS_NORM)  165 us
    psum x1, blocking collectives, per_device(): moved = jnp.sqrt(lax.psum(jnp.sum(change * change), ('gz', 'gy')))  81.2 us
    all_to_all x1, blocking collectives, per_device(): lax.all_to_all(partial_proj, 'gz', split_axis=0, concat_axis=1, tiled=True)  64.1 us
    dot_general x8, matrix products, back_project(): jnp.einsum('gzjc,gjdc->gzjd', picked, chosen, preferred_element_type=jnp....  36.9 us
    dot_general x8, matrix products, project(): jnp.einsum('gzjc,gjcd->gzjd', ray_sums.reshape(group, planes, xtiles, til...  27.5 us
    reduce_scatter x1, waiting for transfers between devices, per_device(): lax.psum_scatter(owner_rows, 'gy', scatter_dimension=2, tiled=True)  27.5 us
    all_to_all x1, blocking collectives, per_device(): lax.all_to_all(band_resid[None], 'gz', split_axis=1, concat_axis=0, tiled...  24.5 us
    gather x8, local copies, waits for them, and re-layouts, back_project(): chosen = jnp.take(tiles, tile_kinds, axis=0)  24.4 us
  transfers between devices with their start and end apart: 14, of which 11 were waited for; matrix products, arithmetic and copies ran while one was open for 0% of the time, Pallas kernels for 0%

commit v1 on v0

v1 whole, which is shorter than its diff:
```python
import jax
import jax.numpy as jnp
from jax import lax
from jax.experimental import pallas as pl
from jax.experimental.pallas import tpu as pltpu
from jax.sharding import PartitionSpec as P

PASSES = 3
EPS_TV = 0.01
EPS_NORM = 1e-06
RELAX = 1.0
TV_ALPHA = 0.2

F32 = jnp.float32
BF16 = jnp.bfloat16
VMEM = pl.BlockSpec(memory_space=pltpu.VMEM)

PLANES, ROWS, HALO, TILE, XT, NK, ANGLES = 4, 16, 8, 128, 16, 16, 64
EXT = ROWS + HALO
WIDTH = XT * TILE
QUARTER = 4
WINDOW = 8
REACH = 10
SLOTS = 8


def iota(shape, dim):
    return lax.broadcasted_iota(jnp.int32, shape, dim)


def onehot(condition, dtype=F32):
    return jnp.where(condition, 1.0, 0.0).astype(dtype)


def dot(a, b, transposed=False):
    dims = (((1,), (1 if transposed else 0,)), ((), ()))
    return lax.dot_general(a, b, dims, preferred_element_type=F32)


def pieces(value, count):
    out = []
    for _ in range(count):
        part = value.astype(BF16)
        out.append(part)
        value = value - part.astype(F32)
    return out


def spread_lanes(parts, order):
    width = parts[0].shape[1]
    lanes = len(order) * width
    copy = onehot(iota((width, lanes), 1) % width == iota((width, lanes), 0), BF16)
    group = iota((parts[0].shape[0], lanes), 1) // width
    total = None
    for index, part in enumerate(parts):
        chosen = group == -1
        for place, which in enumerate(order):
            if which == index:
                chosen = chosen | (group == place)
        term = jnp.where(chosen, dot(part, copy), 0.0)
        total = term if total is None else total + term
    return total.astype(BF16)


def code_column(code, tile):
    lane = iota(code.shape, 1)
    column = jnp.sum(jnp.where(lane == tile, code, 0.0), axis=1, keepdims=True)
    return jnp.broadcast_to(column.astype(jnp.int32), (code.shape[0], TILE))


def slot_masks(kind):
    return [onehot((kind % SLOTS) == k, BF16) for k in range(SLOTS)]


def pick_half(wide, kind):
    return jnp.where(kind >= SLOTS, wide[:, TILE:], wide[:, :TILE])


def project_kernel(
    own, near, far, farnear, w_own, w_near, kinds, bands, tiles, out, weights_out,
    sums, lhs, rhs, acc,
):
    block = lax.axis_index("gy")
    core = block % 2
    first = block * 2 + jnp.where(block >= 2, 2, 0)
    start = pl.multiple_of(first * TILE, TILE)
    inner = pl.multiple_of(core * 2 * TILE, TILE)
    span = WINDOW * TILE
    w_far = far[:, REACH * TILE : (REACH + 1) * TILE][:, :ROWS]
    w_farnear = farnear[:, REACH * TILE : (REACH + 1) * TILE][:, :ROWS]
    sources = (
        (own, start, w_own[...], 0),
        (near, start, w_near[...], 1),
        (far, inner, w_far, 2),
        (farnear, inner, w_farnear, 3),
    )
    row = iota((EXT, ROWS), 0)
    wanted = block * ROWS + row - jnp.where(row >= ROWS + HALO // 2, EXT, 0)
    picked = jnp.zeros((EXT, ANGLES), F32)
    for order, (ref, offset, weight, flip) in enumerate(sources):
        w_parts = pieces(weight, 3)
        left = spread_lanes(w_parts, (0, 0, 1, 1, 0, 2))
        held = (block ^ flip) * ROWS + iota((EXT, ROWS), 1)
        choose = onehot(held == wanted, BF16)
        for part in w_parts:
            picked = picked + dot(choose, part, transposed=True)
        for z in range(PLANES):
            v = pieces(ref[z * ROWS : (z + 1) * ROWS, pl.ds(offset, span)], 3)
            right = jnp.concatenate([v[0], v[1], v[0], v[1], v[2], v[0]], axis=0)
            rays = dot(left, right).astype(BF16).astype(F32)
            here = sums.at[z * ANGLES : (z + 1) * ANGLES, :]
            here[...] = rays if order == 0 else here[...] + rays
    weights_out[...] = picked
    for k in range(SLOTS):
        rhs[k * TILE : (k + 1) * TILE, :TILE] = tiles[k]
        rhs[k * TILE : (k + 1) * TILE, TILE:] = tiles[k + SLOTS]
    acc[...] = jnp.zeros_like(acc)
    code = (kinds[...] + NK * bands[...]).astype(F32)
    rows = PLANES * ANGLES
    for j in range(WINDOW):
        column = code_column(code, first + j)
        kind, band = column % NK, column // NK
        masks = slot_masks(kind)
        for z in range(PLANES):
            part = sums[z * ANGLES : (z + 1) * ANGLES, j * TILE : (j + 1) * TILE]
            for p, piece in enumerate(pieces(part, 2)):
                at = (p * PLANES + z) * ANGLES
                for k in range(SLOTS):
                    lhs[at : at + ANGLES, k * TILE : (k + 1) * TILE] = piece * masks[k]
        wide = dot(lhs[...], rhs[...])
        wide = wide[:rows] + wide[rows:]
        for z in range(PLANES):
            tile = pick_half(wide[z * ANGLES : (z + 1) * ANGLES], kind)
            for t in range(QUARTER):
                here = acc.at[t, z * ANGLES : (z + 1) * ANGLES, :]
                here[...] += jnp.where(band == block * QUARTER + t, tile, 0.0)
    for t in range(QUARTER):
        for z in range(PLANES):
            out[pl.ds(t * PLANES + z, ANGLES, stride=XT), :] = acc[
                t, z * ANGLES : (z + 1) * ANGLES, :
            ]


def residual_kernel(rows_in, measured, norm, starts, resid, band_out, gathered, placed):
    angle = lax.axis_index("gz")
    slabs = starts.shape[1]
    total = PLANES * slabs
    mine = jnp.where(iota(starts.shape, 0) == angle, starts[...], 0).astype(F32)
    first = jnp.sum(mine, axis=0, keepdims=True)
    spread = onehot(iota((slabs, total), 1) % slabs == iota((slabs, total), 0), BF16)
    land = dot(jnp.broadcast_to(first, (8, slabs)).astype(BF16), spread)[:1]
    land = land.astype(jnp.int32) + iota((1, total), 1) // slabs
    place = onehot(iota((total, total), 0) == land, BF16)
    r = iota((total, slabs), 0)
    own = jnp.where(r % slabs == iota((total, slabs), 1), first, 0.0)
    land_col = jnp.sum(own, axis=1, keepdims=True).astype(jnp.int32)
    land_col = land_col + iota((total, 1), 0) // slabs
    take = onehot(iota((total, total), 1) == land_col, BF16)
    for t in range(QUARTER):
        for z in range(PLANES):
            gathered[z * slabs : (z + 1) * slabs, t * TILE : (t + 1) * TILE] = rows_in[
                pl.ds(t * PLANES + z, slabs, stride=XT), :
            ]
    projection = None
    for part in pieces(gathered[...], 3):
        term = dot(place, part)
        projection = term if projection is None else projection + term
    residual = (measured[...] - projection) / norm[...]
    resid[...] = residual
    rows = dot(take, residual.astype(BF16))
    for t in range(QUARTER):
        for z in range(PLANES):
            placed[pl.ds(t * PLANES + z, slabs, stride=XT), :] = rows[
                z * slabs : (z + 1) * slabs, t * TILE : (t + 1) * TILE
            ]
    band_out[...] = placed[...].astype(BF16)


def inside_rows(block):
    row = iota((EXT, 1), 0)
    y = block * ROWS + row - jnp.where(row >= ROWS + HALO // 2, EXT, 0)
    return (y >= 0) & (y < lax.axis_size("gy") * ROWS)


def back_kernel(
    band0, band1, band2, band3, kinds, bands, tiles, weights, volume, norm, after, before,
    updated, first_plane, last_plane, moved, flat, rows_by_tile, lhs, rhs,
):
    block = lax.axis_index("gy")
    for flip, ref in enumerate((band0, band1, band2, band3)):
        flat[...] = ref[...].astype(F32)
        for t in range(QUARTER):
            for z in range(PLANES):
                rows_by_tile[(block ^ flip) * QUARTER + t, z * ANGLES : (z + 1) * ANGLES, :] = (
                    flat[pl.ds(t * PLANES + z, ANGLES, stride=XT), :].astype(BF16)
                )
    for k in range(SLOTS):
        rhs[k * TILE : (k + 1) * TILE, :TILE] = tiles[k]
        rhs[k * TILE : (k + 1) * TILE, TILE:] = tiles[k + SLOTS]
    left = spread_lanes(pieces(weights[...], 2), (0, 0, 1))
    code = (kinds[...] + NK * bands[...]).astype(F32)
    inside = inside_rows(block)
    low = iota((HALO, 2 * TILE), 0) < HALO // 2
    squares = jnp.zeros((ROWS, 2 * TILE), F32)
    for pair in range(XT // 2):
        backs = []
        for j in (2 * pair, 2 * pair + 1):
            column = code_column(code, j)
            kind, band = column % NK, column // NK
            masks = slot_masks(kind)
            near = [t for t in range(j - 2, j + 3) if 0 <= t < XT]
            at_band = [onehot(band == t, BF16) for t in near]
            for z in range(PLANES):
                here = slice(z * ANGLES, (z + 1) * ANGLES)
                chosen = None
                for t, mask in zip(near, at_band):
                    term = rows_by_tile[t, here, :] * mask
                    chosen = term if chosen is None else chosen + term
                for k in range(SLOTS):
                    lhs[here, k * TILE : (k + 1) * TILE] = chosen * masks[k]
            wide = dot(lhs[...], rhs[...])
            backs.append(
                [pick_half(wide[z * ANGLES : (z + 1) * ANGLES], kind) for z in range(PLANES)]
            )
        lanes = slice(2 * pair * TILE, (2 * pair + 2) * TILE)
        for z in range(PLANES):
            back = jnp.concatenate([backs[0][z], backs[1][z]], axis=1)
            b = pieces(back, 2)
            smeared = dot(left, jnp.concatenate([b[0], b[1], b[0]], axis=0))
            up, down = after[z, :, lanes], before[z, :, lanes]
            v = jnp.concatenate(
                [volume[z, :, lanes], jnp.where(low, up, pltpu.roll(down, HALO // 2, 0))], axis=0
            )
            n = jnp.concatenate(
                [norm[z, :, lanes], jnp.where(low, pltpu.roll(up, HALO // 2, 0), down)], axis=0
            )
            new = v + RELAX * smeared / jnp.where(inside, n, 1.0)
            updated[z, :, lanes] = new
            if z == 0:
                first_plane[0, :, lanes] = new
            if z == PLANES - 1:
                last_plane[0, :, lanes] = new
            change = (new - v)[:ROWS]
            squares = squares + change * change
    total = jnp.sum(squares, axis=(0, 1), keepdims=True)
    moved[...] = jnp.where(iota((8, TILE), 1) == 0, total, 0.0)


def gradient_plane(here, above, flux_z_below, inside):
    lane = iota(here.shape, 1)
    ahead = jnp.where(lane == WIDTH - 1, 0.0, pltpu.roll(here, WIDTH - 1, 1))
    dz = above - here
    dy = pltpu.roll(here, EXT - 1, 0) - here
    dx = ahead - here
    scale = lax.rsqrt(dz * dz + dy * dy + dx * dx + EPS_TV)
    scale = jnp.where(inside, scale, 0.0)
    qz, qy, qx = dz * scale, dy * scale, dx * scale
    gradient = flux_z_below - (qz + qy + qx)
    gradient = gradient + pltpu.roll(qy, 1, 0)
    gradient = gradient + jnp.where(lane == 0, 0.0, pltpu.roll(qx, 1, 1))
    return jnp.where(inside, gradient, 0.0), qz


def flux_below(below, here, inside):
    lane = iota(here.shape, 1)
    ahead = jnp.where(lane == WIDTH - 1, 0.0, pltpu.roll(below, WIDTH - 1, 1))
    dz = here - below
    dy = pltpu.roll(below, EXT - 1, 0) - below
    dx = ahead - below
    scale = lax.rsqrt(dz * dz + dy * dy + dx * dx + EPS_TV)
    return jnp.where(inside, dz * scale, 0.0)


def write_gradients(planes, moved, grad, grad_first, grad_last, parts):
    inside = inside_rows(lax.axis_index("gy"))
    exists = inside & (lax.axis_index("gz") > 0)
    flux = flux_below(planes(0), planes(1), exists)
    squares = jnp.zeros((ROWS, WIDTH), F32)
    for z in range(PLANES):
        g, flux = gradient_plane(planes(z + 1), planes(z + 2), flux, inside)
        grad[z] = g
        if z == 0:
            grad_first[0] = g
        if z == PLANES - 1:
            grad_last[0] = g
        squares = squares + g[:ROWS] * g[:ROWS]
    total = jnp.sum(squares, axis=(0, 1), keepdims=True)
    row = moved[:1] + jnp.where(iota((1, TILE), 1) == 1, total, 0.0)
    parts[...] = jnp.broadcast_to(row, parts.shape)


def first_gradient_kernel(f, below, above, moved, grad, grad_first, grad_last, parts):
    def planes(i):
        return below[0] if i == 0 else above[0] if i == PLANES + 1 else f[i - 1]

    write_gradients(planes, moved, grad, grad_first, grad_last, parts)


def step_length(sums):
    row = jnp.sum(sums[...], axis=0, keepdims=True)
    lane = iota(row.shape, 1)
    moved = jnp.sum(jnp.where(lane == 0, row, 0.0), axis=1, keepdims=True)
    total = jnp.sum(jnp.where(lane == 1, row, 0.0), axis=1, keepdims=True)
    return TV_ALPHA * jnp.sqrt(moved) / jnp.sqrt(total + EPS_NORM)


def next_gradient_kernel(
    sums, f, below, above, g, g_below, g_above, moved,
    f_out, below_out, above_out, grad, grad_first, grad_last, parts,
):
    step = step_length(sums)
    below_out[0] = below[0] - step * g_below[0]
    above_out[0] = above[0] - step * g_above[0]
    for z in range(PLANES):
        f_out[z] = f[z] - step * g[z]

    def planes(i):
        return below_out[0] if i == 0 else above_out[0] if i == PLANES + 1 else f_out[i - 1]

    write_gradients(planes, moved, grad, grad_first, grad_last, parts)


def last_step_kernel(sums, f, g, out):
    step = step_length(sums)
    for z in range(PLANES):
        out[z] = f[z, :ROWS] - step * g[z, :ROWS]


def call(kernel, shapes, args, scratch=(), flops=0):
    shapes = [jax.ShapeDtypeStruct(shape, dtype) for shape, dtype in shapes]
    moved = sum(a.size * a.dtype.itemsize for a in list(args) + shapes)
    out = pl.pallas_call(
        kernel,
        out_shape=shapes,
        in_specs=[VMEM] * len(args),
        out_specs=[VMEM] * len(shapes),
        scratch_shapes=list(scratch),
        compiler_params=pltpu.CompilerParams(vmem_limit_bytes=40 * 1024 * 1024),
        cost_estimate=pl.CostEstimate(flops=flops, bytes_accessed=moved, transcendentals=0),
    )(*args)
    return out


def per_device(
    volume, measured, row_norm, col_norm, ray_weight, tiles, tile_kind, tile_band, band_start
):
    slabs, blocks = lax.axis_size("gz"), lax.axis_size("gy")
    block = lax.axis_index("gy")
    other_chip = [(i, i ^ 2) for i in range(blocks)]
    other_core = [(i, i ^ 1) for i in range(blocks)]
    flat = volume.reshape(PLANES * ROWS, WIDTH)
    away = jnp.where(block >= 2, 0, (XT - REACH) * TILE)
    lanes = jnp.pad(ray_weight, ((0, 0), (0, TILE - ROWS)))
    outgoing = lax.dynamic_slice_in_dim(flat, away, REACH * TILE, axis=1)
    far = lax.ppermute(jnp.concatenate([outgoing, lanes], axis=1), "gy", other_chip)
    near = lax.ppermute(flat, "gy", other_core)
    w_near = lax.ppermute(ray_weight, "gy", other_core)
    farnear = lax.ppermute(far, "gy", other_core)
    half = HALO // 2
    to_before = jnp.concatenate([volume[:, :half], col_norm[:, :half]], axis=1)
    to_after = jnp.concatenate([volume[:, ROWS - half :], col_norm[:, ROWS - half :]], axis=1)
    after = lax.ppermute(to_before, "gy", [(i + 1, i) for i in range(blocks - 1)])
    before = lax.ppermute(to_after, "gy", [(i, i + 1) for i in range(blocks - 1)])

    rows = PLANES * ANGLES
    chunk = ANGLES * QUARTER * PLANES
    slab_proj, weights = call(
        project_kernel,
        [((chunk, TILE), F32), ((EXT, ANGLES), F32)],
        (flat, near, far, farnear, ray_weight, w_near, tile_kind, tile_band, tiles),
        [
            pltpu.VMEM((rows, WINDOW * TILE), F32),
            pltpu.VMEM((2 * rows, SLOTS * TILE), BF16),
            pltpu.VMEM((SLOTS * TILE, 2 * TILE), BF16),
            pltpu.VMEM((QUARTER, rows, TILE), F32),
        ],
        flops=2 * WINDOW * 2 * rows * SLOTS * TILE * 2 * TILE,
    )
    chunks = slab_proj.reshape(slabs, XT, TILE)
    owner_rows = lax.all_to_all(chunks, "gz", split_axis=0, concat_axis=0, tiled=True)
    residual, band_resid = call(
        residual_kernel,
        [(measured.shape[1:], F32), ((chunk, TILE), BF16)],
        (owner_rows.reshape(chunk, TILE), measured[0], row_norm[0], band_start),
        [pltpu.VMEM((rows, QUARTER * TILE), F32), pltpu.VMEM((chunk, TILE), F32)],
        flops=2 * 4 * rows * rows * QUARTER * TILE,
    )
    chunks = band_resid.reshape(slabs, XT, TILE)
    bands = lax.all_to_all(chunks, "gz", split_axis=0, concat_axis=0, tiled=True)
    bands = bands.reshape(chunk, TILE)
    bands_far = lax.ppermute(bands, "gy", other_chip)
    bands_near = lax.ppermute(bands, "gy", other_core)
    bands_farnear = lax.ppermute(bands_far, "gy", other_core)

    plane = ((1, EXT, WIDTH), F32)
    block_ext = ((PLANES, EXT, WIDTH), F32)
    f, f_first, f_last, moved = call(
        back_kernel,
        [block_ext, plane, plane, ((8, TILE), F32)],
        (
            bands, bands_near, bands_far, bands_farnear, tile_kind, tile_band,
            jnp.swapaxes(tiles, 1, 2), weights, volume, col_norm, after, before,
        ),
        [
            pltpu.VMEM((chunk, TILE), F32),
            pltpu.VMEM((XT, rows, TILE), BF16),
            pltpu.VMEM((rows, SLOTS * TILE), BF16),
            pltpu.VMEM((SLOTS * TILE, 2 * TILE), BF16),
        ],
        flops=2 * XT * rows * SLOTS * TILE * 2 * TILE,
    )
    upward = [(i, i + 1) for i in range(slabs - 1)]
    downward = [(i + 1, i) for i in range(slabs - 1)]

    def neighbours(first, last):
        return lax.ppermute(last, "gz", upward), lax.ppermute(first, "gz", downward)

    def summed(parts):
        return lax.all_to_all(parts, ("gz", "gy"), split_axis=0, concat_axis=0, tiled=True)

    partial = ((slabs * blocks, TILE), F32)
    work = 40 * PLANES * EXT * WIDTH
    below, above = neighbours(f_first, f_last)
    g, g_first, g_last, parts = call(
        first_gradient_kernel,
        [block_ext, plane, plane, partial],
        (f, below, above, moved),
        flops=work,
    )
    for _ in range(PASSES - 1):
        g_below, g_above = neighbours(g_first, g_last)
        sums = summed(parts)
        f, below, above, g, g_first, g_last, parts = call(
            next_gradient_kernel,
            [block_ext, plane, plane, block_ext, plane, plane, partial],
            (sums, f, below, above, g, g_below, g_above, moved),
            flops=work,
        )
    (smoothed,) = call(
        last_step_kernel,
        [(volume.shape, F32)],
        (summed(parts), f, g),
        flops=2 * volume.size,
    )
    return smoothed, residual[None]


def solution(mesh):
    placed = (
        P("gz", "gy", None),
        P("gz", None, "gy"),
        P("gz", None, "gy"),
        P("gz", "gy", None),
        P(None, "gy"),
        P(),
        P(),
        P(),
        P(),
    )
    return jax.shard_map(
        per_device,
        mesh=mesh,
        in_specs=placed,
        out_specs=(P("gz", "gy", None), P("gz", None, "gy")),
        check_vma=False,
    )
```

time: 636 us -> 205 us (0.32)
  blocking collectives: 335 us -> 59.9 us
  matrix products: 77 us -> 0 us
  local copies, waits for them, and re-layouts: 87.7 us -> 13.1 us
  starting transfers between devices: 31.2 us -> 65.6 us
  waiting for transfers between devices: 70.8 us -> 42.4 us
  Pallas kernels: 0 us -> 20.4 us
  between operations: 17.3 us -> 0.89 us
  other arithmetic: 14.7 us -> 1.54 us
    psum x3 -> x0, blocking collectives: 247 us -> none  [the longest x2 165 us: per_device(): grad_total = jnp.sqrt(lax.psum(own_sum, ('gz', 'gy')) + EPS_NORM)]
    dot_general x28 -> x0, matrix products: 77 us -> none  [the longest x8 36.9 us: back_project(): jnp.einsum('gzjc,gjdc->gzjd', picked, chosen, preferred_element_type=jnp....]
    gather x33 -> x0, local copies, waits for them, and re-layouts: 58.5 us -> none  [the longest x8 24.4 us: back_project(): chosen = jnp.take(tiles, tile_kinds, axis=0)]
    all_to_all x0 -> x3, starting transfers between devices: none -> 36.4 us  [the longest x2 29.5 us: summed(): lax.all_to_all(parts, ('gz', 'gy'), split_axis=0, concat_axis=0, tiled=True)]
    all_to_all x2, blocking collectives: 88.6 us -> 59.9 us  [the longest x1 32.1 us: per_device(): lax.all_to_all(chunks, 'gz', split_axis=0, concat_axis=0, tiled=True)]
    reduce_scatter x1 -> x0, waiting for transfers between devices: 27.5 us -> none  [per_device(): lax.psum_scatter(owner_rows, 'gy', scatter_dimension=2, tiled=True)]
    pallas_call x0 -> x7, Pallas kernels: none -> 20.4 us  [call(): pl.pallas_call(kernel, out_shape=shapes, in_specs=[VMEM] * len(args), out...]
    all_gather x1 -> x0, waiting for transfers between devices: 19.3 us -> none  [per_device(): full_rows = lax.all_gather(slab_rows, 'gy', axis=2, tiled=True)]
  transfers between devices with their start and end apart: 14 -> 18, of which waited for: 11 -> 13; matrix products, arithmetic and copies ran while one was open for 0% -> 1% of each run, Pallas kernels for 0% -> 0%
where the time goes in v1:
time: 205 us; the launch traced here: 204 us
  starting transfers between devices  65.6 us (32%)
  blocking collectives  59.9 us (29%)
  waiting for transfers between devices  42.4 us (21%)
  Pallas kernels  20.4 us (10%)
  local copies, waits for them, and re-layouts  13.1 us (6%)
    all_to_all x1, blocking collectives, per_device(): lax.all_to_all(chunks, 'gz', split_axis=0, concat_axis=0, tiled=True)  32.1 us
    all_to_all x2, starting transfers between devices, summed(): lax.all_to_all(parts, ('gz', 'gy'), split_axis=0, concat_axis=0, tiled=True)  29.5 us
    all_to_all x1, blocking collectives, summed(): lax.all_to_all(parts, ('gz', 'gy'), split_axis=0, concat_axis=0, tiled=True)  27.8 us
    pallas_call x7, Pallas kernels, call(): pl.pallas_call(kernel, out_shape=shapes, in_specs=[VMEM] * len(args), out...  20.4 us
    all_to_all x1, waiting for transfers between devices, per_device(): lax.all_to_all(chunks, 'gz', split_axis=0, concat_axis=0, tiled=True)  12.1 us
    unnamed x50, local copies, waits for them, and re-layouts  12 us
    ppermute x3, waiting for transfers between devices, neighbours(): lax.ppermute(first, 'gz', downward)  9.75 us
    ppermute x3, waiting for transfers between devices, neighbours(): lax.ppermute(last, 'gz', upward)  8.93 us
  transfers between devices with their start and end apart: 18, of which 13 were waited for; matrix products, arithmetic and copies ran while one was open for 1% of the time, Pallas kernels for 0%

profile of v1, /device:TPU:1, one launch (start us, length us, event | category | flops | bytes accessed | tf_op | source)
XLA Modules:
  0.0 203.8 jit_solution(6328134103688755928)
XLA Ops:
  2.5 2.2 %collective-permute-start.1 = (f32[64,1408]{1,0:T(8,128)S(1)}, f32[64,1408]{1,0:T(8,128)S(1)}, u32[]{:S(2)}, u32[]{:S(2)}) collective-permute-start(f32[64,1408]{1,0:T(8,128)S(1)} %select_maximum_fusion), channel_id=1, source_target_pairs={{0,2},{1,3},{2,0},{3,1},{4,6},{5,7},{6,4},{7,5},{8,10},{9,11},{10,... | collective-permute-start | bytes 1081352 | tf_op jit(solution)/shard_map/ppermute | solution.py:355
  4.8 2.0 collective-permute-start
  6.8 4.9 %collective-permute-done.1.far = f32[64,1408]{1,0:T(8,128)S(1)} collective-permute-done((f32[64,1408]{1,0:T(8,128)S(1)}, f32[64,1408]{1,0:T(8,128)S(1)}, u32[]{:S(2)}, u32[]{:S(2)}) %collective-permute-start.1) | collective-permute-done | bytes 360480 | tf_op jit(solution)/shard_map/ppermute | solution.py:355
  11.6 2.5 %collective-permute-start.2 = (f32[64,1408]{1,0:T(8,128)S(1)}, f32[64,1408]{1,0:T(8,128)S(1)}, u32[]{:S(2)}, u32[]{:S(2)}) collective-permute-start(f32[64,1408]{1,0:T(8,128)S(1)} %collective-permute-done.1.far), channel_id=1, source_target_pairs={{0,1},{1,0},{2,3},{3,2},{4,5},{5,4},{6,7},{7,6},{8,9},{9,8},{10,11... | collective-permute-start | bytes 1081352 | tf_op jit(solution)/shard_map/ppermute | solution.py:358
  15.5 5.3 %shard_map.104 = (f32[1024,128]{1,0:T(8,128)S(1)}, f32[24,64]{1,0:T(8,128)S(1)}) custom-call(f32[64,2048]{1,0:T(8,128)S(1)} %bitcast.24, f32[64,2048]{1,0:T(8,128)S(1)} %collective-permute-done.near, f32[64,1408]{1,0:T(8,128)S(1)} %collective-permute-done.1.far, f32[64,1408]{1,0:T(8,128)S(1)} %collective-permute-done.2.farnear, f32[64,16]{1,0:T(8,128)S(1)} %copy.19.w_own, ...), custom_call_target="tpu_custom_call" | custom-call | flops 2147483648 | bytes 2840576 | tf_op jit(solution)/shard_map/pallas_call | solution.py:332
  20.8 32.1 %all_to_all.43 = f32[64,16,128]{2,1,0:T(8,128)S(1)} all-to-all(f32[64,16,128]{2,1,0:T(8,128)S(1)} %bitcast.31), channel_id=1, replica_groups=mesh['gz'=64,'gy'=4] {'gz'}, dimensions={0} | all-to-all | bytes 1048576 | tf_op jit(solution)/shard_map/all_to_all | solution.py:380
  54.5 6.9 %all-to-all-start.1 = ((bf16[64,16,128]{2,1,0:T(8,128)(2,1)}), bf16[64,16,128]{2,1,0:T(8,128)(2,1)S(1)}, u32[]{:S(2)}, u32[]{:S(2)}) async-start(bf16[64,16,128]{2,1,0:T(8,128)(2,1)} %bitcast.5), calls=%async_computation.1 | async-start | bytes 524288 | tf_op jit(solution)/shard_map/all_to_all | solution.py:389
  61.5 12.1 %all-to-all-done.1 = bf16[64,16,128]{2,1,0:T(8,128)(2,1)S(1)} async-done(((bf16[64,16,128]{2,1,0:T(8,128)(2,1)}), bf16[64,16,128]{2,1,0:T(8,128)(2,1)S(1)}, u32[]{:S(2)}, u32[]{:S(2)}) %all-to-all-start.1) | async-done | bytes 262176 | tf_op jit(solution)/shard_map/all_to_all | solution.py:389
  74.8 5.7 %collective-permute-start.7 = (f32[4,8,2048]{2,1,0:T(8,128)}, f32[4,8,2048]{2,1,0:T(8,128)S(1)}, u32[]{:S(2)}, u32[]{:S(2)}) collective-permute-start(f32[4,8,2048]{2,1,0:T(8,128)} %pad_maximum_fusion), channel_id=1, source_target_pairs={{1,0},{2,1},{3,2},{5,4},{6,5},{7,6},{9,8},{10,9},{11,10},{13,12},{... | collective-permute-start | bytes 786440 | tf_op jit(solution)/shard_map/ppermute | solution.py:362
  81.3 2.9 %collective-permute-start.8 = (f32[4,8,2048]{2,1,0:T(8,128)}, f32[4,8,2048]{2,1,0:T(8,128)S(1)}, u32[]{:S(2)}, u32[]{:S(2)}) collective-permute-start(f32[4,8,2048]{2,1,0:T(8,128)} %pad_maximum_fusion.1), channel_id=1, source_target_pairs={{0,1},{1,2},{2,3},{4,5},{5,6},{6,7},{8,9},{9,10},{10,11},{12,13},{... | collective-permute-start | bytes 786440 | tf_op jit(solution)/shard_map/ppermute | solution.py:363
  85.7 2.0 collective-permute-done.8.before
  89.4 7.8 %shard_map.106 = (f32[4,24,2048]{2,1,0:T(8,128)S(1)}, f32[1,24,2048]{2,1,0:T(8,128)S(1)}, f32[1,24,2048]{2,1,0:T(8,128)S(1)}, f32[8,128]{1,0:T(8,128)S(1)}) custom-call(bf16[1024,128]{1,0:T(8,128)(2,1)S(1)} %bitcast.34, bf16[1024,128]{1,0:T(8,128)(2,1)S(1)} %copy-done.18, bf16[1024,128]{1,0:T(8,128)(2,1)S(1)} %collective-permute-done.5.band2, ...), custom_call_target="tpu_custom_call" | custom-call | flops 2147483648 | bytes 4343808 | tf_op jit(solution)/shard_map/pallas_call | solution.py:332
  97.2 2.2 %collective-permute-start.9 = (f32[1,24,2048]{2,1,0:T(8,128)S(1)}, f32[1,24,2048]{2,1,0:T(8,128)S(1)}, u32[]{:S(2)}, u32[]{:S(2)}) collective-permute-start(f32[1,24,2048]{2,1,0:T(8,128)S(1)} %get-tuple-element.28), channel_id=1, source_target_pairs={{0,4},{4,8},{8,12},{12,16},{16,20},{20,24},{24,28},{28,32},{32,36}... | collective-permute-start | bytes 589832 | tf_op jit(solution)/shard_map/ppermute | solution.py:416
  100.8 2.0 collective-permute-done.9.below
  102.8 4.1 %collective-permute-done.10.above = f32[1,24,2048]{2,1,0:T(8,128)S(1)} collective-permute-done((f32[1,24,2048]{2,1,0:T(8,128)S(1)}, f32[1,24,2048]{2,1,0:T(8,128)S(1)}, u32[]{:S(2)}, u32[]{:S(2)}) %collective-permute-start.10) | collective-permute-done | bytes 196640 | tf_op jit(solution)/shard_map/ppermute | solution.py:416
  108.5 14.2 %all-to-all-start.2 = ((f32[256,1,128]{2,1,0:T(1,128)}), f32[256,1,128]{2,1,0:T(1,128)S(1)}, u32[]{:S(2)}, u32[]{:S(2)}) async-start(f32[256,1,128]{2,1,0:T(1,128)} %bitcast.9), calls=%async_computation.2 | async-start | bytes 262144 | tf_op jit(solution)/shard_map/all_to_all | solution.py:419
  122.7 3.3 %collective-permute-start.11 = (f32[1,24,2048]{2,1,0:T(8,128)S(1)}, f32[1,24,2048]{2,1,0:T(8,128)S(1)}, u32[]{:S(2)}, u32[]{:S(2)}) collective-permute-start(f32[1,24,2048]{2,1,0:T(8,128)S(1)} %get-tuple-element.33), channel_id=1, source_target_pairs={{0,4},{4,8},{8,12},{12,16},{16,20},{20,24},{24,28},{28,32},{32,36}... | collective-permute-start | bytes 589832 | tf_op jit(solution)/shard_map/ppermute | solution.py:416
  127.3 3.4 %collective-permute-done.11.g_below = f32[1,24,2048]{2,1,0:T(8,128)S(1)} collective-permute-done((f32[1,24,2048]{2,1,0:T(8,128)S(1)}, f32[1,24,2048]{2,1,0:T(8,128)S(1)}, u32[]{:S(2)}, u32[]{:S(2)}) %collective-permute-start.11) | collective-permute-done | bytes 196640 | tf_op jit(solution)/shard_map/ppermute | solution.py:416
  131.4 2.6 %collective-permute-done.12.g_above = f32[1,24,2048]{2,1,0:T(8,128)S(1)} collective-permute-done((f32[1,24,2048]{2,1,0:T(8,128)S(1)}, f32[1,24,2048]{2,1,0:T(8,128)S(1)}, u32[]{:S(2)}, u32[]{:S(2)}) %collective-permute-start.12) | collective-permute-done | bytes 196640 | tf_op jit(solution)/shard_map/ppermute | solution.py:416
  143.8 15.4 %all-to-all-start.3 = ((f32[256,1,128]{2,1,0:T(1,128)}), f32[256,1,128]{2,1,0:T(1,128)S(1)}, u32[]{:S(2)}, u32[]{:S(2)}) async-start(f32[256,1,128]{2,1,0:T(1,128)} %bitcast.35), calls=%async_computation.3 | async-start | bytes 262144 | tf_op jit(solution)/shard_map/all_to_all | solution.py:419
  159.1 3.3 %collective-permute-start.13 = (f32[1,24,2048]{2,1,0:T(8,128)}, f32[1,24,2048]{2,1,0:T(8,128)S(1)}, u32[]{:S(2)}, u32[]{:S(2)}) collective-permute-start(f32[1,24,2048]{2,1,0:T(8,128)} %copy-done.20), channel_id=1, source_target_pairs={{0,4},{4,8},{8,12},{12,16},{16,20},{20,24},{24,28},{28,32},{32,36}... | collective-permute-start | bytes 589832 | tf_op jit(solution)/shard_map/ppermute | solution.py:416
  164.0 3.5 %collective-permute-done.13.g_below = f32[1,24,2048]{2,1,0:T(8,128)S(1)} collective-permute-done((f32[1,24,2048]{2,1,0:T(8,128)}, f32[1,24,2048]{2,1,0:T(8,128)S(1)}, u32[]{:S(2)}, u32[]{:S(2)}) %collective-permute-start.13) | collective-permute-done | bytes 196640 | tf_op jit(solution)/shard_map/ppermute | solution.py:416
  167.5 3.0 %collective-permute-done.14.g_above = f32[1,24,2048]{2,1,0:T(8,128)S(1)} collective-permute-done((f32[1,24,2048]{2,1,0:T(8,128)}, f32[1,24,2048]{2,1,0:T(8,128)S(1)}, u32[]{:S(2)}, u32[]{:S(2)}) %collective-permute-start.14) | collective-permute-done | bytes 196640 | tf_op jit(solution)/shard_map/ppermute | solution.py:416
  175.0 27.8 %all_to_all.44 = f32[256,1,128]{2,1,0:T(1,128)S(1)} all-to-all(f32[256,1,128]{2,1,0:T(1,128)S(1)} %bitcast.36), channel_id=1, replica_groups=mesh['gz'=64,'gy'=4] {'gz','gy'}, dimensions={0} | all-to-all | bytes 262144 | tf_op jit(solution)/shard_map/all_to_all | solution.py:419
  (77 shorter events, 31.7 us)
Async XLA Ops:
  1.4 14.1 %copy-start.5 = (bf16[16,128,128]{2,1,0:T(8,128)(2,1)S(1)}, bf16[16,128,128]{2,1,0:T(8,128)(2,1)}, u32[]{:S(2)}) copy-start(bf16[16,128,128]{2,1,0:T(8,128)(2,1)} %tiles.1) | copy-start | bytes 1572868
  2.5 11.7 %copy-start.22 = (s32[64,16]{0,1:T(8,128)S(1)}, s32[64,16]{0,1:T(8,128)}, u32[]{:S(2)}) copy-start(s32[64,16]{0,1:T(8,128)} %param.16) | copy-start | bytes 12292
  2.5 9.1 %collective-permute-start.1 = (f32[64,1408]{1,0:T(8,128)S(1)}, f32[64,1408]{1,0:T(8,128)S(1)}, u32[]{:S(2)}, u32[]{:S(2)}) collective-permute-start(f32[64,1408]{1,0:T(8,128)S(1)} %select_maximum_fusion), channel_id=1, source_target_pairs={{0,2},{1,3},{2,0},{3,1},{4,6},{5,7},{6,4},{7,5},{8,10},{9,11},{10,... | collective-permute-start | bytes 1081352 | tf_op jit(solution)/shard_map/ppermute | solution.py:355
  4.8 10.7 %collective-permute-start = (f32[64,2048]{1,0:T(8,128)S(1)}, f32[64,2048]{1,0:T(8,128)S(1)}, u32[]{:S(2)}, u32[]{:S(2)}) collective-permute-start(f32[64,2048]{1,0:T(8,128)S(1)} %bitcast.23), channel_id=1, source_target_pairs={{0,1},{1,0},{2,3},{3,2},{4,5},{5,4},{6,7},{7,6},{8,9},{9,8},{10,11... | collective-permute-start | bytes 1572872 | tf_op jit(solution)/shard_map/ppermute | solution.py:356
  11.6 3.8 %collective-permute-start.2 = (f32[64,1408]{1,0:T(8,128)S(1)}, f32[64,1408]{1,0:T(8,128)S(1)}, u32[]{:S(2)}, u32[]{:S(2)}) collective-permute-start(f32[64,1408]{1,0:T(8,128)S(1)} %collective-permute-done.1.far), channel_id=1, source_target_pairs={{0,1},{1,0},{2,3},{3,2},{4,5},{5,4},{6,7},{7,6},{8,9},{9,8},{10,11... | collective-permute-start | bytes 1081352 | tf_op jit(solution)/shard_map/ppermute | solution.py:358
  14.1 1.3 collective-permute-start.3
  15.5 37.4 %copy-start.16 = (s32[64,64]{1,0:T(8,128)S(1)}, s32[64,64]{1,0:T(8,128)}, u32[]{:S(2)}) copy-start(s32[64,64]{1,0:T(8,128)} %starts.1) | copy-start | bytes 49156
  20.8 32.1 %copy-start.1 = (f32[1,256,512]{2,1,0:T(8,128)S(1)}, f32[1,256,512]{2,1,0:T(8,128)}, u32[]{:S(2)}) copy-start(f32[1,256,512]{2,1,0:T(8,128)} %param.10) | copy-start | bytes 1572868
  20.8 32.1 %copy-start.2 = (f32[1,256,512]{2,1,0:T(8,128)S(1)}, f32[1,256,512]{2,1,0:T(8,128)}, u32[]{:S(2)}) copy-start(f32[1,256,512]{2,1,0:T(8,128)} %param.11) | copy-start | bytes 1572868
  54.5 19.2 %all-to-all-start.1 = ((bf16[64,16,128]{2,1,0:T(8,128)(2,1)}), bf16[64,16,128]{2,1,0:T(8,128)(2,1)S(1)}, u32[]{:S(2)}, u32[]{:S(2)}) async-start(bf16[64,16,128]{2,1,0:T(8,128)(2,1)} %bitcast.5), calls=%async_computation.1 | async-start | bytes 524288 | tf_op jit(solution)/shard_map/all_to_all | solution.py:389
  73.6 10.6 %collective-permute-start.5 = (bf16[1024,128]{1,0:T(8,128)(2,1)S(1)}, bf16[1024,128]{1,0:T(8,128)(2,1)S(1)}, u32[]{:S(2)}, u32[]{:S(2)}) collective-permute-start(bf16[1024,128]{1,0:T(8,128)(2,1)S(1)} %bitcast.32), channel_id=1, source_target_pairs={{0,2},{1,3},{2,0},{3,1},{4,6},{5,7},{6,4},{7,5},{8,10},{9,11},{10,... | collective-permute-start | bytes 786440 | tf_op jit(solution)/shard_map/ppermute | solution.py:391
  74.8 10.9 %collective-permute-start.7 = (f32[4,8,2048]{2,1,0:T(8,128)}, f32[4,8,2048]{2,1,0:T(8,128)S(1)}, u32[]{:S(2)}, u32[]{:S(2)}) collective-permute-start(f32[4,8,2048]{2,1,0:T(8,128)} %pad_maximum_fusion), channel_id=1, source_target_pairs={{1,0},{2,1},{3,2},{5,4},{6,5},{7,6},{9,8},{10,9},{11,10},{13,12},{... | collective-permute-start | bytes 786440 | tf_op jit(solution)/shard_map/ppermute | solution.py:362
  81.3 6.5 %collective-permute-start.8 = (f32[4,8,2048]{2,1,0:T(8,128)}, f32[4,8,2048]{2,1,0:T(8,128)S(1)}, u32[]{:S(2)}, u32[]{:S(2)}) collective-permute-start(f32[4,8,2048]{2,1,0:T(8,128)} %pad_maximum_fusion.1), channel_id=1, source_target_pairs={{0,1},{1,2},{2,3},{4,5},{5,6},{6,7},{8,9},{9,10},{10,11},{12,13},{... | collective-permute-start | bytes 786440 | tf_op jit(solution)/shard_map/ppermute | solution.py:363
  84.1 3.6 %collective-permute-start.4 = (bf16[1024,128]{1,0:T(8,128)(2,1)S(1)}, bf16[1024,128]{1,0:T(8,128)(2,1)S(1)}, u32[]{:S(2)}, u32[]{:S(2)}) collective-permute-start(bf16[1024,128]{1,0:T(8,128)(2,1)S(1)} %bitcast.33), channel_id=1, source_target_pairs={{0,1},{1,0},{2,3},{3,2},{4,5},{5,4},{6,7},{7,6},{8,9},{9,8},{10,11... | collective-permute-start | bytes 786440 | tf_op jit(solution)/shard_map/ppermute | solution.py:392
  84.3 4.2 %collective-permute-start.6 = (bf16[1024,128]{1,0:T(8,128)(2,1)S(1)}, bf16[1024,128]{1,0:T(8,128)(2,1)}, u32[]{:S(2)}, u32[]{:S(2)}) collective-permute-start(bf16[1024,128]{1,0:T(8,128)(2,1)S(1)} %collective-permute-done.5.band2), channel_id=1, source_target_pairs={{0,1},{1,0},{2,3},{3,2},{4,5},{5,4},{6,7},{7,6},{8,9},{9,8},{10,11... | collective-permute-start | bytes 786440 | tf_op jit(solution)/shard_map/ppermute | solution.py:393
  97.2 5.5 %collective-permute-start.9 = (f32[1,24,2048]{2,1,0:T(8,128)S(1)}, f32[1,24,2048]{2,1,0:T(8,128)S(1)}, u32[]{:S(2)}, u32[]{:S(2)}) collective-permute-start(f32[1,24,2048]{2,1,0:T(8,128)S(1)} %get-tuple-element.28), channel_id=1, source_target_pairs={{0,4},{4,8},{8,12},{12,16},{16,20},{20,24},{24,28},{28,32},{32,36}... | collective-permute-start | bytes 589832 | tf_op jit(solution)/shard_map/ppermute | solution.py:416
  99.5 7.4 %collective-permute-start.10 = (f32[1,24,2048]{2,1,0:T(8,128)S(1)}, f32[1,24,2048]{2,1,0:T(8,128)S(1)}, u32[]{:S(2)}, u32[]{:S(2)}) collective-permute-start(f32[1,24,2048]{2,1,0:T(8,128)S(1)} %get-tuple-element.29), channel_id=1, source_target_pairs={{4,0},{8,4},{12,8},{16,12},{20,16},{24,20},{28,24},{32,28},{36,32}... | collective-permute-start | bytes 589832 | tf_op jit(solution)/shard_map/ppermute | solution.py:416
  108.5 27.3 %all-to-all-start.2 = ((f32[256,1,128]{2,1,0:T(1,128)}), f32[256,1,128]{2,1,0:T(1,128)S(1)}, u32[]{:S(2)}, u32[]{:S(2)}) async-start(f32[256,1,128]{2,1,0:T(1,128)} %bitcast.9), calls=%async_computation.2 | async-start | bytes 262144 | tf_op jit(solution)/shard_map/all_to_all | solution.py:419
  122.7 8.0 %collective-permute-start.11 = (f32[1,24,2048]{2,1,0:T(8,128)S(1)}, f32[1,24,2048]{2,1,0:T(8,128)S(1)}, u32[]{:S(2)}, u32[]{:S(2)}) collective-permute-start(f32[1,24,2048]{2,1,0:T(8,128)S(1)} %get-tuple-element.33), channel_id=1, source_target_pairs={{0,4},{4,8},{8,12},{12,16},{16,20},{20,24},{24,28},{28,32},{32,36}... | collective-permute-start | bytes 589832 | tf_op jit(solution)/shard_map/ppermute | solution.py:416
  126.0 8.0 %collective-permute-start.12 = (f32[1,24,2048]{2,1,0:T(8,128)S(1)}, f32[1,24,2048]{2,1,0:T(8,128)S(1)}, u32[]{:S(2)}, u32[]{:S(2)}) collective-permute-start(f32[1,24,2048]{2,1,0:T(8,128)S(1)} %get-tuple-element.34), channel_id=1, source_target_pairs={{4,0},{8,4},{12,8},{16,12},{20,16},{24,20},{28,24},{32,28},{36,32}... | collective-permute-start | bytes 589832 | tf_op jit(solution)/shard_map/ppermute | solution.py:416
  143.8 28.4 %copy-start.7 = (f32[1,24,2048]{2,1,0:T(8,128)S(1)}, f32[1,24,2048]{2,1,0:T(8,128)}, u32[]{:S(2)}) copy-start(f32[1,24,2048]{2,1,0:T(8,128)} %copy-done.6) | copy-start | bytes 589828
  143.8 28.4 %all-to-all-start.3 = ((f32[256,1,128]{2,1,0:T(1,128)}), f32[256,1,128]{2,1,0:T(1,128)S(1)}, u32[]{:S(2)}, u32[]{:S(2)}) async-start(f32[256,1,128]{2,1,0:T(1,128)} %bitcast.35), calls=%async_computation.3 | async-start | bytes 262144 | tf_op jit(solution)/shard_map/all_to_all | solution.py:419
  159.1 8.4 %collective-permute-start.13 = (f32[1,24,2048]{2,1,0:T(8,128)}, f32[1,24,2048]{2,1,0:T(8,128)S(1)}, u32[]{:S(2)}, u32[]{:S(2)}) collective-permute-start(f32[1,24,2048]{2,1,0:T(8,128)} %copy-done.20), channel_id=1, source_target_pairs={{0,4},{4,8},{8,12},{12,16},{16,20},{20,24},{24,28},{28,32},{32,36}... | collective-permute-start | bytes 589832 | tf_op jit(solution)/shard_map/ppermute | solution.py:416
  162.4 8.1 %collective-permute-start.14 = (f32[1,24,2048]{2,1,0:T(8,128)}, f32[1,24,2048]{2,1,0:T(8,128)S(1)}, u32[]{:S(2)}, u32[]{:S(2)}) collective-permute-start(f32[1,24,2048]{2,1,0:T(8,128)} %copy-done.19), channel_id=1, source_target_pairs={{4,0},{8,4},{12,8},{16,12},{20,16},{24,20},{28,24},{32,28},{36,32}... | collective-permute-start | bytes 589832 | tf_op jit(solution)/shard_map/ppermute | solution.py:416
  (17 other events, 31.6 us)

commit v2 on v1

--- a/solution.py
+++ b/solution.py
@@ -46,11 +46,11 @@
     return out
 
 
-def spread_lanes(parts, order):
-    width = parts[0].shape[1]
+def spread_lanes(parts, order, first, width):
+    rows, held = parts[0].shape
     lanes = len(order) * width
-    copy = onehot(iota((width, lanes), 1) % width == iota((width, lanes), 0), BF16)
-    group = iota((parts[0].shape[0], lanes), 1) // width
+    copy = onehot(iota((held, lanes), 1) % width + first == iota((held, lanes), 0), BF16)
+    group = iota((rows, lanes), 1) // width
     total = None
     for index, part in enumerate(parts):
         chosen = group == -1
@@ -62,6 +62,15 @@
     return total.astype(BF16)
 
 
+def start_fetches(pairs, arrived):
+    fetches = [
+        pltpu.make_async_copy(there, here, arrived.at[i]) for i, (there, here) in enumerate(pairs)
+    ]
+    for fetch in fetches:
+        fetch.start()
+    return fetches
+
+
 def code_column(code, tile):
     lane = iota(code.shape, 1)
     column = jnp.sum(jnp.where(lane == tile, code, 0.0), axis=1, keepdims=True)
@@ -77,45 +86,51 @@
 
 
 def project_kernel(
-    own, near, far, farnear, w_own, w_near, kinds, bands, tiles, out, weights_out,
-    sums, lhs, rhs, acc,
+    far, farnear, near, small, own, tiles, out, weights_out,
+    own_here, sums, lhs, rhs, acc, arrived,
 ):
     block = lax.axis_index("gy")
-    core = block % 2
     first = block * 2 + jnp.where(block >= 2, 2, 0)
-    start = pl.multiple_of(first * TILE, TILE)
-    inner = pl.multiple_of(core * 2 * TILE, TILE)
     span = WINDOW * TILE
-    w_far = far[:, REACH * TILE : (REACH + 1) * TILE][:, :ROWS]
-    w_farnear = farnear[:, REACH * TILE : (REACH + 1) * TILE][:, :ROWS]
-    sources = (
-        (own, start, w_own[...], 0),
-        (near, start, w_near[...], 1),
-        (far, inner, w_far, 2),
-        (farnear, inner, w_farnear, 3),
-    )
-    row = iota((EXT, ROWS), 0)
+    window = pl.ds(pl.multiple_of(first * TILE, TILE), span)
+    inner = pl.ds(pl.multiple_of(block % 2 * 2 * TILE, TILE), span)
+    fetches = start_fetches(
+        (
+            (own.at[:, window], own_here),
+            (tiles.at[:SLOTS], rhs.at[:, :, :TILE]),
+            (tiles.at[SLOTS:], rhs.at[:, :, TILE:]),
+        ),
+        arrived,
+    )
+    acc[...] = jnp.zeros_like(acc)
+    sources = ((far, 2, inner), (farnear, 3, inner), (near, 1, slice(0, span)), (own_here, 0, slice(0, span)))
+    weight = [ref[:ROWS, ref.shape[1] - TILE :][:, :ANGLES] for ref in (far, farnear, near)]
+    weight = pieces(jnp.concatenate([*weight, small[XT:]], axis=0).T, 3)
+    row = iota((EXT, 1), 0)
     wanted = block * ROWS + row - jnp.where(row >= ROWS + HALO // 2, EXT, 0)
+    lane = iota((EXT, ANGLES), 1)
+    held_row = jnp.zeros((EXT, ANGLES), jnp.int32)
+    for order, (_, flip, _) in enumerate(sources):
+        mine = lane // ROWS == order
+        held_row = held_row + jnp.where(mine, (block ^ flip) * ROWS + lane % ROWS, 0)
+    choose = onehot(held_row == wanted, BF16)
     picked = jnp.zeros((EXT, ANGLES), F32)
-    for order, (ref, offset, weight, flip) in enumerate(sources):
-        w_parts = pieces(weight, 3)
-        left = spread_lanes(w_parts, (0, 0, 1, 1, 0, 2))
-        held = (block ^ flip) * ROWS + iota((EXT, ROWS), 1)
-        choose = onehot(held == wanted, BF16)
-        for part in w_parts:
-            picked = picked + dot(choose, part, transposed=True)
-        for z in range(PLANES):
-            v = pieces(ref[z * ROWS : (z + 1) * ROWS, pl.ds(offset, span)], 3)
+    for part in weight:
+        picked = picked + dot(choose, part, transposed=True)
+    for order, (ref, _, lanes) in enumerate(sources):
+        if order == 3:
+            fetches[0].wait()
+        left = spread_lanes(weight, (0, 0, 1, 1, 0, 2), order * ROWS, ROWS)
+        for z in range(PLANES):
+            v = pieces(ref[z * ROWS : (z + 1) * ROWS, lanes], 3)
             right = jnp.concatenate([v[0], v[1], v[0], v[1], v[2], v[0]], axis=0)
             rays = dot(left, right).astype(BF16).astype(F32)
             here = sums.at[z * ANGLES : (z + 1) * ANGLES, :]
             here[...] = rays if order == 0 else here[...] + rays
     weights_out[...] = picked
-    for k in range(SLOTS):
-        rhs[k * TILE : (k + 1) * TILE, :TILE] = tiles[k]
-        rhs[k * TILE : (k + 1) * TILE, TILE:] = tiles[k + SLOTS]
-    acc[...] = jnp.zeros_like(acc)
-    code = (kinds[...] + NK * bands[...]).astype(F32)
+    for fetch in fetches[1:]:
+        fetch.wait()
+    code = small[:XT].T
     rows = PLANES * ANGLES
     for j in range(WINDOW):
         column = code_column(code, first + j)
@@ -127,7 +142,7 @@
                 at = (p * PLANES + z) * ANGLES
                 for k in range(SLOTS):
                     lhs[at : at + ANGLES, k * TILE : (k + 1) * TILE] = piece * masks[k]
-        wide = dot(lhs[...], rhs[...])
+        wide = dot(lhs[...], rhs[...].reshape(SLOTS * TILE, 2 * TILE))
         wide = wide[:rows] + wide[rows:]
         for z in range(PLANES):
             tile = pick_half(wide[z * ANGLES : (z + 1) * ANGLES], kind)
@@ -183,22 +198,38 @@
 
 
 def back_kernel(
-    band0, band1, band2, band3, kinds, bands, tiles, weights, volume, norm, after, before,
-    updated, first_plane, last_plane, moved, flat, rows_by_tile, lhs, rhs,
+    b0, b1, b2, b3, small, weights, tiles, volume, norm, after, before,
+    updated, first_planes, last_planes, moved,
+    flat, rows_by_tile, lhs, rhs,
+    volume_here, norm_here, after_here, before_here, arrived,
 ):
     block = lax.axis_index("gy")
-    for flip, ref in enumerate((band0, band1, band2, band3)):
+    fetches = start_fetches(
+        (
+            (tiles.at[:SLOTS], rhs.at[:, :, :TILE]),
+            (tiles.at[SLOTS:], rhs.at[:, :, TILE:]),
+            (volume, volume_here),
+            (norm, norm_here),
+            (after, after_here),
+            (before, before_here),
+        ),
+        arrived,
+    )
+    left = spread_lanes(pieces(weights[...], 2), (0, 0, 1), 0, ANGLES)
+
+    def arrange(flip, ref):
         flat[...] = ref[...].astype(F32)
         for t in range(QUARTER):
             for z in range(PLANES):
                 rows_by_tile[(block ^ flip) * QUARTER + t, z * ANGLES : (z + 1) * ANGLES, :] = (
                     flat[pl.ds(t * PLANES + z, ANGLES, stride=XT), :].astype(BF16)
                 )
-    for k in range(SLOTS):
-        rhs[k * TILE : (k + 1) * TILE, :TILE] = tiles[k]
-        rhs[k * TILE : (k + 1) * TILE, TILE:] = tiles[k + SLOTS]
-    left = spread_lanes(pieces(weights[...], 2), (0, 0, 1))
-    code = (kinds[...] + NK * bands[...]).astype(F32)
+
+    for flip, ref in enumerate((b0, b1, b2, b3)):
+        arrange(flip, ref)
+    for fetch in fetches:
+        fetch.wait()
+    code = small[:XT].T
     inside = inside_rows(block)
     low = iota((HALO, 2 * TILE), 0) < HALO // 2
     squares = jnp.zeros((ROWS, 2 * TILE), F32)
@@ -218,28 +249,28 @@
                     chosen = term if chosen is None else chosen + term
                 for k in range(SLOTS):
                     lhs[here, k * TILE : (k + 1) * TILE] = chosen * masks[k]
-            wide = dot(lhs[...], rhs[...])
+            wide = dot(lhs[...], rhs[...].reshape(SLOTS * TILE, 2 * TILE))
             backs.append(
                 [pick_half(wide[z * ANGLES : (z + 1) * ANGLES], kind) for z in range(PLANES)]
             )
-        lanes = slice(2 * pair * TILE, (2 * pair + 2) * TILE)
+        cut = slice(2 * pair * TILE, (2 * pair + 2) * TILE)
         for z in range(PLANES):
             back = jnp.concatenate([backs[0][z], backs[1][z]], axis=1)
             b = pieces(back, 2)
             smeared = dot(left, jnp.concatenate([b[0], b[1], b[0]], axis=0))
-            up, down = after[z, :, lanes], before[z, :, lanes]
+            up, down = after_here[z, :, cut], before_here[z, :, cut]
             v = jnp.concatenate(
-                [volume[z, :, lanes], jnp.where(low, up, pltpu.roll(down, HALO // 2, 0))], axis=0
+                [volume_here[z, :, cut], jnp.where(low, up, pltpu.roll(down, HALO // 2, 0))], axis=0
             )
             n = jnp.concatenate(
-                [norm[z, :, lanes], jnp.where(low, pltpu.roll(up, HALO // 2, 0), down)], axis=0
+                [norm_here[z, :, cut], jnp.where(low, pltpu.roll(up, HALO // 2, 0), down)], axis=0
             )
             new = v + RELAX * smeared / jnp.where(inside, n, 1.0)
-            updated[z, :, lanes] = new
-            if z == 0:
-                first_plane[0, :, lanes] = new
-            if z == PLANES - 1:
-                last_plane[0, :, lanes] = new
+            updated[z, :, cut] = new
+            if z < PASSES:
+                first_planes[z, :, cut] = new
+            if z >= PLANES - PASSES:
+                last_planes[z - (PLANES - PASSES), :, cut] = new
             change = (new - v)[:ROWS]
             squares = squares + change * change
     total = jnp.sum(squares, axis=(0, 1), keepdims=True)
@@ -271,29 +302,37 @@
     return jnp.where(inside, dz * scale, 0.0)
 
 
-def write_gradients(planes, moved, grad, grad_first, grad_last, parts):
-    inside = inside_rows(lax.axis_index("gy"))
-    exists = inside & (lax.axis_index("gz") > 0)
-    flux = flux_below(planes(0), planes(1), exists)
+def gradients(f, margin):
+    slab, slabs = lax.axis_index("gz"), lax.axis_size("gz")
+    rows = inside_rows(lax.axis_index("gy"))
+    outside = (len(f) - PLANES) // 2
+
+    def inside(i):
+        z = slab * PLANES + i - outside
+        return rows & (z >= 0) & (z < slabs * PLANES)
+
+    flux = flux_below(f[margin - 1][...], f[margin][...], inside(margin - 1))
+    for i in range(margin, len(f) - margin):
+        g, flux = gradient_plane(f[i][...], f[i + 1][...], flux, inside(i))
+        yield i, g
+
+
+def planes_of(*refs):
+    return [ref.at[i] for ref in refs for i in range(ref.shape[0])]
+
+
+def write_sums(f, moved, parts):
     squares = jnp.zeros((ROWS, WIDTH), F32)
-    for z in range(PLANES):
-        g, flux = gradient_plane(planes(z + 1), planes(z + 2), flux, inside)
-        grad[z] = g
-        if z == 0:
-            grad_first[0] = g
-        if z == PLANES - 1:
-            grad_last[0] = g
+    for _, g in gradients(f, (len(f) - PLANES) // 2):
         squares = squares + g[:ROWS] * g[:ROWS]
     total = jnp.sum(squares, axis=(0, 1), keepdims=True)
     row = moved[:1] + jnp.where(iota((1, TILE), 1) == 1, total, 0.0)
     parts[...] = jnp.broadcast_to(row, parts.shape)
 
 
-def first_gradient_kernel(f, below, above, moved, grad, grad_first, grad_last, parts):
-    def planes(i):
-        return below[0] if i == 0 else above[0] if i == PLANES + 1 else f[i - 1]
-
-    write_gradients(planes, moved, grad, grad_first, grad_last, parts)
+def first_sums_kernel(f, below, above, moved, parts):
+    planes = planes_of(below, f, above)
+    write_sums(planes, moved, parts)
 
 
 def step_length(sums):
@@ -304,38 +343,31 @@
     return TV_ALPHA * jnp.sqrt(moved) / jnp.sqrt(total + EPS_NORM)
 
 
-def next_gradient_kernel(
-    sums, f, below, above, g, g_below, g_above, moved,
-    f_out, below_out, above_out, grad, grad_first, grad_last, parts,
-):
+def next_sums_kernel(sums, moved, *refs):
+    f, f_out, parts = planes_of(*refs[:-2]), refs[-2], refs[-1]
     step = step_length(sums)
-    below_out[0] = below[0] - step * g_below[0]
-    above_out[0] = above[0] - step * g_above[0]
-    for z in range(PLANES):
-        f_out[z] = f[z] - step * g[z]
-
-    def planes(i):
-        return below_out[0] if i == 0 else above_out[0] if i == PLANES + 1 else f_out[i - 1]
-
-    write_gradients(planes, moved, grad, grad_first, grad_last, parts)
-
-
-def last_step_kernel(sums, f, g, out):
+    for i, g in gradients(f, 1):
+        f_out[i - 1] = f[i][...] - step * g
+    write_sums(planes_of(f_out), moved, parts)
+
+
+def last_step_kernel(sums, f_in, out):
+    f = planes_of(f_in)
     step = step_length(sums)
-    for z in range(PLANES):
-        out[z] = f[z, :ROWS] - step * g[z, :ROWS]
-
-
-def call(kernel, shapes, args, scratch=(), flops=0):
+    for i, g in gradients(f, 1):
+        out[i - 1] = (f[i][...] - step * g)[:ROWS]
+
+
+def call(kernel, shapes, args, scratch=(), flops=0, fetched=0, room=16):
     shapes = [jax.ShapeDtypeStruct(shape, dtype) for shape, dtype in shapes]
     moved = sum(a.size * a.dtype.itemsize for a in list(args) + shapes)
     out = pl.pallas_call(
         kernel,
         out_shape=shapes,
-        in_specs=[VMEM] * len(args),
+        in_specs=[VMEM] * (len(args) - fetched) + [pl.BlockSpec(memory_space=pltpu.HBM)] * fetched,
         out_specs=[VMEM] * len(shapes),
         scratch_shapes=list(scratch),
-        compiler_params=pltpu.CompilerParams(vmem_limit_bytes=40 * 1024 * 1024),
+        compiler_params=pltpu.CompilerParams(vmem_limit_bytes=room * 1024 * 1024),
         cost_estimate=pl.CostEstimate(flops=flops, bytes_accessed=moved, transcendentals=0),
     )(*args)
     return out
@@ -349,12 +381,20 @@
     other_chip = [(i, i ^ 2) for i in range(blocks)]
     other_core = [(i, i ^ 1) for i in range(blocks)]
     flat = volume.reshape(PLANES * ROWS, WIDTH)
-    away = jnp.where(block >= 2, 0, (XT - REACH) * TILE)
-    lanes = jnp.pad(ray_weight, ((0, 0), (0, TILE - ROWS)))
-    outgoing = lax.dynamic_slice_in_dim(flat, away, REACH * TILE, axis=1)
-    far = lax.ppermute(jnp.concatenate([outgoing, lanes], axis=1), "gy", other_chip)
-    near = lax.ppermute(flat, "gy", other_core)
-    w_near = lax.ppermute(ray_weight, "gy", other_core)
+    weight = jnp.swapaxes(ray_weight, 0, 1)
+    kinds, bands = jnp.swapaxes(tile_kind, 0, 1), jnp.swapaxes(tile_band, 0, 1)
+    small = jnp.concatenate([(kinds + NK * bands).astype(F32), weight], axis=0)
+    lanes = jnp.pad(weight, ((0, PLANES * ROWS - ROWS), (0, TILE - ANGLES)))
+
+    def outgoing(first, tiles_sent):
+        columns = lax.dynamic_slice_in_dim(flat, first * TILE, tiles_sent * TILE, axis=1)
+        return jnp.concatenate([columns, lanes], axis=1)
+
+    far = lax.ppermute(outgoing(jnp.where(block >= 2, 0, XT - REACH), REACH), "gy", other_chip)
+    beside = block ^ 1
+    window = beside * 2 + jnp.where(beside >= 2, 2, 0)
+    near = lax.ppermute(outgoing(window, WINDOW), "gy", other_core)
+    far, near, small = lax.optimization_barrier((far, near, small))
     farnear = lax.ppermute(far, "gy", other_core)
     half = HALO // 2
     to_before = jnp.concatenate([volume[:, :half], col_norm[:, :half]], axis=1)
@@ -367,13 +407,17 @@
     slab_proj, weights = call(
         project_kernel,
         [((chunk, TILE), F32), ((EXT, ANGLES), F32)],
-        (flat, near, far, farnear, ray_weight, w_near, tile_kind, tile_band, tiles),
+        (far, farnear, near, small, flat, tiles),
         [
+            pltpu.VMEM((PLANES * ROWS, WINDOW * TILE), F32),
             pltpu.VMEM((rows, WINDOW * TILE), F32),
             pltpu.VMEM((2 * rows, SLOTS * TILE), BF16),
-            pltpu.VMEM((SLOTS * TILE, 2 * TILE), BF16),
+            pltpu.VMEM((SLOTS, TILE, 2 * TILE), BF16),
             pltpu.VMEM((QUARTER, rows, TILE), F32),
+            pltpu.SemaphoreType.DMA((3,)),
         ],
+        fetched=2,
+        room=40,
         flops=2 * WINDOW * 2 * rows * SLOTS * TILE * 2 * TILE,
     )
     chunks = slab_proj.reshape(slabs, XT, TILE)
@@ -386,61 +430,60 @@
         flops=2 * 4 * rows * rows * QUARTER * TILE,
     )
     chunks = band_resid.reshape(slabs, XT, TILE)
-    bands = lax.all_to_all(chunks, "gz", split_axis=0, concat_axis=0, tiled=True)
-    bands = bands.reshape(chunk, TILE)
-    bands_far = lax.ppermute(bands, "gy", other_chip)
-    bands_near = lax.ppermute(bands, "gy", other_core)
-    bands_farnear = lax.ppermute(bands_far, "gy", other_core)
-
-    plane = ((1, EXT, WIDTH), F32)
-    block_ext = ((PLANES, EXT, WIDTH), F32)
-    f, f_first, f_last, moved = call(
+    held = lax.all_to_all(chunks, "gz", split_axis=0, concat_axis=0, tiled=True)
+    held, after, before = lax.optimization_barrier((held.reshape(chunk, TILE), after, before))
+    held_far = lax.ppermute(held, "gy", other_chip)
+    held_near = lax.ppermute(held, "gy", other_core)
+    held_farnear = lax.ppermute(held_far, "gy", other_core)
+
+    ends = ((PASSES, EXT, WIDTH), F32)
+    f, first, last, moved = call(
         back_kernel,
-        [block_ext, plane, plane, ((8, TILE), F32)],
+        [((PLANES, EXT, WIDTH), F32), ends, ends, ((8, TILE), F32)],
         (
-            bands, bands_near, bands_far, bands_farnear, tile_kind, tile_band,
-            jnp.swapaxes(tiles, 1, 2), weights, volume, col_norm, after, before,
+            held, held_near, held_far, held_farnear, small, weights,
+            jnp.swapaxes(tiles, 1, 2), volume, col_norm, after, before,
         ),
         [
             pltpu.VMEM((chunk, TILE), F32),
             pltpu.VMEM((XT, rows, TILE), BF16),
             pltpu.VMEM((rows, SLOTS * TILE), BF16),
-            pltpu.VMEM((SLOTS * TILE, 2 * TILE), BF16),
+            pltpu.VMEM((SLOTS, TILE, 2 * TILE), BF16),
+            pltpu.VMEM(volume.shape, F32),
+            pltpu.VMEM(volume.shape, F32),
+            pltpu.VMEM(after.shape, F32),
+            pltpu.VMEM(before.shape, F32),
+            pltpu.SemaphoreType.DMA((6,)),
         ],
+        fetched=5,
+        room=46,
         flops=2 * XT * rows * SLOTS * TILE * 2 * TILE,
     )
     upward = [(i, i + 1) for i in range(slabs - 1)]
     downward = [(i + 1, i) for i in range(slabs - 1)]
-
-    def neighbours(first, last):
-        return lax.ppermute(last, "gz", upward), lax.ppermute(first, "gz", downward)
-
-    def summed(parts):
+    below, above = lax.ppermute(last, "gz", upward), lax.ppermute(first, "gz", downward)
+
+    def exchanged(parts):
         return lax.all_to_all(parts, ("gz", "gy"), split_axis=0, concat_axis=0, tiled=True)
 
     partial = ((slabs * blocks, TILE), F32)
-    work = 40 * PLANES * EXT * WIDTH
-    below, above = neighbours(f_first, f_last)
-    g, g_first, g_last, parts = call(
-        first_gradient_kernel,
-        [block_ext, plane, plane, partial],
-        (f, below, above, moved),
-        flops=work,
-    )
-    for _ in range(PASSES - 1):
-        g_below, g_above = neighbours(g_first, g_last)
-        sums = summed(parts)
-        f, below, above, g, g_first, g_last, parts = call(
-            next_gradient_kernel,
-            [block_ext, plane, plane, block_ext, plane, plane, partial],
-            (sums, f, below, above, g, g_below, g_above, moved),
-            flops=work,
+    work = 40 * EXT * WIDTH
+    (parts,) = call(
+        first_sums_kernel, [partial], (f, below, above, moved), flops=work * PLANES
+    )
+    sums, pieces_of_f = exchanged(parts), (below, f, above)
+    planes = PLANES + 2 * PASSES
+    for step in range(PASSES - 1):
+        planes -= 2
+        f, parts = call(
+            next_sums_kernel,
+            [((planes, EXT, WIDTH), F32), partial],
+            (sums, moved, *pieces_of_f),
+            flops=work * (planes + PLANES),
         )
+        sums, pieces_of_f = exchanged(parts), (f,)
     (smoothed,) = call(
-        last_step_kernel,
-        [(volume.shape, F32)],
-        (summed(parts), f, g),
-        flops=2 * volume.size,
+        last_step_kernel, [(volume.shape, F32)], (sums, f), flops=work * PLANES
     )
     return smoothed, residual[None]
 

time: 205 us -> 186 us (0.907)
  starting transfers between devices: 65.6 us -> 45.5 us
  local copies, waits for them, and re-layouts: 13.1 us -> 3.51 us
  blocking collectives: 59.9 us -> 64.3 us
  Pallas kernels: 20.4 us -> 24.7 us
  waiting for transfers between devices: 42.4 us -> 45.4 us
    all_to_all x2 -> x1, starting transfers between devices: 29.5 us -> 6.8 us  [per_device(): held = lax.all_to_all(chunks, 'gz', split_axis=0, concat_axis=0, tiled=True)]
    unnamed x50 -> x19, local copies, waits for them, and re-layouts: 12 us -> 0.33 us
    all_to_all x1, starting transfers between devices: 6.94 us -> 14.6 us  [per_device(): lax.all_to_all(chunks, 'gz', split_axis=0, concat_axis=0, tiled=True)]
    all_to_all x2 -> x3, blocking collectives: 59.9 us -> 64.3 us  [exchanged(): lax.all_to_all(parts, ('gz', 'gy'), split_axis=0, concat_axis=0, tiled=True)]
    pallas_call x7, Pallas kernels: 20.4 us -> 24.7 us  [call(): pl.pallas_call(kernel, out_shape=shapes, in_specs=[VMEM] * (len(args) - f...]
    all_to_all x1, waiting for transfers between devices: 12.1 us -> 16.3 us  [per_device(): lax.all_to_all(chunks, 'gz', split_axis=0, concat_axis=0, tiled=True)]
    ppermute x1, waiting for transfers between devices: 0.69 us -> 3.7 us  [per_device(): lax.ppermute(to_before, 'gy', [(i + 1, i) for i in range(blocks - 1)])]
    ppermute x12 -> x7, waiting for transfers between devices: 24.7 us -> 22.4 us  [the longest x1 11 us: per_device(): lax.ppermute(last, 'gz', upward)]
  transfers between devices with their start and end apart: 18 -> 12, of which waited for: 13 -> 11; matrix products, arithmetic and copies ran while one was open for 1% -> 2% of each run, Pallas kernels for 0% -> 0%
where the time goes in v2:
time: 186 us; the launch traced here: 185 us
  blocking collectives  64.3 us (35%)
  starting transfers between devices  45.5 us (24%)
  waiting for transfers between devices  45.4 us (24%)
  Pallas kernels  24.7 us (13%)
  local copies, waits for them, and re-layouts  3.51 us (2%)
    all_to_all x3, blocking collectives, exchanged(): lax.all_to_all(parts, ('gz', 'gy'), split_axis=0, concat_axis=0, tiled=True)  64.3 us
    pallas_call x7, Pallas kernels, call(): pl.pallas_call(kernel, out_shape=shapes, in_specs=[VMEM] * (len(args) - f...  24.7 us
    all_to_all x1, waiting for transfers between devices, per_device(): lax.all_to_all(chunks, 'gz', split_axis=0, concat_axis=0, tiled=True)  16.3 us
    all_to_all x1, starting transfers between devices, per_device(): lax.all_to_all(chunks, 'gz', split_axis=0, concat_axis=0, tiled=True)  14.6 us
    ppermute x1, waiting for transfers between devices, per_device(): lax.ppermute(last, 'gz', upward)  11 us
    all_to_all x1, starting transfers between devices, per_device(): held = lax.all_to_all(chunks, 'gz', split_axis=0, concat_axis=0, tiled=True)  6.8 us
    ppermute x1, starting transfers between devices, per_device(): held_farnear = lax.ppermute(held_far, 'gy', other_core)  4.69 us
    ppermute x1, waiting for transfers between devices, per_device(): lax.ppermute(outgoing(jnp.where(block >= 2, 0, XT - REACH), REACH), 'gy',...  4.38 us
  transfers between devices with their start and end apart: 12, of which 11 were waited for; matrix products, arithmetic and copies ran while one was open for 2% of the time, Pallas kernels for 0%

profile of v2, /device:TPU:1, one launch (start us, length us, event | category | flops | bytes accessed | tf_op | source)
XLA Modules:
  0.0 185.4 jit_solution(9070334838969169567)
XLA Ops:
  2.5 2.2 %collective-permute-start = (f32[64,1408]{1,0:T(8,128)S(1)}, f32[64,1408]{1,0:T(8,128)S(1)}, u32[]{:S(2)}, u32[]{:S(2)}) collective-permute-start(f32[64,1408]{1,0:T(8,128)S(1)} %pad_maximum_fusion), channel_id=1, source_target_pairs={{0,2},{1,3},{2,0},{3,1},{4,6},{5,7},{6,4},{7,5},{8,10},{9,11},{10,... | collective-permute-start | bytes 1081352 | tf_op jit(solution)/shard_map/ppermute | solution.py:393
  7.2 4.4 %collective-permute-done.far = f32[64,1408]{1,0:T(8,128)S(1)} collective-permute-done((f32[64,1408]{1,0:T(8,128)S(1)}, f32[64,1408]{1,0:T(8,128)S(1)}, u32[]{:S(2)}, u32[]{:S(2)}) %collective-permute-start) | collective-permute-done | bytes 360480 | tf_op jit(solution)/shard_map/ppermute | solution.py:393
  11.6 2.5 %collective-permute-start.2 = (f32[64,1408]{1,0:T(8,128)S(1)}, f32[64,1408]{1,0:T(8,128)S(1)}, u32[]{:S(2)}, u32[]{:S(2)}) collective-permute-start(f32[64,1408]{1,0:T(8,128)S(1)} %collective-permute-done.far), channel_id=1, source_target_pairs={{0,1},{1,0},{2,3},{3,2},{4,5},{5,4},{6,7},{7,6},{8,9},{9,8},{10,11... | collective-permute-start | bytes 1081352 | tf_op jit(solution)/shard_map/ppermute | solution.py:398
  15.4 7.0 %shard_map.104 = (f32[1024,128]{1,0:T(8,128)}, f32[24,64]{1,0:T(8,128)S(1)}) custom-call(f32[64,1408]{1,0:T(8,128)S(1)} %collective-permute-done.far, f32[64,1408]{1,0:T(8,128)S(1)} %collective-permute-done.2.farnear, f32[64,1152]{1,0:T(8,128)S(1)} %collective-permute-done.1.near, f32[32,64]{1,0:T(8,128)S(1)} %pad_maximum_fusion.4.small, ...), custom_call_target="tpu_custom_call" | custom-call | flops 2147483648 | bytes 2603008 | tf_op jit(solution)/shard_map/pallas_call | solution.py:364
  22.5 14.6 %all-to-all-start = ((f32[64,16,128]{2,1,0:T(8,128)}), f32[64,16,128]{2,1,0:T(8,128)S(1)}, u32[]{:S(2)}, u32[]{:S(2)}) async-start(f32[64,16,128]{2,1,0:T(8,128)} %bitcast.3), calls=%async_computation | async-start | bytes 1048576 | tf_op jit(solution)/shard_map/all_to_all | solution.py:424
  38.5 16.3 %all-to-all-done = f32[64,16,128]{2,1,0:T(8,128)S(1)} async-done(((f32[64,16,128]{2,1,0:T(8,128)}), f32[64,16,128]{2,1,0:T(8,128)S(1)}, u32[]{:S(2)}, u32[]{:S(2)}) %all-to-all-start) | async-done | bytes 524320 | tf_op jit(solution)/shard_map/all_to_all | solution.py:424
  54.8 1.5 shard_map.105
  56.3 6.8 %all-to-all-start.1 = ((bf16[64,16,128]{2,1,0:T(8,128)(2,1)}), bf16[64,16,128]{2,1,0:T(8,128)(2,1)S(1)}, u32[]{:S(2)}, u32[]{:S(2)}) async-start(bf16[64,16,128]{2,1,0:T(8,128)(2,1)} %bitcast.7), calls=%async_computation.1 | async-start | bytes 524288 | tf_op jit(solution)/shard_map/all_to_all | solution.py:433
  64.2 3.5 %collective-permute-start.3 = (f32[4,8,2048]{2,1,0:T(8,128)S(1)}, f32[4,8,2048]{2,1,0:T(8,128)S(1)}, u32[]{:S(2)}, u32[]{:S(2)}) collective-permute-start(f32[4,8,2048]{2,1,0:T(8,128)S(1)} %pad_maximum_fusion.2), channel_id=1, source_target_pairs={{1,0},{2,1},{3,2},{5,4},{6,5},{7,6},{9,8},{10,9},{11,10},{13,12},{... | collective-permute-start | bytes 786440 | tf_op jit(solution)/shard_map/ppermute | solution.py:402
  67.7 2.2 %collective-permute-start.4 = (f32[4,8,2048]{2,1,0:T(8,128)S(1)}, f32[4,8,2048]{2,1,0:T(8,128)S(1)}, u32[]{:S(2)}, u32[]{:S(2)}) collective-permute-start(f32[4,8,2048]{2,1,0:T(8,128)S(1)} %pad_maximum_fusion.3), channel_id=1, source_target_pairs={{0,1},{1,2},{2,3},{4,5},{5,6},{6,7},{8,9},{9,10},{10,11},{12,13},{... | collective-permute-start | bytes 786440 | tf_op jit(solution)/shard_map/ppermute | solution.py:403
  69.9 3.7 %collective-permute-done.3.after = f32[4,8,2048]{2,1,0:T(8,128)S(1)} collective-permute-done((f32[4,8,2048]{2,1,0:T(8,128)S(1)}, f32[4,8,2048]{2,1,0:T(8,128)S(1)}, u32[]{:S(2)}, u32[]{:S(2)}) %collective-permute-start.3) | collective-permute-done | bytes 262176 | tf_op jit(solution)/shard_map/ppermute | solution.py:402
  74.0 1.4 all-to-all-done.1
  75.8 3.8 %collective-permute-start.5 = (bf16[1024,128]{1,0:T(8,128)(2,1)S(1)}, bf16[1024,128]{1,0:T(8,128)(2,1)S(1)}, u32[]{:S(2)}, u32[]{:S(2)}) collective-permute-start(bf16[1024,128]{1,0:T(8,128)(2,1)S(1)} %bitcast.36), channel_id=1, source_target_pairs={{0,1},{1,0},{2,3},{3,2},{4,5},{5,4},{6,7},{7,6},{8,9},{9,8},{10,11... | collective-permute-start | bytes 786440 | tf_op jit(solution)/shard_map/ppermute | solution.py:436
  80.6 4.7 %collective-permute-start.7 = (bf16[1024,128]{1,0:T(8,128)(2,1)S(1)}, bf16[1024,128]{1,0:T(8,128)(2,1)}, u32[]{:S(2)}, u32[]{:S(2)}) collective-permute-start(bf16[1024,128]{1,0:T(8,128)(2,1)S(1)} %collective-permute-done.6.b2), channel_id=1, source_target_pairs={{0,1},{1,0},{2,3},{3,2},{4,5},{5,4},{6,7},{7,6},{8,9},{9,8},{10,11... | collective-permute-start | bytes 786440 | tf_op jit(solution)/shard_map/ppermute | solution.py:437
  86.6 9.0 %shard_map.106 = (f32[4,24,2048]{2,1,0:T(8,128)S(1)}, f32[3,24,2048]{2,1,0:T(8,128)S(1)}, f32[3,24,2048]{2,1,0:T(8,128)S(1)}, f32[8,128]{1,0:T(8,128)S(1)}) custom-call(bf16[1024,128]{1,0:T(8,128)(2,1)S(1)} %bitcast.37, bf16[1024,128]{1,0:T(8,128)(2,1)S(1)} %collective-permute-done.5.b1, bf16[1024,128]{1,0:T(8,128)(2,1)S(1)} %collective-permute-done.6.b2, ...), custom_call_target="tpu_custom_call" | custom-call | flops 2147483648 | bytes 5130240 | tf_op jit(solution)/shard_map/pallas_call | solution.py:364
  95.5 2.3 %collective-permute-start.8 = (f32[3,24,2048]{2,1,0:T(8,128)S(1)}, f32[3,24,2048]{2,1,0:T(8,128)S(1)}, u32[]{:S(2)}, u32[]{:S(2)}) collective-permute-start(f32[3,24,2048]{2,1,0:T(8,128)S(1)} %get-tuple-element.30), channel_id=1, source_target_pairs={{0,4},{4,8},{8,12},{12,16},{16,20},{20,24},{24,28},{28,32},{32,36}... | collective-permute-start | bytes 1769480 | tf_op jit(solution)/shard_map/ppermute | solution.py:464
  99.1 11.0 %collective-permute-done.8.below.refs_0_ = f32[3,24,2048]{2,1,0:T(8,128)S(1)} collective-permute-done((f32[3,24,2048]{2,1,0:T(8,128)S(1)}, f32[3,24,2048]{2,1,0:T(8,128)S(1)}, u32[]{:S(2)}, u32[]{:S(2)}) %collective-permute-start.8) | collective-permute-done | bytes 589856 | tf_op jit(solution)/shard_map/ppermute | solution.py:464
  110.1 3.8 %collective-permute-done.9.above.refs_2_ = f32[3,24,2048]{2,1,0:T(8,128)S(1)} collective-permute-done((f32[3,24,2048]{2,1,0:T(8,128)S(1)}, f32[3,24,2048]{2,1,0:T(8,128)S(1)}, u32[]{:S(2)}, u32[]{:S(2)}) %collective-permute-start.9) | collective-permute-done | bytes 589856 | tf_op jit(solution)/shard_map/ppermute | solution.py:464
  114.8 27.3 %all_to_all.43 = f32[256,1,128]{2,1,0:T(1,128)S(1)} all-to-all(f32[256,1,128]{2,1,0:T(1,128)S(1)} %bitcast.32), channel_id=1, replica_groups=mesh['gz'=64,'gy'=4] {'gz','gy'}, dimensions={0} | all-to-all | bytes 262144 | tf_op jit(solution)/shard_map/all_to_all | solution.py:467
  142.1 2.6 %shard_map.108 = (f32[8,24,2048]{2,1,0:T(8,128)S(1)}, f32[256,128]{1,0:T(8,128)S(1)}) custom-call(f32[256,128]{1,0:T(8,128)S(1)} %bitcast.31, f32[8,128]{1,0:T(8,128)S(1)} %get-tuple-element.32.moved, f32[3,24,2048]{2,1,0:T(8,128)S(1)} %collective-permute-done.8.below.refs_0_, f32[4,24,2048]{2,1,0:T(8,128)S(1)} %get-tuple-element.29.f.refs_1_, ...), custom_call_target="tpu_custom_call" | custom-call | flops 23592960 | bytes 3805184 | tf_op jit(solution)/shard_map/pallas_call | solution.py:364
  144.6 18.6 %all_to_all.44 = f32[256,1,128]{2,1,0:T(1,128)S(1)} all-to-all(f32[256,1,128]{2,1,0:T(1,128)S(1)} %bitcast.38), channel_id=1, replica_groups=mesh['gz'=64,'gy'=4] {'gz','gy'}, dimensions={0} | all-to-all | bytes 262144 | tf_op jit(solution)/shard_map/all_to_all | solution.py:467
  163.3 2.2 %shard_map.109 = (f32[6,24,2048]{2,1,0:T(8,128)S(1)}, f32[256,128]{1,0:T(8,128)S(1)}) custom-call(f32[256,128]{1,0:T(8,128)S(1)} %bitcast.34, f32[8,128]{1,0:T(8,128)S(1)} %get-tuple-element.32.moved, f32[8,24,2048]{2,1,0:T(8,128)S(1)} %get-tuple-element.34.refs_0_), custom_call_target="tpu_custom_call" | custom-call | flops 19660800 | bytes 3018752 | tf_op jit(solution)/shard_map/pallas_call | solution.py:364
  165.5 18.4 %all_to_all.45 = f32[256,1,128]{2,1,0:T(1,128)S(1)} all-to-all(f32[256,1,128]{2,1,0:T(1,128)S(1)} %bitcast.39), channel_id=1, replica_groups=mesh['gz'=64,'gy'=4] {'gz','gy'}, dimensions={0} | all-to-all | bytes 262144 | tf_op jit(solution)/shard_map/all_to_all | solution.py:467
  183.9 1.6 shard_map.110
  (40 shorter events, 13.3 us)
Async XLA Ops:
  0.6 5.4 %copy-start.6 = (f32[64,16]{0,1:T(8,128)S(1)}, f32[64,16]{0,1:T(8,128)}, u32[]{:S(2)}) copy-start(f32[64,16]{0,1:T(8,128)} %param.13) | copy-start | bytes 12292
  0.6 4.1 %copy-start = (f32[4,16,2048]{2,1,0:T(8,128)S(1)}, f32[4,16,2048]{2,1,0:T(8,128)}, u32[]{:S(2)}) copy-start(f32[4,16,2048]{2,1,0:T(8,128)} %volume.1) | copy-start | bytes 1572868
  0.7 5.4 %copy-start.8 = (s32[64,16]{0,1:T(8,128)S(1)}, s32[64,16]{0,1:T(8,128)}, u32[]{:S(2)}) copy-start(s32[64,16]{0,1:T(8,128)} %param.16) | copy-start | bytes 12292
  0.7 5.4 %copy-start.7 = (s32[64,16]{0,1:T(8,128)S(1)}, s32[64,16]{0,1:T(8,128)}, u32[]{:S(2)}) copy-start(s32[64,16]{0,1:T(8,128)} %param.15) | copy-start | bytes 12292
  0.7 14.7 %copy-start.3 = (bf16[16,128,128]{2,1,0:T(8,128)(2,1)S(1)}, bf16[16,128,128]{2,1,0:T(8,128)(2,1)}, u32[]{:S(2)}) copy-start(bf16[16,128,128]{2,1,0:T(8,128)(2,1)} %tiles.1) | copy-start | bytes 1572868
  2.5 9.1 %collective-permute-start = (f32[64,1408]{1,0:T(8,128)S(1)}, f32[64,1408]{1,0:T(8,128)S(1)}, u32[]{:S(2)}, u32[]{:S(2)}) collective-permute-start(f32[64,1408]{1,0:T(8,128)S(1)} %pad_maximum_fusion), channel_id=1, source_target_pairs={{0,2},{1,3},{2,0},{3,1},{4,6},{5,7},{6,4},{7,5},{8,10},{9,11},{10,... | collective-permute-start | bytes 1081352 | tf_op jit(solution)/shard_map/ppermute | solution.py:393
  4.8 2.5 %collective-permute-start.1 = (f32[64,1152]{1,0:T(8,128)S(1)}, f32[64,1152]{1,0:T(8,128)S(1)}, u32[]{:S(2)}, u32[]{:S(2)}) collective-permute-start(f32[64,1152]{1,0:T(8,128)S(1)} %pad_maximum_fusion.1), channel_id=1, source_target_pairs={{0,1},{1,0},{2,3},{3,2},{4,5},{5,4},{6,7},{7,6},{8,9},{9,8},{10,11... | collective-permute-start | bytes 884744 | tf_op jit(solution)/shard_map/ppermute | solution.py:396
  11.6 3.8 %collective-permute-start.2 = (f32[64,1408]{1,0:T(8,128)S(1)}, f32[64,1408]{1,0:T(8,128)S(1)}, u32[]{:S(2)}, u32[]{:S(2)}) collective-permute-start(f32[64,1408]{1,0:T(8,128)S(1)} %collective-permute-done.far), channel_id=1, source_target_pairs={{0,1},{1,0},{2,3},{3,2},{4,5},{5,4},{6,7},{7,6},{8,9},{9,8},{10,11... | collective-permute-start | bytes 1081352 | tf_op jit(solution)/shard_map/ppermute | solution.py:398
  22.4 15.4 %copy-start.4 = (f32[4,16,2048]{2,1,0:T(8,128)S(1)}, f32[4,16,2048]{2,1,0:T(8,128)}, u32[]{:S(2)}) copy-start(f32[4,16,2048]{2,1,0:T(8,128)} %norm.1) | copy-start | bytes 1572868
  22.4 32.4 %copy-start.1 = (f32[1,256,512]{2,1,0:T(8,128)S(1)}, f32[1,256,512]{2,1,0:T(8,128)}, u32[]{:S(2)}) copy-start(f32[1,256,512]{2,1,0:T(8,128)} %param.10) | copy-start | bytes 1572868
  22.4 32.4 %copy-start.2 = (f32[1,256,512]{2,1,0:T(8,128)S(1)}, f32[1,256,512]{2,1,0:T(8,128)}, u32[]{:S(2)}) copy-start(f32[1,256,512]{2,1,0:T(8,128)} %param.11) | copy-start | bytes 1572868
  22.5 32.4 %copy-start.5 = (s32[64,64]{1,0:T(8,128)S(1)}, s32[64,64]{1,0:T(8,128)}, u32[]{:S(2)}) copy-start(s32[64,64]{1,0:T(8,128)} %starts.1) | copy-start | bytes 49156
  22.5 32.3 %all-to-all-start = ((f32[64,16,128]{2,1,0:T(8,128)}), f32[64,16,128]{2,1,0:T(8,128)S(1)}, u32[]{:S(2)}, u32[]{:S(2)}) async-start(f32[64,16,128]{2,1,0:T(8,128)} %bitcast.3), calls=%async_computation | async-start | bytes 1048576 | tf_op jit(solution)/shard_map/all_to_all | solution.py:424
  56.3 19.0 %all-to-all-start.1 = ((bf16[64,16,128]{2,1,0:T(8,128)(2,1)}), bf16[64,16,128]{2,1,0:T(8,128)(2,1)S(1)}, u32[]{:S(2)}, u32[]{:S(2)}) async-start(bf16[64,16,128]{2,1,0:T(8,128)(2,1)} %bitcast.7), calls=%async_computation.1 | async-start | bytes 524288 | tf_op jit(solution)/shard_map/all_to_all | solution.py:433
  64.2 9.4 %collective-permute-start.3 = (f32[4,8,2048]{2,1,0:T(8,128)S(1)}, f32[4,8,2048]{2,1,0:T(8,128)S(1)}, u32[]{:S(2)}, u32[]{:S(2)}) collective-permute-start(f32[4,8,2048]{2,1,0:T(8,128)S(1)} %pad_maximum_fusion.2), channel_id=1, source_target_pairs={{1,0},{2,1},{3,2},{5,4},{6,5},{7,6},{9,8},{10,9},{11,10},{13,12},{... | collective-permute-start | bytes 786440 | tf_op jit(solution)/shard_map/ppermute | solution.py:402
  67.7 6.3 %collective-permute-start.4 = (f32[4,8,2048]{2,1,0:T(8,128)S(1)}, f32[4,8,2048]{2,1,0:T(8,128)S(1)}, u32[]{:S(2)}, u32[]{:S(2)}) collective-permute-start(f32[4,8,2048]{2,1,0:T(8,128)S(1)} %pad_maximum_fusion.3), channel_id=1, source_target_pairs={{0,1},{1,2},{2,3},{4,5},{5,6},{6,7},{8,9},{9,10},{10,11},{12,13},{... | collective-permute-start | bytes 786440 | tf_op jit(solution)/shard_map/ppermute | solution.py:403
  75.3 5.2 %collective-permute-start.6 = (bf16[1024,128]{1,0:T(8,128)(2,1)S(1)}, bf16[1024,128]{1,0:T(8,128)(2,1)S(1)}, u32[]{:S(2)}, u32[]{:S(2)}) collective-permute-start(bf16[1024,128]{1,0:T(8,128)(2,1)S(1)} %bitcast.35), channel_id=1, source_target_pairs={{0,2},{1,3},{2,0},{3,1},{4,6},{5,7},{6,4},{7,5},{8,10},{9,11},{10,... | collective-permute-start | bytes 786440 | tf_op jit(solution)/shard_map/ppermute | solution.py:435
  75.8 9.8 %collective-permute-start.5 = (bf16[1024,128]{1,0:T(8,128)(2,1)S(1)}, bf16[1024,128]{1,0:T(8,128)(2,1)S(1)}, u32[]{:S(2)}, u32[]{:S(2)}) collective-permute-start(bf16[1024,128]{1,0:T(8,128)(2,1)S(1)} %bitcast.36), channel_id=1, source_target_pairs={{0,1},{1,0},{2,3},{3,2},{4,5},{5,4},{6,7},{7,6},{8,9},{9,8},{10,11... | collective-permute-start | bytes 786440 | tf_op jit(solution)/shard_map/ppermute | solution.py:436
  80.6 6.0 %collective-permute-start.7 = (bf16[1024,128]{1,0:T(8,128)(2,1)S(1)}, bf16[1024,128]{1,0:T(8,128)(2,1)}, u32[]{:S(2)}, u32[]{:S(2)}) collective-permute-start(bf16[1024,128]{1,0:T(8,128)(2,1)S(1)} %collective-permute-done.6.b2), channel_id=1, source_target_pairs={{0,1},{1,0},{2,3},{3,2},{4,5},{5,4},{6,7},{7,6},{8,9},{9,8},{10,11... | collective-permute-start | bytes 786440 | tf_op jit(solution)/shard_map/ppermute | solution.py:437
  95.5 14.5 %collective-permute-start.8 = (f32[3,24,2048]{2,1,0:T(8,128)S(1)}, f32[3,24,2048]{2,1,0:T(8,128)S(1)}, u32[]{:S(2)}, u32[]{:S(2)}) collective-permute-start(f32[3,24,2048]{2,1,0:T(8,128)S(1)} %get-tuple-element.30), channel_id=1, source_target_pairs={{0,4},{4,8},{8,12},{12,16},{16,20},{20,24},{24,28},{28,32},{32,36}... | collective-permute-start | bytes 1769480 | tf_op jit(solution)/shard_map/ppermute | solution.py:464
  97.8 16.1 %collective-permute-start.9 = (f32[3,24,2048]{2,1,0:T(8,128)S(1)}, f32[3,24,2048]{2,1,0:T(8,128)S(1)}, u32[]{:S(2)}, u32[]{:S(2)}) collective-permute-start(f32[3,24,2048]{2,1,0:T(8,128)S(1)} %get-tuple-element.31), channel_id=1, source_target_pairs={{4,0},{8,4},{12,8},{16,12},{20,16},{24,20},{28,24},{32,28},{36,32}... | collective-permute-start | bytes 1769480 | tf_op jit(solution)/shard_map/ppermute | solution.py:464

commit v3 on v2

--- a/solution.py
+++ b/solution.py
@@ -22,6 +22,8 @@
 WINDOW = 8
 REACH = 10
 SLOTS = 8
+GROUP = 4
+PAIR = 2
 
 
 def iota(shape, dim):
@@ -78,7 +80,7 @@
 
 
 def slot_masks(kind):
-    return [onehot((kind % SLOTS) == k, BF16) for k in range(SLOTS)]
+    return [onehot((kind & (SLOTS - 1)) == k, BF16) for k in range(SLOTS)]
 
 
 def pick_half(wide, kind):
@@ -87,7 +89,7 @@
 
 def project_kernel(
     far, farnear, near, small, own, tiles, out, weights_out,
-    own_here, sums, lhs, rhs, acc, arrived,
+    own_here, sums, lhs, rhs, wide, acc, arrived,
 ):
     block = lax.axis_index("gy")
     first = block * 2 + jnp.where(block >= 2, 2, 0)
@@ -132,23 +134,35 @@
         fetch.wait()
     code = small[:XT].T
     rows = PLANES * ANGLES
-    for j in range(WINDOW):
-        column = code_column(code, first + j)
-        kind, band = column % NK, column // NK
-        masks = slot_masks(kind)
-        for z in range(PLANES):
-            part = sums[z * ANGLES : (z + 1) * ANGLES, j * TILE : (j + 1) * TILE]
-            for p, piece in enumerate(pieces(part, 2)):
-                at = (p * PLANES + z) * ANGLES
-                for k in range(SLOTS):
-                    lhs[at : at + ANGLES, k * TILE : (k + 1) * TILE] = piece * masks[k]
-        wide = dot(lhs[...], rhs[...].reshape(SLOTS * TILE, 2 * TILE))
-        wide = wide[:rows] + wide[rows:]
-        for z in range(PLANES):
-            tile = pick_half(wide[z * ANGLES : (z + 1) * ANGLES], kind)
-            for t in range(QUARTER):
-                here = acc.at[t, z * ANGLES : (z + 1) * ANGLES, :]
-                here[...] += jnp.where(band == block * QUARTER + t, tile, 0.0)
+    columns = [code_column(code, first + j) for j in range(WINDOW)]
+
+    def build(group):
+        for j in range(group * PAIR, (group + 1) * PAIR):
+            masks = slot_masks(columns[j] & (NK - 1))
+            for z in range(PLANES):
+                part = sums[z * ANGLES : (z + 1) * ANGLES, j * TILE : (j + 1) * TILE]
+                for p, piece in enumerate(pieces(part, 2)):
+                    at = ((j * 2 + p) * PLANES + z) * ANGLES
+                    for k in range(SLOTS):
+                        lhs[at : at + ANGLES, k * TILE : (k + 1) * TILE] = piece * masks[k]
+        part = slice(group * PAIR * 2 * rows, (group + 1) * PAIR * 2 * rows)
+        wide[part] = dot(lhs[part], rhs[...].reshape(SLOTS * TILE, 2 * TILE))
+
+    def place(group):
+        for j in range(group * PAIR, (group + 1) * PAIR):
+            kind, band = columns[j] & (NK - 1), columns[j] >> 4
+            for z in range(PLANES):
+                at = (j * 2 * PLANES + z) * ANGLES
+                tile = pick_half(wide[at : at + ANGLES] + wide[at + rows : at + rows + ANGLES], kind)
+                for t in range(QUARTER):
+                    here = acc.at[t, z * ANGLES : (z + 1) * ANGLES, :]
+                    here[...] += jnp.where(band == block * QUARTER + t, tile, 0.0)
+
+    for group in range(WINDOW // PAIR):
+        build(group)
+        if group > 0:
+            place(group - 1)
+    place(WINDOW // PAIR - 1)
     for t in range(QUARTER):
         for z in range(PLANES):
             out[pl.ds(t * PLANES + z, ANGLES, stride=XT), :] = acc[
@@ -200,14 +214,12 @@
 def back_kernel(
     b0, b1, b2, b3, small, weights, tiles, volume, norm, after, before,
     updated, first_planes, last_planes, moved,
-    flat, rows_by_tile, lhs, rhs,
+    flat, rows_by_tile, lhs, rhs, wide,
     volume_here, norm_here, after_here, before_here, arrived,
 ):
     block = lax.axis_index("gy")
     fetches = start_fetches(
         (
-            (tiles.at[:SLOTS], rhs.at[:, :, :TILE]),
-            (tiles.at[SLOTS:], rhs.at[:, :, TILE:]),
             (volume, volume_here),
             (norm, norm_here),
             (after, after_here),
@@ -227,17 +239,23 @@
 
     for flip, ref in enumerate((b0, b1, b2, b3)):
         arrange(flip, ref)
+    for k in range(SLOTS):
+        rhs[k, :, :TILE] = tiles[k]
+        rhs[k, :, TILE:] = tiles[k + SLOTS]
     for fetch in fetches:
         fetch.wait()
     code = small[:XT].T
     inside = inside_rows(block)
     low = iota((HALO, 2 * TILE), 0) < HALO // 2
     squares = jnp.zeros((ROWS, 2 * TILE), F32)
-    for pair in range(XT // 2):
-        backs = []
-        for j in (2 * pair, 2 * pair + 1):
+    kinds = []
+    rows = PLANES * ANGLES
+
+    def build(group):
+        for j in range(group * GROUP, (group + 1) * GROUP):
             column = code_column(code, j)
-            kind, band = column % NK, column // NK
+            kind, band = column & (NK - 1), column >> 4
+            kinds.append(kind)
             masks = slot_masks(kind)
             near = [t for t in range(j - 2, j + 3) if 0 <= t < XT]
             at_band = [onehot(band == t, BF16) for t in near]
@@ -247,34 +265,65 @@
                 for t, mask in zip(near, at_band):
                     term = rows_by_tile[t, here, :] * mask
                     chosen = term if chosen is None else chosen + term
+                first = (j * PLANES + z) * ANGLES
                 for k in range(SLOTS):
-                    lhs[here, k * TILE : (k + 1) * TILE] = chosen * masks[k]
-            wide = dot(lhs[...], rhs[...].reshape(SLOTS * TILE, 2 * TILE))
-            backs.append(
-                [pick_half(wide[z * ANGLES : (z + 1) * ANGLES], kind) for z in range(PLANES)]
-            )
-        cut = slice(2 * pair * TILE, (2 * pair + 2) * TILE)
-        for z in range(PLANES):
-            back = jnp.concatenate([backs[0][z], backs[1][z]], axis=1)
-            b = pieces(back, 2)
-            smeared = dot(left, jnp.concatenate([b[0], b[1], b[0]], axis=0))
-            up, down = after_here[z, :, cut], before_here[z, :, cut]
-            v = jnp.concatenate(
-                [volume_here[z, :, cut], jnp.where(low, up, pltpu.roll(down, HALO // 2, 0))], axis=0
-            )
-            n = jnp.concatenate(
-                [norm_here[z, :, cut], jnp.where(low, pltpu.roll(up, HALO // 2, 0), down)], axis=0
-            )
-            new = v + RELAX * smeared / jnp.where(inside, n, 1.0)
-            updated[z, :, cut] = new
-            if z < PASSES:
-                first_planes[z, :, cut] = new
-            if z >= PLANES - PASSES:
-                last_planes[z - (PLANES - PASSES), :, cut] = new
-            change = (new - v)[:ROWS]
-            squares = squares + change * change
+                    lhs[first : first + ANGLES, k * TILE : (k + 1) * TILE] = chosen * masks[k]
+        part = slice(group * GROUP * rows, (group + 1) * GROUP * rows)
+        wide[part] = dot(lhs[part], rhs[...].reshape(SLOTS * TILE, 2 * TILE))
+
+    def back_tile(j, z):
+        first = (j * PLANES + z) * ANGLES
+        return pick_half(wide[first : first + ANGLES], kinds[j])
+
+    def finish(group, squares):
+        for pair in range(group * GROUP // 2, (group + 1) * GROUP // 2):
+            cut = slice(2 * pair * TILE, (2 * pair + 2) * TILE)
+            news = []
+            for z in range(PLANES):
+                back = jnp.concatenate([back_tile(2 * pair, z), back_tile(2 * pair + 1, z)], axis=1)
+                b = pieces(back, 2)
+                smeared = dot(left, jnp.concatenate([b[0], b[1], b[0]], axis=0))
+                up, down = after_here[z, :, cut], before_here[z, :, cut]
+                v = jnp.concatenate(
+                    [volume_here[z, :, cut], jnp.where(low, up, pltpu.roll(down, HALO // 2, 0))], axis=0
+                )
+                n = jnp.concatenate(
+                    [norm_here[z, :, cut], jnp.where(low, pltpu.roll(up, HALO // 2, 0), down)], axis=0
+                )
+                new = v + RELAX * smeared / jnp.where(inside, n, 1.0)
+                updated[z, :, cut] = new
+                news.append(new)
+                change = (new - v)[:ROWS]
+                squares = squares + change * change
+            first_planes[:, cut] = packed_end(news)
+            last_planes[:, cut] = packed_end(news[::-1])
+        return squares
+
+    for group in range(XT // GROUP):
+        build(group)
+        if group > 0:
+            squares = finish(group - 1, squares)
+    squares = finish(XT // GROUP - 1, squares)
     total = jnp.sum(squares, axis=(0, 1), keepdims=True)
     moved[...] = jnp.where(iota((8, TILE), 1) == 0, total, 0.0)
+
+
+def packed_end(planes):
+    near, *others = planes[:PASSES]
+    sent = pieces(near, 2)
+    held = sent[0].astype(F32) + sent[1].astype(F32)
+    for plane in others:
+        sent.append((plane - held).astype(BF16))
+        held = held + sent[-1].astype(F32)
+    return jnp.concatenate([part.astype(F32) for part in sent], axis=0).astype(BF16)
+
+
+def unpack_end(ref, planes):
+    sent = ref[...].astype(F32)
+    held = sent[:EXT]
+    for i, plane in enumerate(planes):
+        held = held + sent[(i + 1) * EXT : (i + 2) * EXT]
+        plane[...] = held
 
 
 def gradient_plane(here, above, flux_z_below, inside):
@@ -302,7 +351,7 @@
     return jnp.where(inside, dz * scale, 0.0)
 
 
-def gradients(f, margin):
+def gradients(f, first, last):
     slab, slabs = lax.axis_index("gz"), lax.axis_size("gz")
     rows = inside_rows(lax.axis_index("gy"))
     outside = (len(f) - PLANES) // 2
@@ -311,28 +360,36 @@
         z = slab * PLANES + i - outside
         return rows & (z >= 0) & (z < slabs * PLANES)
 
-    flux = flux_below(f[margin - 1][...], f[margin][...], inside(margin - 1))
-    for i in range(margin, len(f) - margin):
-        g, flux = gradient_plane(f[i][...], f[i + 1][...], flux, inside(i))
+    flux = flux_below(f[first - 1](), f[first](), inside(first - 1))
+    for i in range(first, last):
+        g, flux = gradient_plane(f[i](), f[i + 1](), flux, inside(i))
         yield i, g
 
 
-def planes_of(*refs):
-    return [ref.at[i] for ref in refs for i in range(ref.shape[0])]
-
-
-def write_sums(f, moved, parts):
+def loaders(ref):
+    return [lambda i=i: ref[i] for i in range(ref.shape[0])]
+
+
+def write_sums(f, moved, g_out, parts):
+    outside = (len(f) - PLANES) // 2
     squares = jnp.zeros((ROWS, WIDTH), F32)
-    for _, g in gradients(f, (len(f) - PLANES) // 2):
+    for i, g in gradients(f, outside, outside + PLANES):
+        g_out[i - outside] = g
         squares = squares + g[:ROWS] * g[:ROWS]
     total = jnp.sum(squares, axis=(0, 1), keepdims=True)
     row = moved[:1] + jnp.where(iota((1, TILE), 1) == 1, total, 0.0)
     parts[...] = jnp.broadcast_to(row, parts.shape)
 
 
-def first_sums_kernel(f, below, above, moved, parts):
-    planes = planes_of(below, f, above)
-    write_sums(planes, moved, parts)
+def with_ends(f, below, above, low, high):
+    count = low.shape[0]
+    unpack_end(below, [low.at[count - 1 - i] for i in range(count)])
+    unpack_end(above, [high.at[i] for i in range(count)])
+    return [*loaders(low), *loaders(f), *loaders(high)]
+
+
+def first_sums_kernel(f, below, above, moved, g_out, parts, low, high):
+    write_sums(with_ends(f, below, above, low, high), moved, g_out, parts)
 
 
 def step_length(sums):
@@ -343,19 +400,29 @@
     return TV_ALPHA * jnp.sqrt(moved) / jnp.sqrt(total + EPS_NORM)
 
 
-def next_sums_kernel(sums, moved, *refs):
-    f, f_out, parts = planes_of(*refs[:-2]), refs[-2], refs[-1]
+def next_sums(sums, f, g, moved, f_out, g_out, parts):
     step = step_length(sums)
-    for i, g in gradients(f, 1):
-        f_out[i - 1] = f[i][...] - step * g
-    write_sums(planes_of(f_out), moved, parts)
-
-
-def last_step_kernel(sums, f_in, out):
-    f = planes_of(f_in)
+    outside = (len(f) - PLANES) // 2
+    for z in range(PLANES):
+        f_out[outside - 1 + z] = f[outside + z]() - step * g[z]
+    for first, last in ((1, outside), (outside + PLANES, len(f) - 1)):
+        for i, gradient in gradients(f, first, last):
+            f_out[i - 1] = f[i]() - step * gradient
+    write_sums(loaders(f_out), moved, g_out, parts)
+
+
+def second_sums_kernel(sums, moved, f, below, above, g, f_out, g_out, parts, low, high):
+    next_sums(sums, with_ends(f, below, above, low, high), g, moved, f_out, g_out, parts)
+
+
+def third_sums_kernel(sums, moved, f, g, f_out, g_out, parts):
+    next_sums(sums, loaders(f), g, moved, f_out, g_out, parts)
+
+
+def last_step_kernel(sums, f, g, out):
     step = step_length(sums)
-    for i, g in gradients(f, 1):
-        out[i - 1] = (f[i][...] - step * g)[:ROWS]
+    for z in range(PLANES):
+        out[z] = f[1 + z, :ROWS] - step * g[z, :ROWS]
 
 
 def call(kernel, shapes, args, scratch=(), flops=0, fetched=0, room=16):
@@ -384,16 +451,18 @@
     weight = jnp.swapaxes(ray_weight, 0, 1)
     kinds, bands = jnp.swapaxes(tile_kind, 0, 1), jnp.swapaxes(tile_band, 0, 1)
     small = jnp.concatenate([(kinds + NK * bands).astype(F32), weight], axis=0)
-    lanes = jnp.pad(weight, ((0, PLANES * ROWS - ROWS), (0, TILE - ANGLES)))
-
-    def outgoing(first, tiles_sent):
-        columns = lax.dynamic_slice_in_dim(flat, first * TILE, tiles_sent * TILE, axis=1)
+
+    def outgoing(rows_sent, weight_sent, first, tiles_sent):
+        columns = lax.dynamic_slice_in_dim(rows_sent, first * TILE, tiles_sent * TILE, axis=1)
+        lanes = jnp.pad(weight_sent, ((0, PLANES * ROWS - ROWS), (0, TILE - ANGLES)))
         return jnp.concatenate([columns, lanes], axis=1)
 
-    far = lax.ppermute(outgoing(jnp.where(block >= 2, 0, XT - REACH), REACH), "gy", other_chip)
+    to_chip = outgoing(flat, weight, jnp.where(block >= 2, 0, XT - REACH), REACH)
+    to_chip, flat_later, weight_later = lax.optimization_barrier((to_chip, flat, weight))
+    far = lax.ppermute(to_chip, "gy", other_chip)
     beside = block ^ 1
     window = beside * 2 + jnp.where(beside >= 2, 2, 0)
-    near = lax.ppermute(outgoing(window, WINDOW), "gy", other_core)
+    near = lax.ppermute(outgoing(flat_later, weight_later, window, WINDOW), "gy", other_core)
     far, near, small = lax.optimization_barrier((far, near, small))
     farnear = lax.ppermute(far, "gy", other_core)
     half = HALO // 2
@@ -411,8 +480,9 @@
         [
             pltpu.VMEM((PLANES * ROWS, WINDOW * TILE), F32),
             pltpu.VMEM((rows, WINDOW * TILE), F32),
-            pltpu.VMEM((2 * rows, SLOTS * TILE), BF16),
+            pltpu.VMEM((WINDOW * 2 * rows, SLOTS * TILE), BF16),
             pltpu.VMEM((SLOTS, TILE, 2 * TILE), BF16),
+            pltpu.VMEM((WINDOW * 2 * rows, 2 * TILE), F32),
             pltpu.VMEM((QUARTER, rows, TILE), F32),
             pltpu.SemaphoreType.DMA((3,)),
         ],
@@ -422,6 +492,7 @@
     )
     chunks = slab_proj.reshape(slabs, XT, TILE)
     owner_rows = lax.all_to_all(chunks, "gz", split_axis=0, concat_axis=0, tiled=True)
+    owner_rows, after, before = lax.optimization_barrier((owner_rows, after, before))
     residual, band_resid = call(
         residual_kernel,
         [(measured.shape[1:], F32), ((chunk, TILE), BF16)],
@@ -431,12 +502,12 @@
     )
     chunks = band_resid.reshape(slabs, XT, TILE)
     held = lax.all_to_all(chunks, "gz", split_axis=0, concat_axis=0, tiled=True)
-    held, after, before = lax.optimization_barrier((held.reshape(chunk, TILE), after, before))
+    held = held.reshape(chunk, TILE)
     held_far = lax.ppermute(held, "gy", other_chip)
     held_near = lax.ppermute(held, "gy", other_core)
     held_farnear = lax.ppermute(held_far, "gy", other_core)
 
-    ends = ((PASSES, EXT, WIDTH), F32)
+    ends = (((PASSES + 1) * EXT, WIDTH), BF16)
     f, first, last, moved = call(
         back_kernel,
         [((PLANES, EXT, WIDTH), F32), ends, ends, ((8, TILE), F32)],
@@ -447,15 +518,16 @@
         [
             pltpu.VMEM((chunk, TILE), F32),
             pltpu.VMEM((XT, rows, TILE), BF16),
-            pltpu.VMEM((rows, SLOTS * TILE), BF16),
+            pltpu.VMEM((XT * rows, SLOTS * TILE), BF16),
             pltpu.VMEM((SLOTS, TILE, 2 * TILE), BF16),
+            pltpu.VMEM((XT * rows, 2 * TILE), F32),
             pltpu.VMEM(volume.shape, F32),
             pltpu.VMEM(volume.shape, F32),
             pltpu.VMEM(after.shape, F32),
             pltpu.VMEM(before.shape, F32),
             pltpu.SemaphoreType.DMA((6,)),
         ],
-        fetched=5,
+        fetched=4,
         room=46,
         flops=2 * XT * rows * SLOTS * TILE * 2 * TILE,
     )
@@ -467,23 +539,30 @@
         return lax.all_to_all(parts, ("gz", "gy"), split_axis=0, concat_axis=0, tiled=True)
 
     partial = ((slabs * blocks, TILE), F32)
+    block_ext = ((PLANES, EXT, WIDTH), F32)
     work = 40 * EXT * WIDTH
-    (parts,) = call(
-        first_sums_kernel, [partial], (f, below, above, moved), flops=work * PLANES
-    )
-    sums, pieces_of_f = exchanged(parts), (below, f, above)
-    planes = PLANES + 2 * PASSES
-    for step in range(PASSES - 1):
-        planes -= 2
-        f, parts = call(
-            next_sums_kernel,
-            [((planes, EXT, WIDTH), F32), partial],
-            (sums, moved, *pieces_of_f),
-            flops=work * (planes + PLANES),
-        )
-        sums, pieces_of_f = exchanged(parts), (f,)
+    g, parts = call(
+        first_sums_kernel,
+        [block_ext, partial],
+        (f, below, above, moved),
+        [pltpu.VMEM((1, EXT, WIDTH), F32), pltpu.VMEM((1, EXT, WIDTH), F32)],
+        flops=work * PLANES,
+    )
+    f, g, parts = call(
+        second_sums_kernel,
+        [((PLANES + 4, EXT, WIDTH), F32), block_ext, partial],
+        (exchanged(parts), moved, f, below, above, g),
+        [pltpu.VMEM((PASSES, EXT, WIDTH), F32), pltpu.VMEM((PASSES, EXT, WIDTH), F32)],
+        flops=work * (2 * PLANES + 4),
+    )
+    f, g, parts = call(
+        third_sums_kernel,
+        [((PLANES + 2, EXT, WIDTH), F32), block_ext, partial],
+        (exchanged(parts), moved, f, g),
+        flops=work * (2 * PLANES + 2),
+    )
     (smoothed,) = call(
-        last_step_kernel, [(volume.shape, F32)], (sums, f), flops=work * PLANES
+        last_step_kernel, [(volume.shape, F32)], (exchanged(parts), f, g), flops=2 * volume.size
     )
     return smoothed, residual[None]
 

time: 186 us -> 176 us (0.946)
  blocking collectives: 64.3 us -> 82.5 us
  waiting for transfers between devices: 45.4 us -> 29.7 us
  starting transfers between devices: 45.5 us -> 38.5 us
  Pallas kernels: 24.7 us -> 19.7 us
    all_to_all x0 -> x1, blocking collectives: none -> 18.9 us  [per_device(): held = lax.all_to_all(chunks, 'gz', split_axis=0, concat_axis=0, tiled=True)]
    all_to_all x1, waiting for transfers between devices: 16.3 us -> 5.79 us  [per_device(): lax.all_to_all(chunks, 'gz', split_axis=0, concat_axis=0, tiled=True)]
    all_to_all x1 -> x0, starting transfers between devices: 6.8 us -> none  [per_device(): held = lax.all_to_all(chunks, 'gz', split_axis=0, concat_axis=0, tiled=True)]
    pallas_call x7, Pallas kernels: 24.7 us -> 19.7 us  [call(): pl.pallas_call(kernel, out_shape=shapes, in_specs=[VMEM] * (len(args) - f...]
    ppermute x1, waiting for transfers between devices: 11 us -> 6.78 us  [per_device(): lax.ppermute(last, 'gz', upward)]
  transfers between devices with their start and end apart: 12 -> 11, of which waited for: 11 -> 10; matrix products, arithmetic and copies ran while one was open for 2% -> 1% of each run, Pallas kernels for 0% -> 0%
where the time goes in v3:
time: 176 us; the launch traced here: 175 us
  blocking collectives  82.5 us (47%)
  starting transfers between devices  38.5 us (22%)
  waiting for transfers between devices  29.7 us (17%)
  Pallas kernels  19.7 us (11%)
  local copies, waits for them, and re-layouts  3.19 us (2%)
    all_to_all x3, blocking collectives, exchanged(): lax.all_to_all(parts, ('gz', 'gy'), split_axis=0, concat_axis=0, tiled=True)  63.5 us
    pallas_call x7, Pallas kernels, call(): pl.pallas_call(kernel, out_shape=shapes, in_specs=[VMEM] * (len(args) - f...  19.7 us
    all_to_all x1, blocking collectives, per_device(): held = lax.all_to_all(chunks, 'gz', split_axis=0, concat_axis=0, tiled=True)  18.9 us
    all_to_all x1, starting transfers between devices, per_device(): lax.all_to_all(chunks, 'gz', split_axis=0, concat_axis=0, tiled=True)  14.6 us
    ppermute x1, waiting for transfers between devices, per_device(): lax.ppermute(last, 'gz', upward)  6.78 us
    all_to_all x1, waiting for transfers between devices, per_device(): lax.all_to_all(chunks, 'gz', split_axis=0, concat_axis=0, tiled=True)  5.79 us
    ppermute x1, starting transfers between devices, per_device(): held_farnear = lax.ppermute(held_far, 'gy', other_core)  4.7 us
    ppermute x1, waiting for transfers between devices, per_device(): lax.ppermute(to_before, 'gy', [(i + 1, i) for i in range(blocks - 1)])  4.17 us
  transfers between devices with their start and end apart: 11, of which 10 were waited for; matrix products, arithmetic and copies ran while one was open for 1% of the time, Pallas kernels for 0%

profile of v3, /device:TPU:1, one launch (start us, length us, event | category | flops | bytes accessed | tf_op | source)
XLA Modules:
  0.0 175.3 jit_solution(11814465835519381873)
XLA Ops:
  2.5 2.2 %collective-permute-start = (f32[64,1408]{1,0:T(8,128)S(1)}, f32[64,1408]{1,0:T(8,128)S(1)}, u32[]{:S(2)}, u32[]{:S(2)}) collective-permute-start(f32[64,1408]{1,0:T(8,128)S(1)} %select_maximum_fusion), channel_id=1, source_target_pairs={{0,2},{1,3},{2,0},{3,1},{4,6},{5,7},{6,4},{7,5},{8,10},{9,11},{10,... | collective-permute-start | bytes 1081352 | tf_op jit(solution)/shard_map/ppermute | solution.py:462
  8.2 3.4 %collective-permute-done.far = f32[64,1408]{1,0:T(8,128)S(1)} collective-permute-done((f32[64,1408]{1,0:T(8,128)S(1)}, f32[64,1408]{1,0:T(8,128)S(1)}, u32[]{:S(2)}, u32[]{:S(2)}) %collective-permute-start) | collective-permute-done | bytes 360480 | tf_op jit(solution)/shard_map/ppermute | solution.py:462
  11.6 2.5 %collective-permute-start.2 = (f32[64,1408]{1,0:T(8,128)S(1)}, f32[64,1408]{1,0:T(8,128)S(1)}, u32[]{:S(2)}, u32[]{:S(2)}) collective-permute-start(f32[64,1408]{1,0:T(8,128)S(1)} %collective-permute-done.far), channel_id=1, source_target_pairs={{0,1},{1,0},{2,3},{3,2},{4,5},{5,4},{6,7},{7,6},{8,9},{9,8},{10,11... | collective-permute-start | bytes 1081352 | tf_op jit(solution)/shard_map/ppermute | solution.py:467
  14.1 1.3 collective-permute-done.2.farnear
  15.4 5.6 %shard_map.104 = (f32[1024,128]{1,0:T(8,128)}, f32[24,64]{1,0:T(8,128)S(1)}) custom-call(f32[64,1408]{1,0:T(8,128)S(1)} %collective-permute-done.far, f32[64,1408]{1,0:T(8,128)S(1)} %collective-permute-done.2.farnear, f32[64,1152]{1,0:T(8,128)S(1)} %collective-permute-done.1.near, f32[32,64]{1,0:T(8,128)S(1)} %pad_maximum_fusion.2.small, ...), custom_call_target="tpu_custom_call" | custom-call | flops 2147483648 | bytes 2603008 | tf_op jit(solution)/shard_map/pallas_call | solution.py:431
  21.0 14.6 %all-to-all-start = ((f32[64,16,128]{2,1,0:T(8,128)}), f32[64,16,128]{2,1,0:T(8,128)S(1)}, u32[]{:S(2)}, u32[]{:S(2)}) async-start(f32[64,16,128]{2,1,0:T(8,128)} %bitcast.3), calls=%async_computation | async-start | bytes 1048576 | tf_op jit(solution)/shard_map/all_to_all | solution.py:494
  35.9 2.6 %collective-permute-start.3 = (f32[4,8,2048]{2,1,0:T(8,128)S(1)}, f32[4,8,2048]{2,1,0:T(8,128)S(1)}, u32[]{:S(2)}, u32[]{:S(2)}) collective-permute-start(f32[4,8,2048]{2,1,0:T(8,128)S(1)} %pad_maximum_fusion), channel_id=1, source_target_pairs={{1,0},{2,1},{3,2},{5,4},{6,5},{7,6},{9,8},{10,9},{11,10},{13,12},{... | collective-permute-start | bytes 786440 | tf_op jit(solution)/shard_map/ppermute | solution.py:471
  38.5 3.0 %collective-permute-start.4 = (f32[4,8,2048]{2,1,0:T(8,128)S(1)}, f32[4,8,2048]{2,1,0:T(8,128)S(1)}, u32[]{:S(2)}, u32[]{:S(2)}) collective-permute-start(f32[4,8,2048]{2,1,0:T(8,128)S(1)} %pad_maximum_fusion.1), channel_id=1, source_target_pairs={{0,1},{1,2},{2,3},{4,5},{5,6},{6,7},{8,9},{9,10},{10,11},{12,13},{... | collective-permute-start | bytes 786440 | tf_op jit(solution)/shard_map/ppermute | solution.py:472
  41.5 4.2 %collective-permute-done.3.after = f32[4,8,2048]{2,1,0:T(8,128)S(1)} collective-permute-done((f32[4,8,2048]{2,1,0:T(8,128)S(1)}, f32[4,8,2048]{2,1,0:T(8,128)S(1)}, u32[]{:S(2)}, u32[]{:S(2)}) %collective-permute-start.3) | collective-permute-done | bytes 262176 | tf_op jit(solution)/shard_map/ppermute | solution.py:471
  47.6 5.8 %all-to-all-done = f32[64,16,128]{2,1,0:T(8,128)S(1)} async-done(((f32[64,16,128]{2,1,0:T(8,128)}), f32[64,16,128]{2,1,0:T(8,128)S(1)}, u32[]{:S(2)}, u32[]{:S(2)}) %all-to-all-start) | async-done | bytes 524320 | tf_op jit(solution)/shard_map/all_to_all | solution.py:494
  53.4 1.3 shard_map.105
  54.7 18.9 %all_to_all.43 = bf16[64,16,128]{2,1,0:T(8,128)(2,1)S(1)} all-to-all(bf16[64,16,128]{2,1,0:T(8,128)(2,1)S(1)} %bitcast.37), channel_id=1, replica_groups=mesh['gz'=64,'gy'=4] {'gz'}, dimensions={0} | all-to-all | bytes 524288 | tf_op jit(solution)/shard_map/all_to_all | solution.py:504
  74.1 3.8 %collective-permute-start.5 = (bf16[1024,128]{1,0:T(8,128)(2,1)S(1)}, bf16[1024,128]{1,0:T(8,128)(2,1)S(1)}, u32[]{:S(2)}, u32[]{:S(2)}) collective-permute-start(bf16[1024,128]{1,0:T(8,128)(2,1)S(1)} %bitcast.35), channel_id=1, source_target_pairs={{0,1},{1,0},{2,3},{3,2},{4,5},{5,4},{6,7},{7,6},{8,9},{9,8},{10,11... | collective-permute-start | bytes 786440 | tf_op jit(solution)/shard_map/ppermute | solution.py:507
  78.9 4.7 %collective-permute-start.7 = (bf16[1024,128]{1,0:T(8,128)(2,1)S(1)}, bf16[1024,128]{1,0:T(8,128)(2,1)}, u32[]{:S(2)}, u32[]{:S(2)}) collective-permute-start(bf16[1024,128]{1,0:T(8,128)(2,1)S(1)} %collective-permute-done.6.b2), channel_id=1, source_target_pairs={{0,1},{1,0},{2,3},{3,2},{4,5},{5,4},{6,7},{7,6},{8,9},{9,8},{10,11... | collective-permute-start | bytes 786440 | tf_op jit(solution)/shard_map/ppermute | solution.py:508
  84.9 6.8 %shard_map.106 = (f32[4,24,2048]{2,1,0:T(8,128)S(1)}, bf16[96,2048]{1,0:T(8,128)(2,1)S(1)}, bf16[96,2048]{1,0:T(8,128)(2,1)S(1)}, f32[8,128]{1,0:T(8,128)S(1)}) custom-call(bf16[1024,128]{1,0:T(8,128)(2,1)S(1)} %bitcast.36, bf16[1024,128]{1,0:T(8,128)(2,1)S(1)} %collective-permute-done.5.b1, bf16[1024,128]{1,0:T(8,128)(2,1)S(1)} %collective-permute-done.6.b2, ...), custom_call_target="tpu_custom_call" | custom-call | flops 2147483648 | bytes 4737024 | tf_op jit(solution)/shard_map/pallas_call | solution.py:431
  91.6 2.2 %collective-permute-start.8 = (bf16[96,2048]{1,0:T(8,128)(2,1)S(1)}, bf16[96,2048]{1,0:T(8,128)(2,1)S(1)}, u32[]{:S(2)}, u32[]{:S(2)}) collective-permute-start(bf16[96,2048]{1,0:T(8,128)(2,1)S(1)} %get-tuple-element.40), channel_id=1, source_target_pairs={{0,4},{4,8},{8,12},{12,16},{16,20},{20,24},{24,28},{28,32},{32,36}... | collective-permute-start | bytes 1179656 | tf_op jit(solution)/shard_map/ppermute | solution.py:536
  93.9 1.3 collective-permute-start.9
  95.2 6.8 %collective-permute-done.8.below = bf16[96,2048]{1,0:T(8,128)(2,1)S(1)} collective-permute-done((bf16[96,2048]{1,0:T(8,128)(2,1)S(1)}, bf16[96,2048]{1,0:T(8,128)(2,1)S(1)}, u32[]{:S(2)}, u32[]{:S(2)}) %collective-permute-start.8) | collective-permute-done | bytes 393248 | tf_op jit(solution)/shard_map/ppermute | solution.py:536
  102.0 3.8 %collective-permute-done.9.above = bf16[96,2048]{1,0:T(8,128)(2,1)S(1)} collective-permute-done((bf16[96,2048]{1,0:T(8,128)(2,1)S(1)}, bf16[96,2048]{1,0:T(8,128)(2,1)S(1)}, u32[]{:S(2)}, u32[]{:S(2)}) %collective-permute-start.9) | collective-permute-done | bytes 393248 | tf_op jit(solution)/shard_map/ppermute | solution.py:536
  106.8 26.7 %all_to_all.44 = f32[256,1,128]{2,1,0:T(1,128)S(1)} all-to-all(f32[256,1,128]{2,1,0:T(1,128)S(1)} %bitcast.40), channel_id=1, replica_groups=mesh['gz'=64,'gy'=4] {'gz','gy'}, dimensions={0} | all-to-all | bytes 262144 | tf_op jit(solution)/shard_map/all_to_all | solution.py:539
  133.5 2.2 %shard_map.108 = (f32[8,24,2048]{2,1,0:T(8,128)S(1)}, f32[4,24,2048]{2,1,0:T(8,128)S(1)}, f32[256,128]{1,0:T(8,128)S(1)}) custom-call(f32[256,128]{1,0:T(8,128)S(1)} %bitcast.30, f32[8,128]{1,0:T(8,128)S(1)} %get-tuple-element.42.moved, f32[4,24,2048]{2,1,0:T(8,128)S(1)} %get-tuple-element.39.f, bf16[96,2048]{1,0:T(8,128)(2,1)S(1)} %collective-permute-done.8.below, ...), custom_call_target="tpu_custom_call" | custom-call | flops 23592960 | bytes 4984832 | tf_op jit(solution)/shard_map/pallas_call | solution.py:431
  135.7 18.4 %all_to_all.45 = f32[256,1,128]{2,1,0:T(1,128)S(1)} all-to-all(f32[256,1,128]{2,1,0:T(1,128)S(1)} %bitcast.38), channel_id=1, replica_groups=mesh['gz'=64,'gy'=4] {'gz','gy'}, dimensions={0} | all-to-all | bytes 262144 | tf_op jit(solution)/shard_map/all_to_all | solution.py:539
  154.1 1.7 shard_map.109
  155.9 18.4 %all_to_all.46 = f32[256,1,128]{2,1,0:T(1,128)S(1)} all-to-all(f32[256,1,128]{2,1,0:T(1,128)S(1)} %bitcast.39), channel_id=1, replica_groups=mesh['gz'=64,'gy'=4] {'gz','gy'}, dimensions={0} | all-to-all | bytes 262144 | tf_op jit(solution)/shard_map/all_to_all | solution.py:539
  (41 shorter events, 12.1 us)
Async XLA Ops:
  0.6 14.8 %copy-start = (f32[4,16,2048]{2,1,0:T(8,128)S(1)}, f32[4,16,2048]{2,1,0:T(8,128)}, u32[]{:S(2)}) copy-start(f32[4,16,2048]{2,1,0:T(8,128)} %volume.1) | copy-start | bytes 1572868
  0.6 5.0 %copy-start.8 = (f32[64,16]{0,1:T(8,128)S(1)}, f32[64,16]{0,1:T(8,128)}, u32[]{:S(2)}) copy-start(f32[64,16]{0,1:T(8,128)} %param.13) | copy-start | bytes 12292
  0.7 6.3 %copy-start.10 = (s32[64,16]{0,1:T(8,128)S(1)}, s32[64,16]{0,1:T(8,128)}, u32[]{:S(2)}) copy-start(s32[64,16]{0,1:T(8,128)} %param.16) | copy-start | bytes 12292
  0.7 6.3 %copy-start.9 = (s32[64,16]{0,1:T(8,128)S(1)}, s32[64,16]{0,1:T(8,128)}, u32[]{:S(2)}) copy-start(s32[64,16]{0,1:T(8,128)} %param.15) | copy-start | bytes 12292
  0.7 14.7 %copy-start.3 = (bf16[16,128,128]{2,1,0:T(8,128)(2,1)S(1)}, bf16[16,128,128]{2,1,0:T(8,128)(2,1)}, u32[]{:S(2)}) copy-start(bf16[16,128,128]{2,1,0:T(8,128)(2,1)} %tiles.1) | copy-start | bytes 1572868
  2.5 9.1 %collective-permute-start = (f32[64,1408]{1,0:T(8,128)S(1)}, f32[64,1408]{1,0:T(8,128)S(1)}, u32[]{:S(2)}, u32[]{:S(2)}) collective-permute-start(f32[64,1408]{1,0:T(8,128)S(1)} %select_maximum_fusion), channel_id=1, source_target_pairs={{0,2},{1,3},{2,0},{3,1},{4,6},{5,7},{6,4},{7,5},{8,10},{9,11},{10,... | collective-permute-start | bytes 1081352 | tf_op jit(solution)/shard_map/ppermute | solution.py:462
  5.7 2.4 %collective-permute-start.1 = (f32[64,1152]{1,0:T(8,128)S(1)}, f32[64,1152]{1,0:T(8,128)S(1)}, u32[]{:S(2)}, u32[]{:S(2)}) collective-permute-start(f32[64,1152]{1,0:T(8,128)S(1)} %select_maximum_fusion.1), channel_id=1, source_target_pairs={{0,1},{1,0},{2,3},{3,2},{4,5},{5,4},{6,7},{7,6},{8,9},{9,8},{10,11... | collective-permute-start | bytes 884744 | tf_op jit(solution)/shard_map/ppermute | solution.py:465
  7.0 28.7 %copy-start.4 = (f32[4,16,2048]{2,1,0:T(8,128)S(1)}, f32[4,16,2048]{2,1,0:T(8,128)}, u32[]{:S(2)}) copy-start(f32[4,16,2048]{2,1,0:T(8,128)} %norm.1) | copy-start | bytes 1572868
  11.6 3.8 %collective-permute-start.2 = (f32[64,1408]{1,0:T(8,128)S(1)}, f32[64,1408]{1,0:T(8,128)S(1)}, u32[]{:S(2)}, u32[]{:S(2)}) collective-permute-start(f32[64,1408]{1,0:T(8,128)S(1)} %collective-permute-done.far), channel_id=1, source_target_pairs={{0,1},{1,0},{2,3},{3,2},{4,5},{5,4},{6,7},{7,6},{8,9},{9,8},{10,11... | collective-permute-start | bytes 1081352 | tf_op jit(solution)/shard_map/ppermute | solution.py:467
  21.0 32.4 %copy-start.1 = (f32[1,256,512]{2,1,0:T(8,128)S(1)}, f32[1,256,512]{2,1,0:T(8,128)}, u32[]{:S(2)}) copy-start(f32[1,256,512]{2,1,0:T(8,128)} %param.10) | copy-start | bytes 1572868
  21.0 32.4 %copy-start.2 = (f32[1,256,512]{2,1,0:T(8,128)S(1)}, f32[1,256,512]{2,1,0:T(8,128)}, u32[]{:S(2)}) copy-start(f32[1,256,512]{2,1,0:T(8,128)} %param.11) | copy-start | bytes 1572868
  21.0 32.3 %copy-start.5 = (s32[64,64]{1,0:T(8,128)S(1)}, s32[64,64]{1,0:T(8,128)}, u32[]{:S(2)}) copy-start(s32[64,64]{1,0:T(8,128)} %starts.1) | copy-start | bytes 49156
  21.0 32.3 %all-to-all-start = ((f32[64,16,128]{2,1,0:T(8,128)}), f32[64,16,128]{2,1,0:T(8,128)S(1)}, u32[]{:S(2)}, u32[]{:S(2)}) async-start(f32[64,16,128]{2,1,0:T(8,128)} %bitcast.3), calls=%async_computation | async-start | bytes 1048576 | tf_op jit(solution)/shard_map/all_to_all | solution.py:494
  35.9 9.8 %collective-permute-start.3 = (f32[4,8,2048]{2,1,0:T(8,128)S(1)}, f32[4,8,2048]{2,1,0:T(8,128)S(1)}, u32[]{:S(2)}, u32[]{:S(2)}) collective-permute-start(f32[4,8,2048]{2,1,0:T(8,128)S(1)} %pad_maximum_fusion), channel_id=1, source_target_pairs={{1,0},{2,1},{3,2},{5,4},{6,5},{7,6},{9,8},{10,9},{11,10},{13,12},{... | collective-permute-start | bytes 786440 | tf_op jit(solution)/shard_map/ppermute | solution.py:471
  38.5 8.4 %collective-permute-start.4 = (f32[4,8,2048]{2,1,0:T(8,128)S(1)}, f32[4,8,2048]{2,1,0:T(8,128)S(1)}, u32[]{:S(2)}, u32[]{:S(2)}) collective-permute-start(f32[4,8,2048]{2,1,0:T(8,128)S(1)} %pad_maximum_fusion.1), channel_id=1, source_target_pairs={{0,1},{1,2},{2,3},{4,5},{5,6},{6,7},{8,9},{9,10},{10,11},{12,13},{... | collective-permute-start | bytes 786440 | tf_op jit(solution)/shard_map/ppermute | solution.py:472
  46.9 0.7 copy-start.6
  54.7 30.2 %copy-start.7 = (f32[4,8,2048]{2,1,0:T(8,128)S(1)}, f32[4,8,2048]{2,1,0:T(8,128)}, u32[]{:S(2)}) copy-start(f32[4,8,2048]{2,1,0:T(8,128)} %copy-done.6) | copy-start | bytes 786436
  73.6 5.2 %collective-permute-start.6 = (bf16[1024,128]{1,0:T(8,128)(2,1)S(1)}, bf16[1024,128]{1,0:T(8,128)(2,1)S(1)}, u32[]{:S(2)}, u32[]{:S(2)}) collective-permute-start(bf16[1024,128]{1,0:T(8,128)(2,1)S(1)} %bitcast.34), channel_id=1, source_target_pairs={{0,2},{1,3},{2,0},{3,1},{4,6},{5,7},{6,4},{7,5},{8,10},{9,11},{10,... | collective-permute-start | bytes 786440 | tf_op jit(solution)/shard_map/ppermute | solution.py:506
  74.1 9.8 %collective-permute-start.5 = (bf16[1024,128]{1,0:T(8,128)(2,1)S(1)}, bf16[1024,128]{1,0:T(8,128)(2,1)S(1)}, u32[]{:S(2)}, u32[]{:S(2)}) collective-permute-start(bf16[1024,128]{1,0:T(8,128)(2,1)S(1)} %bitcast.35), channel_id=1, source_target_pairs={{0,1},{1,0},{2,3},{3,2},{4,5},{5,4},{6,7},{7,6},{8,9},{9,8},{10,11... | collective-permute-start | bytes 786440 | tf_op jit(solution)/shard_map/ppermute | solution.py:507
  78.9 6.0 %collective-permute-start.7 = (bf16[1024,128]{1,0:T(8,128)(2,1)S(1)}, bf16[1024,128]{1,0:T(8,128)(2,1)}, u32[]{:S(2)}, u32[]{:S(2)}) collective-permute-start(bf16[1024,128]{1,0:T(8,128)(2,1)S(1)} %collective-permute-done.6.b2), channel_id=1, source_target_pairs={{0,1},{1,0},{2,3},{3,2},{4,5},{5,4},{6,7},{7,6},{8,9},{9,8},{10,11... | collective-permute-start | bytes 786440 | tf_op jit(solution)/shard_map/ppermute | solution.py:508
  91.6 10.3 %collective-permute-start.8 = (bf16[96,2048]{1,0:T(8,128)(2,1)S(1)}, bf16[96,2048]{1,0:T(8,128)(2,1)S(1)}, u32[]{:S(2)}, u32[]{:S(2)}) collective-permute-start(bf16[96,2048]{1,0:T(8,128)(2,1)S(1)} %get-tuple-element.40), channel_id=1, source_target_pairs={{0,4},{4,8},{8,12},{12,16},{16,20},{20,24},{24,28},{28,32},{32,36}... | collective-permute-start | bytes 1179656 | tf_op jit(solution)/shard_map/ppermute | solution.py:536
  93.9 11.9 %collective-permute-start.9 = (bf16[96,2048]{1,0:T(8,128)(2,1)S(1)}, bf16[96,2048]{1,0:T(8,128)(2,1)S(1)}, u32[]{:S(2)}, u32[]{:S(2)}) collective-permute-start(bf16[96,2048]{1,0:T(8,128)(2,1)S(1)} %get-tuple-element.41), channel_id=1, source_target_pairs={{4,0},{8,4},{12,8},{16,12},{20,16},{24,20},{28,24},{32,28},{36,32}... | collective-permute-start | bytes 1179656 | tf_op jit(solution)/shard_map/ppermute | solution.py:536

commit v4 on v3

--- a/solution.py
+++ b/solution.py
@@ -22,6 +22,7 @@
 WINDOW = 8
 REACH = 10
 SLOTS = 8
+CHIP_ROW = 4
 GROUP = 4
 PAIR = 2
 
@@ -213,7 +214,7 @@
 
 def back_kernel(
     b0, b1, b2, b3, small, weights, tiles, volume, norm, after, before,
-    updated, first_planes, last_planes, moved,
+    updated, first_planes, last_planes, far_planes, moved,
     flat, rows_by_tile, lhs, rhs, wide,
     volume_here, norm_here, after_here, before_here, arrived,
 ):
@@ -248,6 +249,7 @@
     inside = inside_rows(block)
     low = iota((HALO, 2 * TILE), 0) < HALO // 2
     squares = jnp.zeros((ROWS, 2 * TILE), F32)
+    starts_row = lax.axis_index("gz") % CHIP_ROW == 0
     kinds = []
     rows = PLANES * ANGLES
 
@@ -295,8 +297,10 @@
                 news.append(new)
                 change = (new - v)[:ROWS]
                 squares = squares + change * change
-            first_planes[:, cut] = packed_end(news)
-            last_planes[:, cut] = packed_end(news[::-1])
+            lower, upper = packed_end(news), packed_end(news[::-1])
+            first_planes[:, cut] = lower.astype(BF16)
+            last_planes[:, cut] = upper.astype(BF16)
+            far_planes[:, cut] = jnp.where(starts_row, lower, upper).astype(BF16)
         return squares
 
     for group in range(XT // GROUP):
@@ -315,11 +319,12 @@
     for plane in others:
         sent.append((plane - held).astype(BF16))
         held = held + sent[-1].astype(F32)
-    return jnp.concatenate([part.astype(F32) for part in sent], axis=0).astype(BF16)
-
-
-def unpack_end(ref, planes):
-    sent = ref[...].astype(F32)
+    return jnp.concatenate([part.astype(F32) for part in sent], axis=0)
+
+
+def unpack_end(ref, far, from_far, planes):
+    rows = (len(planes) + 1) * EXT
+    sent = jnp.where(from_far, far[...].astype(F32)[:rows], ref[...].astype(F32)[:rows])
     held = sent[:EXT]
     for i, plane in enumerate(planes):
         held = held + sent[(i + 1) * EXT : (i + 2) * EXT]
@@ -381,15 +386,16 @@
     parts[...] = jnp.broadcast_to(row, parts.shape)
 
 
-def with_ends(f, below, above, low, high):
+def with_ends(f, below, above, far, low, high):
     count = low.shape[0]
-    unpack_end(below, [low.at[count - 1 - i] for i in range(count)])
-    unpack_end(above, [high.at[i] for i in range(count)])
+    place = lax.axis_index("gz") % CHIP_ROW
+    unpack_end(below, far, place == 0, [low.at[count - 1 - i] for i in range(count)])
+    unpack_end(above, far, place == CHIP_ROW - 1, [high.at[i] for i in range(count)])
     return [*loaders(low), *loaders(f), *loaders(high)]
 
 
-def first_sums_kernel(f, below, above, moved, g_out, parts, low, high):
-    write_sums(with_ends(f, below, above, low, high), moved, g_out, parts)
+def first_sums_kernel(far, f, below, above, moved, g_out, parts, low, high):
+    write_sums(with_ends(f, below, above, far, low, high), moved, g_out, parts)
 
 
 def step_length(sums):
@@ -411,8 +417,8 @@
     write_sums(loaders(f_out), moved, g_out, parts)
 
 
-def second_sums_kernel(sums, moved, f, below, above, g, f_out, g_out, parts, low, high):
-    next_sums(sums, with_ends(f, below, above, low, high), g, moved, f_out, g_out, parts)
+def second_sums_kernel(sums, moved, f, below, above, far, g, f_out, g_out, parts, low, high):
+    next_sums(sums, with_ends(f, below, above, far, low, high), g, moved, f_out, g_out, parts)
 
 
 def third_sums_kernel(sums, moved, f, g, f_out, g_out, parts):
@@ -452,17 +458,18 @@
     kinds, bands = jnp.swapaxes(tile_kind, 0, 1), jnp.swapaxes(tile_band, 0, 1)
     small = jnp.concatenate([(kinds + NK * bands).astype(F32), weight], axis=0)
 
-    def outgoing(rows_sent, weight_sent, first, tiles_sent):
-        columns = lax.dynamic_slice_in_dim(rows_sent, first * TILE, tiles_sent * TILE, axis=1)
+    def outgoing(columns, weight_sent):
         lanes = jnp.pad(weight_sent, ((0, PLANES * ROWS - ROWS), (0, TILE - ANGLES)))
         return jnp.concatenate([columns, lanes], axis=1)
 
-    to_chip = outgoing(flat, weight, jnp.where(block >= 2, 0, XT - REACH), REACH)
+    reach = REACH * TILE
+    to_chip = outgoing(jnp.where(block >= 2, flat[:, :reach], flat[:, WIDTH - reach :]), weight)
     to_chip, flat_later, weight_later = lax.optimization_barrier((to_chip, flat, weight))
     far = lax.ppermute(to_chip, "gy", other_chip)
     beside = block ^ 1
     window = beside * 2 + jnp.where(beside >= 2, 2, 0)
-    near = lax.ppermute(outgoing(flat_later, weight_later, window, WINDOW), "gy", other_core)
+    columns = lax.dynamic_slice_in_dim(flat_later, window * TILE, WINDOW * TILE, axis=1)
+    near = lax.ppermute(outgoing(columns, weight_later), "gy", other_core)
     far, near, small = lax.optimization_barrier((far, near, small))
     farnear = lax.ppermute(far, "gy", other_core)
     half = HALO // 2
@@ -508,9 +515,9 @@
     held_farnear = lax.ppermute(held_far, "gy", other_core)
 
     ends = (((PASSES + 1) * EXT, WIDTH), BF16)
-    f, first, last, moved = call(
+    f, first, last, far_end, moved = call(
         back_kernel,
-        [((PLANES, EXT, WIDTH), F32), ends, ends, ((8, TILE), F32)],
+        [((PLANES, EXT, WIDTH), F32), ends, ends, ends, ((8, TILE), F32)],
         (
             held, held_near, held_far, held_farnear, small, weights,
             jnp.swapaxes(tiles, 1, 2), volume, col_norm, after, before,
@@ -531,9 +538,12 @@
         room=46,
         flops=2 * XT * rows * SLOTS * TILE * 2 * TILE,
     )
-    upward = [(i, i + 1) for i in range(slabs - 1)]
-    downward = [(i + 1, i) for i in range(slabs - 1)]
-    below, above = lax.ppermute(last, "gz", upward), lax.ppermute(first, "gz", downward)
+    pairs = [(i, i + 1) for i in range(slabs - 1)]
+    within = [(i, j) for i, j in pairs if j % CHIP_ROW]
+    across = [(i, j) for i, j in pairs if j % CHIP_ROW == 0]
+    far_end = lax.ppermute(far_end, "gz", across + [(j, i) for i, j in across])
+    below = lax.ppermute(last, "gz", within)
+    above = lax.ppermute(first, "gz", [(j, i) for i, j in within])
 
     def exchanged(parts):
         return lax.all_to_all(parts, ("gz", "gy"), split_axis=0, concat_axis=0, tiled=True)
@@ -544,14 +554,14 @@
     g, parts = call(
         first_sums_kernel,
         [block_ext, partial],
-        (f, below, above, moved),
+        (far_end, f, below, above, moved),
         [pltpu.VMEM((1, EXT, WIDTH), F32), pltpu.VMEM((1, EXT, WIDTH), F32)],
         flops=work * PLANES,
     )
     f, g, parts = call(
         second_sums_kernel,
         [((PLANES + 4, EXT, WIDTH), F32), block_ext, partial],
-        (exchanged(parts), moved, f, below, above, g),
+        (exchanged(parts), moved, f, below, above, far_end, g),
         [pltpu.VMEM((PASSES, EXT, WIDTH), F32), pltpu.VMEM((PASSES, EXT, WIDTH), F32)],
         flops=work * (2 * PLANES + 4),
     )

time: 176 us -> 174 us (0.989)
  blocking collectives: 82.5 us -> 79.4 us
  local copies, waits for them, and re-layouts: 3.19 us -> 1.18 us
    all_to_all x3, blocking collectives: 63.5 us -> 60.4 us  [exchanged(): lax.all_to_all(parts, ('gz', 'gy'), split_axis=0, concat_axis=0, tiled=True)]
    dynamic_slice x2 -> x1, local copies, waits for them, and re-layouts: 2.04 us -> 0.02 us  [per_device(): lax.dynamic_slice_in_dim(flat_later, window * TILE, WINDOW * TILE, axis=1)]
    ppermute x3 -> x4, starting transfers between devices: 4.75 us -> 5.45 us  [the longest x1 2.23 us: per_device(): below = lax.ppermute(last, 'gz', within)]
    ppermute x3 -> x4, waiting for transfers between devices: 11.8 us -> 11.8 us  [the longest x1 6.78 us: per_device(): below = lax.ppermute(last, 'gz', within)]
  transfers between devices with their start and end apart: 11 -> 12, of which waited for: 10 -> 10; matrix products, arithmetic and copies ran while one was open for 1% -> 0% of each run, Pallas kernels for 0% -> 0%
where the time goes in v4:
time: 174 us; the launch traced here: 173 us
  blocking collectives  79.4 us (46%)
  starting transfers between devices  39.2 us (23%)
  waiting for transfers between devices  30.6 us (18%)
  Pallas kernels  19.9 us (11%)
  other arithmetic  2.06 us (1%)
    all_to_all x3, blocking collectives, exchanged(): lax.all_to_all(parts, ('gz', 'gy'), split_axis=0, concat_axis=0, tiled=True)  60.4 us
    pallas_call x7, Pallas kernels, call(): pl.pallas_call(kernel, out_shape=shapes, in_specs=[VMEM] * (len(args) - f...  19.9 us
    all_to_all x1, blocking collectives, per_device(): held = lax.all_to_all(chunks, 'gz', split_axis=0, concat_axis=0, tiled=True)  18.9 us
    all_to_all x1, starting transfers between devices, per_device(): lax.all_to_all(chunks, 'gz', split_axis=0, concat_axis=0, tiled=True)  14.6 us
    ppermute x1, waiting for transfers between devices, per_device(): below = lax.ppermute(last, 'gz', within)  6.78 us
    all_to_all x1, waiting for transfers between devices, per_device(): lax.all_to_all(chunks, 'gz', split_axis=0, concat_axis=0, tiled=True)  5.77 us
    ppermute x1, starting transfers between devices, per_device(): held_farnear = lax.ppermute(held_far, 'gy', other_core)  4.69 us
    ppermute x1, waiting for transfers between devices, per_device(): far = lax.ppermute(to_chip, 'gy', other_chip)  4.37 us
  transfers between devices with their start and end apart: 12, of which 10 were waited for; matrix products, arithmetic and copies ran while one was open for 0% of the time, Pallas kernels for 0%

profile of v4, /device:TPU:1, one launch (start us, length us, event | category | flops | bytes accessed | tf_op | source)
XLA Modules:
  0.0 173.2 jit_solution(13379014259905253652)
XLA Ops:
  2.6 2.2 %collective-permute-start = (f32[64,1408]{1,0:T(8,128)S(1)}, f32[64,1408]{1,0:T(8,128)S(1)}, u32[]{:S(2)}, u32[]{:S(2)}) collective-permute-start(f32[64,1408]{1,0:T(8,128)S(1)} %select_maximum_fusion), channel_id=1, source_target_pairs={{0,2},{1,3},{2,0},{3,1},{4,6},{5,7},{6,4},{7,5},{8,10},{9,11},{10,... | collective-permute-start | bytes 1081352 | tf_op jit(solution)/shard_map/ppermute | solution.py:468
  7.3 4.4 %collective-permute-done.far = f32[64,1408]{1,0:T(8,128)S(1)} collective-permute-done((f32[64,1408]{1,0:T(8,128)S(1)}, f32[64,1408]{1,0:T(8,128)S(1)}, u32[]{:S(2)}, u32[]{:S(2)}) %collective-permute-start) | collective-permute-done | bytes 360480 | tf_op jit(solution)/shard_map/ppermute | solution.py:468
  11.7 2.5 %collective-permute-start.2 = (f32[64,1408]{1,0:T(8,128)S(1)}, f32[64,1408]{1,0:T(8,128)S(1)}, u32[]{:S(2)}, u32[]{:S(2)}) collective-permute-start(f32[64,1408]{1,0:T(8,128)S(1)} %collective-permute-done.far), channel_id=1, source_target_pairs={{0,1},{1,0},{2,3},{3,2},{4,5},{5,4},{6,7},{7,6},{8,9},{9,8},{10,11... | collective-permute-start | bytes 1081352 | tf_op jit(solution)/shard_map/ppermute | solution.py:474
  14.2 1.3 collective-permute-done.2.farnear
  15.5 5.6 %shard_map.104 = (f32[1024,128]{1,0:T(8,128)}, f32[24,64]{1,0:T(8,128)S(1)}) custom-call(f32[64,1408]{1,0:T(8,128)S(1)} %collective-permute-done.far, f32[64,1408]{1,0:T(8,128)S(1)} %collective-permute-done.2.farnear, f32[64,1152]{1,0:T(8,128)S(1)} %collective-permute-done.1.near, f32[32,64]{1,0:T(8,128)S(1)} %pad_maximum_fusion.2.small, ...), custom_call_target="tpu_custom_call" | custom-call | flops 2147483648 | bytes 2603008 | tf_op jit(solution)/shard_map/pallas_call | solution.py:437
  21.2 14.6 %all-to-all-start = ((f32[64,16,128]{2,1,0:T(8,128)}), f32[64,16,128]{2,1,0:T(8,128)S(1)}, u32[]{:S(2)}, u32[]{:S(2)}) async-start(f32[64,16,128]{2,1,0:T(8,128)} %bitcast.3), calls=%async_computation | async-start | bytes 1048576 | tf_op jit(solution)/shard_map/all_to_all | solution.py:501
  35.9 2.6 %collective-permute-start.3 = (f32[4,8,2048]{2,1,0:T(8,128)S(1)}, f32[4,8,2048]{2,1,0:T(8,128)S(1)}, u32[]{:S(2)}, u32[]{:S(2)}) collective-permute-start(f32[4,8,2048]{2,1,0:T(8,128)S(1)} %pad_maximum_fusion), channel_id=1, source_target_pairs={{1,0},{2,1},{3,2},{5,4},{6,5},{7,6},{9,8},{10,9},{11,10},{13,12},{... | collective-permute-start | bytes 786440 | tf_op jit(solution)/shard_map/ppermute | solution.py:478
  38.6 3.0 %collective-permute-start.4 = (f32[4,8,2048]{2,1,0:T(8,128)S(1)}, f32[4,8,2048]{2,1,0:T(8,128)S(1)}, u32[]{:S(2)}, u32[]{:S(2)}) collective-permute-start(f32[4,8,2048]{2,1,0:T(8,128)S(1)} %pad_maximum_fusion.1), channel_id=1, source_target_pairs={{0,1},{1,2},{2,3},{4,5},{5,6},{6,7},{8,9},{9,10},{10,11},{12,13},{... | collective-permute-start | bytes 786440 | tf_op jit(solution)/shard_map/ppermute | solution.py:479
  41.6 4.2 %collective-permute-done.3.after = f32[4,8,2048]{2,1,0:T(8,128)S(1)} collective-permute-done((f32[4,8,2048]{2,1,0:T(8,128)S(1)}, f32[4,8,2048]{2,1,0:T(8,128)S(1)}, u32[]{:S(2)}, u32[]{:S(2)}) %collective-permute-start.3) | collective-permute-done | bytes 262176 | tf_op jit(solution)/shard_map/ppermute | solution.py:478
  47.7 5.8 %all-to-all-done = f32[64,16,128]{2,1,0:T(8,128)S(1)} async-done(((f32[64,16,128]{2,1,0:T(8,128)}), f32[64,16,128]{2,1,0:T(8,128)S(1)}, u32[]{:S(2)}, u32[]{:S(2)}) %all-to-all-start) | async-done | bytes 524320 | tf_op jit(solution)/shard_map/all_to_all | solution.py:501
  53.5 1.3 shard_map.105
  54.8 18.9 %all_to_all.43 = bf16[64,16,128]{2,1,0:T(8,128)(2,1)S(1)} all-to-all(bf16[64,16,128]{2,1,0:T(8,128)(2,1)S(1)} %bitcast.37), channel_id=1, replica_groups=mesh['gz'=64,'gy'=4] {'gz'}, dimensions={0} | all-to-all | bytes 524288 | tf_op jit(solution)/shard_map/all_to_all | solution.py:511
  74.1 3.8 %collective-permute-start.5 = (bf16[1024,128]{1,0:T(8,128)(2,1)S(1)}, bf16[1024,128]{1,0:T(8,128)(2,1)S(1)}, u32[]{:S(2)}, u32[]{:S(2)}) collective-permute-start(bf16[1024,128]{1,0:T(8,128)(2,1)S(1)} %bitcast.35), channel_id=1, source_target_pairs={{0,1},{1,0},{2,3},{3,2},{4,5},{5,4},{6,7},{7,6},{8,9},{9,8},{10,11... | collective-permute-start | bytes 786440 | tf_op jit(solution)/shard_map/ppermute | solution.py:514
  79.0 4.7 %collective-permute-start.7 = (bf16[1024,128]{1,0:T(8,128)(2,1)S(1)}, bf16[1024,128]{1,0:T(8,128)(2,1)}, u32[]{:S(2)}, u32[]{:S(2)}) collective-permute-start(bf16[1024,128]{1,0:T(8,128)(2,1)S(1)} %collective-permute-done.6.b2), channel_id=1, source_target_pairs={{0,1},{1,0},{2,3},{3,2},{4,5},{5,4},{6,7},{7,6},{8,9},{9,8},{10,11... | collective-permute-start | bytes 786440 | tf_op jit(solution)/shard_map/ppermute | solution.py:515
  84.9 6.8 %shard_map.106 = (f32[4,24,2048]{2,1,0:T(8,128)S(1)}, bf16[96,2048]{1,0:T(8,128)(2,1)S(1)}, bf16[96,2048]{1,0:T(8,128)(2,1)S(1)}, bf16[96,2048]{1,0:T(8,128)(2,1)S(1)}, f32[8,128]{1,0:T(8,128)S(1)}) custom-call(bf16[1024,128]{1,0:T(8,128)(2,1)S(1)} %bitcast.36, bf16[1024,128]{1,0:T(8,128)(2,1)S(1)} %collective-permute-done.5.b1, ...), custom_call_target="tpu_custom_call" | custom-call | flops 2147483648 | bytes 5130240 | tf_op jit(solution)/shard_map/pallas_call | solution.py:437
  92.4 2.2 %collective-permute-start.9 = (bf16[96,2048]{1,0:T(8,128)(2,1)S(1)}, bf16[96,2048]{1,0:T(8,128)(2,1)S(1)}, u32[]{:S(2)}, u32[]{:S(2)}) collective-permute-start(bf16[96,2048]{1,0:T(8,128)(2,1)S(1)} %get-tuple-element.42), channel_id=1, source_target_pairs={{0,4},{4,8},{8,12},{16,20},{20,24},{24,28},{32,36},{36,40},{40,44}... | collective-permute-start | bytes 1179656 | tf_op jit(solution)/shard_map/ppermute | solution.py:545
  94.7 1.3 collective-permute-start.10
  96.0 6.8 %collective-permute-done.9.below = bf16[96,2048]{1,0:T(8,128)(2,1)S(1)} collective-permute-done((bf16[96,2048]{1,0:T(8,128)(2,1)S(1)}, bf16[96,2048]{1,0:T(8,128)(2,1)S(1)}, u32[]{:S(2)}, u32[]{:S(2)}) %collective-permute-start.9) | collective-permute-done | bytes 393248 | tf_op jit(solution)/shard_map/ppermute | solution.py:545
  102.8 3.8 %collective-permute-done.10.above = bf16[96,2048]{1,0:T(8,128)(2,1)S(1)} collective-permute-done((bf16[96,2048]{1,0:T(8,128)(2,1)S(1)}, bf16[96,2048]{1,0:T(8,128)(2,1)S(1)}, u32[]{:S(2)}, u32[]{:S(2)}) %collective-permute-start.10) | collective-permute-done | bytes 393248 | tf_op jit(solution)/shard_map/ppermute | solution.py:546
  107.7 23.6 %all_to_all.44 = f32[256,1,128]{2,1,0:T(1,128)S(1)} all-to-all(f32[256,1,128]{2,1,0:T(1,128)S(1)} %bitcast.40), channel_id=1, replica_groups=mesh['gz'=64,'gy'=4] {'gz','gy'}, dimensions={0} | all-to-all | bytes 262144 | tf_op jit(solution)/shard_map/all_to_all | solution.py:549
  131.3 2.3 %shard_map.108 = (f32[8,24,2048]{2,1,0:T(8,128)S(1)}, f32[4,24,2048]{2,1,0:T(8,128)S(1)}, f32[256,128]{1,0:T(8,128)S(1)}) custom-call(f32[256,128]{1,0:T(8,128)S(1)} %bitcast.30, f32[8,128]{1,0:T(8,128)S(1)} %get-tuple-element.44.moved, f32[4,24,2048]{2,1,0:T(8,128)S(1)} %get-tuple-element.41.f, bf16[96,2048]{1,0:T(8,128)(2,1)S(1)} %collective-permute-done.9.below, ...), custom_call_target="tpu_custom_call" | custom-call | flops 23592960 | bytes 5378048 | tf_op jit(solution)/shard_map/pallas_call | solution.py:437
  133.6 18.4 %all_to_all.45 = f32[256,1,128]{2,1,0:T(1,128)S(1)} all-to-all(f32[256,1,128]{2,1,0:T(1,128)S(1)} %bitcast.38), channel_id=1, replica_groups=mesh['gz'=64,'gy'=4] {'gz','gy'}, dimensions={0} | all-to-all | bytes 262144 | tf_op jit(solution)/shard_map/all_to_all | solution.py:549
  152.1 1.7 %shard_map.109 = (f32[6,24,2048]{2,1,0:T(8,128)S(1)}, f32[4,24,2048]{2,1,0:T(8,128)S(1)}, f32[256,128]{1,0:T(8,128)S(1)}) custom-call(f32[256,128]{1,0:T(8,128)S(1)} %bitcast.31, f32[8,128]{1,0:T(8,128)S(1)} %get-tuple-element.44.moved, f32[8,24,2048]{2,1,0:T(8,128)S(1)} %get-tuple-element.48.f, f32[4,24,2048]{2,1,0:T(8,128)S(1)} %get-tuple-element.49.g), custom_call_target="tpu_custom_call" | custom-call | flops 19660800 | bytes 4591616 | tf_op jit(solution)/shard_map/pallas_call | solution.py:437
  153.8 18.4 %all_to_all.46 = f32[256,1,128]{2,1,0:T(1,128)S(1)} all-to-all(f32[256,1,128]{2,1,0:T(1,128)S(1)} %bitcast.39), channel_id=1, replica_groups=mesh['gz'=64,'gy'=4] {'gz','gy'}, dimensions={0} | all-to-all | bytes 262144 | tf_op jit(solution)/shard_map/all_to_all | solution.py:549
  (43 shorter events, 12.1 us)
Async XLA Ops:
  0.6 4.2 %copy-start = (f32[4,16,2048]{2,1,0:T(8,128)S(1)}, f32[4,16,2048]{2,1,0:T(8,128)}, u32[]{:S(2)}) copy-start(f32[4,16,2048]{2,1,0:T(8,128)} %volume.1) | copy-start | bytes 1572868
  0.6 4.2 %copy-start.8 = (f32[64,16]{0,1:T(8,128)S(1)}, f32[64,16]{0,1:T(8,128)}, u32[]{:S(2)}) copy-start(f32[64,16]{0,1:T(8,128)} %param.13) | copy-start | bytes 12292
  0.7 5.5 %copy-start.10 = (s32[64,16]{0,1:T(8,128)S(1)}, s32[64,16]{0,1:T(8,128)}, u32[]{:S(2)}) copy-start(s32[64,16]{0,1:T(8,128)} %param.16) | copy-start | bytes 12292
  0.7 5.5 %copy-start.9 = (s32[64,16]{0,1:T(8,128)S(1)}, s32[64,16]{0,1:T(8,128)}, u32[]{:S(2)}) copy-start(s32[64,16]{0,1:T(8,128)} %param.15) | copy-start | bytes 12292
  0.7 14.8 %copy-start.3 = (bf16[16,128,128]{2,1,0:T(8,128)(2,1)S(1)}, bf16[16,128,128]{2,1,0:T(8,128)(2,1)}, u32[]{:S(2)}) copy-start(bf16[16,128,128]{2,1,0:T(8,128)(2,1)} %tiles.1) | copy-start | bytes 1572868
  2.6 9.1 %collective-permute-start = (f32[64,1408]{1,0:T(8,128)S(1)}, f32[64,1408]{1,0:T(8,128)S(1)}, u32[]{:S(2)}, u32[]{:S(2)}) collective-permute-start(f32[64,1408]{1,0:T(8,128)S(1)} %select_maximum_fusion), channel_id=1, source_target_pairs={{0,2},{1,3},{2,0},{3,1},{4,6},{5,7},{6,4},{7,5},{8,10},{9,11},{10,... | collective-permute-start | bytes 1081352 | tf_op jit(solution)/shard_map/ppermute | solution.py:468
  4.9 2.5 %collective-permute-start.1 = (f32[64,1152]{1,0:T(8,128)S(1)}, f32[64,1152]{1,0:T(8,128)S(1)}, u32[]{:S(2)}, u32[]{:S(2)}) collective-permute-start(f32[64,1152]{1,0:T(8,128)S(1)} %select_maximum_fusion.1), channel_id=1, source_target_pairs={{0,1},{1,0},{2,3},{3,2},{4,5},{5,4},{6,7},{7,6},{8,9},{9,8},{10,11... | collective-permute-start | bytes 884744 | tf_op jit(solution)/shard_map/ppermute | solution.py:472
  6.2 29.6 %copy-start.4 = (f32[4,16,2048]{2,1,0:T(8,128)S(1)}, f32[4,16,2048]{2,1,0:T(8,128)}, u32[]{:S(2)}) copy-start(f32[4,16,2048]{2,1,0:T(8,128)} %norm.1) | copy-start | bytes 1572868
  11.7 3.8 %collective-permute-start.2 = (f32[64,1408]{1,0:T(8,128)S(1)}, f32[64,1408]{1,0:T(8,128)S(1)}, u32[]{:S(2)}, u32[]{:S(2)}) collective-permute-start(f32[64,1408]{1,0:T(8,128)S(1)} %collective-permute-done.far), channel_id=1, source_target_pairs={{0,1},{1,0},{2,3},{3,2},{4,5},{5,4},{6,7},{7,6},{8,9},{9,8},{10,11... | collective-permute-start | bytes 1081352 | tf_op jit(solution)/shard_map/ppermute | solution.py:474
  21.1 32.3 %copy-start.1 = (f32[1,256,512]{2,1,0:T(8,128)S(1)}, f32[1,256,512]{2,1,0:T(8,128)}, u32[]{:S(2)}) copy-start(f32[1,256,512]{2,1,0:T(8,128)} %param.10) | copy-start | bytes 1572868
  21.1 32.3 %copy-start.2 = (f32[1,256,512]{2,1,0:T(8,128)S(1)}, f32[1,256,512]{2,1,0:T(8,128)}, u32[]{:S(2)}) copy-start(f32[1,256,512]{2,1,0:T(8,128)} %param.11) | copy-start | bytes 1572868
  21.1 32.3 %copy-start.5 = (s32[64,64]{1,0:T(8,128)S(1)}, s32[64,64]{1,0:T(8,128)}, u32[]{:S(2)}) copy-start(s32[64,64]{1,0:T(8,128)} %starts.1) | copy-start | bytes 49156
  21.2 32.3 %all-to-all-start = ((f32[64,16,128]{2,1,0:T(8,128)}), f32[64,16,128]{2,1,0:T(8,128)S(1)}, u32[]{:S(2)}, u32[]{:S(2)}) async-start(f32[64,16,128]{2,1,0:T(8,128)} %bitcast.3), calls=%async_computation | async-start | bytes 1048576 | tf_op jit(solution)/shard_map/all_to_all | solution.py:501
  35.9 9.8 %collective-permute-start.3 = (f32[4,8,2048]{2,1,0:T(8,128)S(1)}, f32[4,8,2048]{2,1,0:T(8,128)S(1)}, u32[]{:S(2)}, u32[]{:S(2)}) collective-permute-start(f32[4,8,2048]{2,1,0:T(8,128)S(1)} %pad_maximum_fusion), channel_id=1, source_target_pairs={{1,0},{2,1},{3,2},{5,4},{6,5},{7,6},{9,8},{10,9},{11,10},{13,12},{... | collective-permute-start | bytes 786440 | tf_op jit(solution)/shard_map/ppermute | solution.py:478
  38.6 8.4 %collective-permute-start.4 = (f32[4,8,2048]{2,1,0:T(8,128)S(1)}, f32[4,8,2048]{2,1,0:T(8,128)S(1)}, u32[]{:S(2)}, u32[]{:S(2)}) collective-permute-start(f32[4,8,2048]{2,1,0:T(8,128)S(1)} %pad_maximum_fusion.1), channel_id=1, source_target_pairs={{0,1},{1,2},{2,3},{4,5},{5,6},{6,7},{8,9},{9,10},{10,11},{12,13},{... | collective-permute-start | bytes 786440 | tf_op jit(solution)/shard_map/ppermute | solution.py:479
  47.0 0.7 copy-start.6
  54.8 30.1 %copy-start.7 = (f32[4,8,2048]{2,1,0:T(8,128)S(1)}, f32[4,8,2048]{2,1,0:T(8,128)}, u32[]{:S(2)}) copy-start(f32[4,8,2048]{2,1,0:T(8,128)} %copy-done.6) | copy-start | bytes 786436
  73.7 5.2 %collective-permute-start.6 = (bf16[1024,128]{1,0:T(8,128)(2,1)S(1)}, bf16[1024,128]{1,0:T(8,128)(2,1)S(1)}, u32[]{:S(2)}, u32[]{:S(2)}) collective-permute-start(bf16[1024,128]{1,0:T(8,128)(2,1)S(1)} %bitcast.34), channel_id=1, source_target_pairs={{0,2},{1,3},{2,0},{3,1},{4,6},{5,7},{6,4},{7,5},{8,10},{9,11},{10,... | collective-permute-start | bytes 786440 | tf_op jit(solution)/shard_map/ppermute | solution.py:513
  74.1 9.8 %collective-permute-start.5 = (bf16[1024,128]{1,0:T(8,128)(2,1)S(1)}, bf16[1024,128]{1,0:T(8,128)(2,1)S(1)}, u32[]{:S(2)}, u32[]{:S(2)}) collective-permute-start(bf16[1024,128]{1,0:T(8,128)(2,1)S(1)} %bitcast.35), channel_id=1, source_target_pairs={{0,1},{1,0},{2,3},{3,2},{4,5},{5,4},{6,7},{7,6},{8,9},{9,8},{10,11... | collective-permute-start | bytes 786440 | tf_op jit(solution)/shard_map/ppermute | solution.py:514
  79.0 6.0 %collective-permute-start.7 = (bf16[1024,128]{1,0:T(8,128)(2,1)S(1)}, bf16[1024,128]{1,0:T(8,128)(2,1)}, u32[]{:S(2)}, u32[]{:S(2)}) collective-permute-start(bf16[1024,128]{1,0:T(8,128)(2,1)S(1)} %collective-permute-done.6.b2), channel_id=1, source_target_pairs={{0,1},{1,0},{2,3},{3,2},{4,5},{5,4},{6,7},{7,6},{8,9},{9,8},{10,11... | collective-permute-start | bytes 786440 | tf_op jit(solution)/shard_map/ppermute | solution.py:515
  91.8 4.2 %collective-permute-start.8 = (bf16[96,2048]{1,0:T(8,128)(2,1)S(1)}, bf16[96,2048]{1,0:T(8,128)(2,1)S(1)}, u32[]{:S(2)}, u32[]{:S(2)}) collective-permute-start(bf16[96,2048]{1,0:T(8,128)(2,1)S(1)} %get-tuple-element.40), channel_id=1, source_target_pairs={{12,16},{28,32},{44,48},{60,64},{76,80},{92,96},{108,112},{124,128... | collective-permute-start | bytes 1179656 | tf_op jit(solution)/shard_map/ppermute | solution.py:544
  92.4 10.3 %collective-permute-start.9 = (bf16[96,2048]{1,0:T(8,128)(2,1)S(1)}, bf16[96,2048]{1,0:T(8,128)(2,1)S(1)}, u32[]{:S(2)}, u32[]{:S(2)}) collective-permute-start(bf16[96,2048]{1,0:T(8,128)(2,1)S(1)} %get-tuple-element.42), channel_id=1, source_target_pairs={{0,4},{4,8},{8,12},{16,20},{20,24},{24,28},{32,36},{36,40},{40,44}... | collective-permute-start | bytes 1179656 | tf_op jit(solution)/shard_map/ppermute | solution.py:545
  94.7 11.9 %collective-permute-start.10 = (bf16[96,2048]{1,0:T(8,128)(2,1)S(1)}, bf16[96,2048]{1,0:T(8,128)(2,1)S(1)}, u32[]{:S(2)}, u32[]{:S(2)}) collective-permute-start(bf16[96,2048]{1,0:T(8,128)(2,1)S(1)} %get-tuple-element.43), channel_id=1, source_target_pairs={{4,0},{8,4},{12,8},{20,16},{24,20},{28,24},{36,32},{40,36},{44,40}... | collective-permute-start | bytes 1179656 | tf_op jit(solution)/shard_map/ppermute | solution.py:546

commit v5 on v4

--- a/solution.py
+++ b/solution.py
@@ -260,13 +260,13 @@
             kinds.append(kind)
             masks = slot_masks(kind)
             near = [t for t in range(j - 2, j + 3) if 0 <= t < XT]
-            at_band = [onehot(band == t, BF16) for t in near]
+            at_band = [band == t for t in near]
             for z in range(PLANES):
                 here = slice(z * ANGLES, (z + 1) * ANGLES)
                 chosen = None
                 for t, mask in zip(near, at_band):
-                    term = rows_by_tile[t, here, :] * mask
-                    chosen = term if chosen is None else chosen + term
+                    term = rows_by_tile[t, here, :]
+                    chosen = term if chosen is None else jnp.where(mask, term, chosen)
                 first = (j * PLANES + z) * ANGLES
                 for k in range(SLOTS):
                     lhs[first : first + ANGLES, k * TILE : (k + 1) * TILE] = chosen * masks[k]
@@ -297,7 +297,7 @@
                 news.append(new)
                 change = (new - v)[:ROWS]
                 squares = squares + change * change
-            lower, upper = packed_end(news), packed_end(news[::-1])
+            lower, upper = packed_end(news, False), packed_end(news[::-1], True)
             first_planes[:, cut] = lower.astype(BF16)
             last_planes[:, cut] = upper.astype(BF16)
             far_planes[:, cut] = jnp.where(starts_row, lower, upper).astype(BF16)
@@ -312,22 +312,36 @@
     moved[...] = jnp.where(iota((8, TILE), 1) == 0, total, 0.0)
 
 
-def packed_end(planes):
+def shared_rows(last):
+    row = iota((HALO, 1), 0)
+    return ((row >= 3) & (row < 7), 3) if last else ((row >= 1) & (row < 5), HALO - 3)
+
+
+def packed_end(planes, last):
     near, *others = planes[:PASSES]
-    sent = pieces(near, 2)
-    held = sent[0].astype(F32) + sent[1].astype(F32)
+    sent = [part.astype(F32) for part in pieces(near, 2)]
+    held = sent[0] + sent[1]
     for plane in others:
-        sent.append((plane - held).astype(BF16))
-        held = held + sent[-1].astype(F32)
-    return jnp.concatenate([part.astype(F32) for part in sent], axis=0)
-
-
-def unpack_end(ref, far, from_far, planes):
-    rows = (len(planes) + 1) * EXT
-    sent = jnp.where(from_far, far[...].astype(F32)[:rows], ref[...].astype(F32)[:rows])
+        sent.append((plane - held).astype(BF16).astype(F32))
+        held = held + sent[-1]
+    second, third = sent[2:]
+    from_third, shift = shared_rows(last)
+    shared = jnp.where(from_third, pltpu.roll(third[ROWS:], shift, 0), second[ROWS:])
+    return jnp.concatenate([*sent[:2], second[:ROWS], third[:ROWS], shared], axis=0)
+
+
+def unpack_end(ref, far, from_far, last, planes):
+    sent = jnp.where(from_far, far[...].astype(F32), ref[...].astype(F32))
+    second, third, shared = 2 * EXT, 2 * EXT + ROWS, 2 * EXT + 2 * ROWS
+    rolled = pltpu.roll(sent[shared:], HALO - shared_rows(last)[1], 0)
+    steps = (
+        sent[EXT:second],
+        jnp.concatenate([sent[second:third], sent[shared:]], axis=0),
+        jnp.concatenate([sent[third:shared], rolled], axis=0),
+    )
     held = sent[:EXT]
-    for i, plane in enumerate(planes):
-        held = held + sent[(i + 1) * EXT : (i + 2) * EXT]
+    for step, plane in zip(steps, planes):
+        held = held + step
         plane[...] = held
 
 
@@ -389,8 +403,9 @@
 def with_ends(f, below, above, far, low, high):
     count = low.shape[0]
     place = lax.axis_index("gz") % CHIP_ROW
-    unpack_end(below, far, place == 0, [low.at[count - 1 - i] for i in range(count)])
-    unpack_end(above, far, place == CHIP_ROW - 1, [high.at[i] for i in range(count)])
+    unpack_end(below, far, place == 0, True, [low.at[count - 1 - i] for i in range(count)])
+    far_above = place == CHIP_ROW - 1
+    unpack_end(above, far, far_above, False, [high.at[i] for i in range(count)])
     return [*loaders(low), *loaders(f), *loaders(high)]
 
 
@@ -514,7 +529,7 @@
     held_near = lax.ppermute(held, "gy", other_core)
     held_farnear = lax.ppermute(held_far, "gy", other_core)
 
-    ends = (((PASSES + 1) * EXT, WIDTH), BF16)
+    ends = ((2 * (EXT + ROWS) + HALO, WIDTH), BF16)
     f, first, last, far_end, moved = call(
         back_kernel,
         [((PLANES, EXT, WIDTH), F32), ends, ends, ends, ((8, TILE), F32)],

time: 174 us -> 173 us (level)
  no operation moved by 1% of the time
where the time goes in v5:
time: 173 us; the launch traced here: 172 us
  blocking collectives  79.4 us (46%)
  starting transfers between devices  39.2 us (23%)
  waiting for transfers between devices  29.9 us (17%)
  Pallas kernels  19.5 us (11%)
  other arithmetic  2.06 us (1%)
    all_to_all x3, blocking collectives, exchanged(): lax.all_to_all(parts, ('gz', 'gy'), split_axis=0, concat_axis=0, tiled=True)  60.4 us
    pallas_call x7, Pallas kernels, call(): pl.pallas_call(kernel, out_shape=shapes, in_specs=[VMEM] * (len(args) - f...  19.5 us
    all_to_all x1, blocking collectives, per_device(): held = lax.all_to_all(chunks, 'gz', split_axis=0, concat_axis=0, tiled=True)  18.9 us
    all_to_all x1, starting transfers between devices, per_device(): lax.all_to_all(chunks, 'gz', split_axis=0, concat_axis=0, tiled=True)  14.6 us
    ppermute x1, waiting for transfers between devices, per_device(): below = lax.ppermute(last, 'gz', within)  6.08 us
    all_to_all x1, waiting for transfers between devices, per_device(): lax.all_to_all(chunks, 'gz', split_axis=0, concat_axis=0, tiled=True)  5.77 us
    ppermute x1, starting transfers between devices, per_device(): held_farnear = lax.ppermute(held_far, 'gy', other_core)  4.69 us
    ppermute x1, waiting for transfers between devices, per_device(): far = lax.ppermute(to_chip, 'gy', other_chip)  4.37 us
  transfers between devices with their start and end apart: 12, of which 10 were waited for; matrix products, arithmetic and copies ran while one was open for 0% of the time, Pallas kernels for 0%

profile of v5, /device:TPU:1, one launch (start us, length us, event | category | flops | bytes accessed | tf_op | source)
XLA Modules:
  0.0 172.1 jit_solution(12386463892105886277)
XLA Ops:
  2.6 2.2 %collective-permute-start = (f32[64,1408]{1,0:T(8,128)S(1)}, f32[64,1408]{1,0:T(8,128)S(1)}, u32[]{:S(2)}, u32[]{:S(2)}) collective-permute-start(f32[64,1408]{1,0:T(8,128)S(1)} %select_maximum_fusion), channel_id=1, source_target_pairs={{0,2},{1,3},{2,0},{3,1},{4,6},{5,7},{6,4},{7,5},{8,10},{9,11},{10,... | collective-permute-start | bytes 1081352 | tf_op jit(solution)/shard_map/ppermute | solution.py:483
  7.3 4.4 %collective-permute-done.far = f32[64,1408]{1,0:T(8,128)S(1)} collective-permute-done((f32[64,1408]{1,0:T(8,128)S(1)}, f32[64,1408]{1,0:T(8,128)S(1)}, u32[]{:S(2)}, u32[]{:S(2)}) %collective-permute-start) | collective-permute-done | bytes 360480 | tf_op jit(solution)/shard_map/ppermute | solution.py:483
  11.7 2.5 %collective-permute-start.2 = (f32[64,1408]{1,0:T(8,128)S(1)}, f32[64,1408]{1,0:T(8,128)S(1)}, u32[]{:S(2)}, u32[]{:S(2)}) collective-permute-start(f32[64,1408]{1,0:T(8,128)S(1)} %collective-permute-done.far), channel_id=1, source_target_pairs={{0,1},{1,0},{2,3},{3,2},{4,5},{5,4},{6,7},{7,6},{8,9},{9,8},{10,11... | collective-permute-start | bytes 1081352 | tf_op jit(solution)/shard_map/ppermute | solution.py:489
  14.2 1.3 collective-permute-done.2.farnear
  15.5 5.6 %shard_map.104 = (f32[1024,128]{1,0:T(8,128)}, f32[24,64]{1,0:T(8,128)S(1)}) custom-call(f32[64,1408]{1,0:T(8,128)S(1)} %collective-permute-done.far, f32[64,1408]{1,0:T(8,128)S(1)} %collective-permute-done.2.farnear, f32[64,1152]{1,0:T(8,128)S(1)} %collective-permute-done.1.near, f32[32,64]{1,0:T(8,128)S(1)} %pad_maximum_fusion.2.small, ...), custom_call_target="tpu_custom_call" | custom-call | flops 2147483648 | bytes 2603008 | tf_op jit(solution)/shard_map/pallas_call | solution.py:452
  21.2 14.6 %all-to-all-start = ((f32[64,16,128]{2,1,0:T(8,128)}), f32[64,16,128]{2,1,0:T(8,128)S(1)}, u32[]{:S(2)}, u32[]{:S(2)}) async-start(f32[64,16,128]{2,1,0:T(8,128)} %bitcast.3), calls=%async_computation | async-start | bytes 1048576 | tf_op jit(solution)/shard_map/all_to_all | solution.py:516
  35.9 2.6 %collective-permute-start.3 = (f32[4,8,2048]{2,1,0:T(8,128)S(1)}, f32[4,8,2048]{2,1,0:T(8,128)S(1)}, u32[]{:S(2)}, u32[]{:S(2)}) collective-permute-start(f32[4,8,2048]{2,1,0:T(8,128)S(1)} %pad_maximum_fusion), channel_id=1, source_target_pairs={{1,0},{2,1},{3,2},{5,4},{6,5},{7,6},{9,8},{10,9},{11,10},{13,12},{... | collective-permute-start | bytes 786440 | tf_op jit(solution)/shard_map/ppermute | solution.py:493
  38.6 3.0 %collective-permute-start.4 = (f32[4,8,2048]{2,1,0:T(8,128)S(1)}, f32[4,8,2048]{2,1,0:T(8,128)S(1)}, u32[]{:S(2)}, u32[]{:S(2)}) collective-permute-start(f32[4,8,2048]{2,1,0:T(8,128)S(1)} %pad_maximum_fusion.1), channel_id=1, source_target_pairs={{0,1},{1,2},{2,3},{4,5},{5,6},{6,7},{8,9},{9,10},{10,11},{12,13},{... | collective-permute-start | bytes 786440 | tf_op jit(solution)/shard_map/ppermute | solution.py:494
  41.6 4.2 %collective-permute-done.3.after = f32[4,8,2048]{2,1,0:T(8,128)S(1)} collective-permute-done((f32[4,8,2048]{2,1,0:T(8,128)S(1)}, f32[4,8,2048]{2,1,0:T(8,128)S(1)}, u32[]{:S(2)}, u32[]{:S(2)}) %collective-permute-start.3) | collective-permute-done | bytes 262176 | tf_op jit(solution)/shard_map/ppermute | solution.py:493
  47.7 5.8 %all-to-all-done = f32[64,16,128]{2,1,0:T(8,128)S(1)} async-done(((f32[64,16,128]{2,1,0:T(8,128)}), f32[64,16,128]{2,1,0:T(8,128)S(1)}, u32[]{:S(2)}, u32[]{:S(2)}) %all-to-all-start) | async-done | bytes 524320 | tf_op jit(solution)/shard_map/all_to_all | solution.py:516
  53.5 1.3 shard_map.105
  54.8 18.9 %all_to_all.43 = bf16[64,16,128]{2,1,0:T(8,128)(2,1)S(1)} all-to-all(bf16[64,16,128]{2,1,0:T(8,128)(2,1)S(1)} %bitcast.37), channel_id=1, replica_groups=mesh['gz'=64,'gy'=4] {'gz'}, dimensions={0} | all-to-all | bytes 524288 | tf_op jit(solution)/shard_map/all_to_all | solution.py:526
  74.1 3.8 %collective-permute-start.5 = (bf16[1024,128]{1,0:T(8,128)(2,1)S(1)}, bf16[1024,128]{1,0:T(8,128)(2,1)S(1)}, u32[]{:S(2)}, u32[]{:S(2)}) collective-permute-start(bf16[1024,128]{1,0:T(8,128)(2,1)S(1)} %bitcast.35), channel_id=1, source_target_pairs={{0,1},{1,0},{2,3},{3,2},{4,5},{5,4},{6,7},{7,6},{8,9},{9,8},{10,11... | collective-permute-start | bytes 786440 | tf_op jit(solution)/shard_map/ppermute | solution.py:529
  79.0 4.7 %collective-permute-start.7 = (bf16[1024,128]{1,0:T(8,128)(2,1)S(1)}, bf16[1024,128]{1,0:T(8,128)(2,1)}, u32[]{:S(2)}, u32[]{:S(2)}) collective-permute-start(bf16[1024,128]{1,0:T(8,128)(2,1)S(1)} %collective-permute-done.6.b2), channel_id=1, source_target_pairs={{0,1},{1,0},{2,3},{3,2},{4,5},{5,4},{6,7},{7,6},{8,9},{9,8},{10,11... | collective-permute-start | bytes 786440 | tf_op jit(solution)/shard_map/ppermute | solution.py:530
  84.9 6.4 %shard_map.106 = (f32[4,24,2048]{2,1,0:T(8,128)S(1)}, bf16[88,2048]{1,0:T(8,128)(2,1)S(1)}, bf16[88,2048]{1,0:T(8,128)(2,1)S(1)}, bf16[88,2048]{1,0:T(8,128)(2,1)S(1)}, f32[8,128]{1,0:T(8,128)S(1)}) custom-call(bf16[1024,128]{1,0:T(8,128)(2,1)S(1)} %bitcast.36, bf16[1024,128]{1,0:T(8,128)(2,1)S(1)} %collective-permute-done.5.b1, ...), custom_call_target="tpu_custom_call" | custom-call | flops 2147483648 | bytes 5031936 | tf_op jit(solution)/shard_map/pallas_call | solution.py:452
  92.1 2.2 %collective-permute-start.9 = (bf16[88,2048]{1,0:T(8,128)(2,1)S(1)}, bf16[88,2048]{1,0:T(8,128)(2,1)S(1)}, u32[]{:S(2)}, u32[]{:S(2)}) collective-permute-start(bf16[88,2048]{1,0:T(8,128)(2,1)S(1)} %get-tuple-element.42), channel_id=1, source_target_pairs={{0,4},{4,8},{8,12},{16,20},{20,24},{24,28},{32,36},{36,40},{40,44}... | collective-permute-start | bytes 1081352 | tf_op jit(solution)/shard_map/ppermute | solution.py:560
  94.3 1.3 collective-permute-start.10
  95.6 6.1 %collective-permute-done.9.below = bf16[88,2048]{1,0:T(8,128)(2,1)S(1)} collective-permute-done((bf16[88,2048]{1,0:T(8,128)(2,1)S(1)}, bf16[88,2048]{1,0:T(8,128)(2,1)S(1)}, u32[]{:S(2)}, u32[]{:S(2)}) %collective-permute-start.9) | collective-permute-done | bytes 360480 | tf_op jit(solution)/shard_map/ppermute | solution.py:560
  101.7 3.8 %collective-permute-done.10.above = bf16[88,2048]{1,0:T(8,128)(2,1)S(1)} collective-permute-done((bf16[88,2048]{1,0:T(8,128)(2,1)S(1)}, bf16[88,2048]{1,0:T(8,128)(2,1)S(1)}, u32[]{:S(2)}, u32[]{:S(2)}) %collective-permute-start.10) | collective-permute-done | bytes 360480 | tf_op jit(solution)/shard_map/ppermute | solution.py:561
  106.7 23.6 %all_to_all.44 = f32[256,1,128]{2,1,0:T(1,128)S(1)} all-to-all(f32[256,1,128]{2,1,0:T(1,128)S(1)} %bitcast.40), channel_id=1, replica_groups=mesh['gz'=64,'gy'=4] {'gz','gy'}, dimensions={0} | all-to-all | bytes 262144 | tf_op jit(solution)/shard_map/all_to_all | solution.py:564
  130.3 2.3 %shard_map.108 = (f32[8,24,2048]{2,1,0:T(8,128)S(1)}, f32[4,24,2048]{2,1,0:T(8,128)S(1)}, f32[256,128]{1,0:T(8,128)S(1)}) custom-call(f32[256,128]{1,0:T(8,128)S(1)} %bitcast.30, f32[8,128]{1,0:T(8,128)S(1)} %get-tuple-element.44.moved, f32[4,24,2048]{2,1,0:T(8,128)S(1)} %get-tuple-element.41.f, bf16[88,2048]{1,0:T(8,128)(2,1)S(1)} %collective-permute-done.9.below, ...), custom_call_target="tpu_custom_call" | custom-call | flops 23592960 | bytes 5279744 | tf_op jit(solution)/shard_map/pallas_call | solution.py:452
  132.6 18.4 %all_to_all.45 = f32[256,1,128]{2,1,0:T(1,128)S(1)} all-to-all(f32[256,1,128]{2,1,0:T(1,128)S(1)} %bitcast.38), channel_id=1, replica_groups=mesh['gz'=64,'gy'=4] {'gz','gy'}, dimensions={0} | all-to-all | bytes 262144 | tf_op jit(solution)/shard_map/all_to_all | solution.py:564
  151.0 1.7 %shard_map.109 = (f32[6,24,2048]{2,1,0:T(8,128)S(1)}, f32[4,24,2048]{2,1,0:T(8,128)S(1)}, f32[256,128]{1,0:T(8,128)S(1)}) custom-call(f32[256,128]{1,0:T(8,128)S(1)} %bitcast.31, f32[8,128]{1,0:T(8,128)S(1)} %get-tuple-element.44.moved, f32[8,24,2048]{2,1,0:T(8,128)S(1)} %get-tuple-element.48.f, f32[4,24,2048]{2,1,0:T(8,128)S(1)} %get-tuple-element.49.g), custom_call_target="tpu_custom_call" | custom-call | flops 19660800 | bytes 4591616 | tf_op jit(solution)/shard_map/pallas_call | solution.py:452
  152.7 18.4 %all_to_all.46 = f32[256,1,128]{2,1,0:T(1,128)S(1)} all-to-all(f32[256,1,128]{2,1,0:T(1,128)S(1)} %bitcast.39), channel_id=1, replica_groups=mesh['gz'=64,'gy'=4] {'gz','gy'}, dimensions={0} | all-to-all | bytes 262144 | tf_op jit(solution)/shard_map/all_to_all | solution.py:564
  (43 shorter events, 12.1 us)
Async XLA Ops:
  0.6 4.2 %copy-start = (f32[4,16,2048]{2,1,0:T(8,128)S(1)}, f32[4,16,2048]{2,1,0:T(8,128)}, u32[]{:S(2)}) copy-start(f32[4,16,2048]{2,1,0:T(8,128)} %volume.1) | copy-start | bytes 1572868
  0.6 4.2 %copy-start.8 = (f32[64,16]{0,1:T(8,128)S(1)}, f32[64,16]{0,1:T(8,128)}, u32[]{:S(2)}) copy-start(f32[64,16]{0,1:T(8,128)} %param.13) | copy-start | bytes 12292
  0.7 5.5 %copy-start.10 = (s32[64,16]{0,1:T(8,128)S(1)}, s32[64,16]{0,1:T(8,128)}, u32[]{:S(2)}) copy-start(s32[64,16]{0,1:T(8,128)} %param.16) | copy-start | bytes 12292
  0.7 5.5 %copy-start.9 = (s32[64,16]{0,1:T(8,128)S(1)}, s32[64,16]{0,1:T(8,128)}, u32[]{:S(2)}) copy-start(s32[64,16]{0,1:T(8,128)} %param.15) | copy-start | bytes 12292
  0.7 14.8 %copy-start.3 = (bf16[16,128,128]{2,1,0:T(8,128)(2,1)S(1)}, bf16[16,128,128]{2,1,0:T(8,128)(2,1)}, u32[]{:S(2)}) copy-start(bf16[16,128,128]{2,1,0:T(8,128)(2,1)} %tiles.1) | copy-start | bytes 1572868
  2.6 9.1 %collective-permute-start = (f32[64,1408]{1,0:T(8,128)S(1)}, f32[64,1408]{1,0:T(8,128)S(1)}, u32[]{:S(2)}, u32[]{:S(2)}) collective-permute-start(f32[64,1408]{1,0:T(8,128)S(1)} %select_maximum_fusion), channel_id=1, source_target_pairs={{0,2},{1,3},{2,0},{3,1},{4,6},{5,7},{6,4},{7,5},{8,10},{9,11},{10,... | collective-permute-start | bytes 1081352 | tf_op jit(solution)/shard_map/ppermute | solution.py:483
  4.9 2.5 %collective-permute-start.1 = (f32[64,1152]{1,0:T(8,128)S(1)}, f32[64,1152]{1,0:T(8,128)S(1)}, u32[]{:S(2)}, u32[]{:S(2)}) collective-permute-start(f32[64,1152]{1,0:T(8,128)S(1)} %select_maximum_fusion.1), channel_id=1, source_target_pairs={{0,1},{1,0},{2,3},{3,2},{4,5},{5,4},{6,7},{7,6},{8,9},{9,8},{10,11... | collective-permute-start | bytes 884744 | tf_op jit(solution)/shard_map/ppermute | solution.py:487
  6.2 29.6 %copy-start.4 = (f32[4,16,2048]{2,1,0:T(8,128)S(1)}, f32[4,16,2048]{2,1,0:T(8,128)}, u32[]{:S(2)}) copy-start(f32[4,16,2048]{2,1,0:T(8,128)} %norm.1) | copy-start | bytes 1572868
  11.7 3.8 %collective-permute-start.2 = (f32[64,1408]{1,0:T(8,128)S(1)}, f32[64,1408]{1,0:T(8,128)S(1)}, u32[]{:S(2)}, u32[]{:S(2)}) collective-permute-start(f32[64,1408]{1,0:T(8,128)S(1)} %collective-permute-done.far), channel_id=1, source_target_pairs={{0,1},{1,0},{2,3},{3,2},{4,5},{5,4},{6,7},{7,6},{8,9},{9,8},{10,11... | collective-permute-start | bytes 1081352 | tf_op jit(solution)/shard_map/ppermute | solution.py:489
  21.1 32.3 %copy-start.1 = (f32[1,256,512]{2,1,0:T(8,128)S(1)}, f32[1,256,512]{2,1,0:T(8,128)}, u32[]{:S(2)}) copy-start(f32[1,256,512]{2,1,0:T(8,128)} %param.10) | copy-start | bytes 1572868
  21.1 32.3 %copy-start.2 = (f32[1,256,512]{2,1,0:T(8,128)S(1)}, f32[1,256,512]{2,1,0:T(8,128)}, u32[]{:S(2)}) copy-start(f32[1,256,512]{2,1,0:T(8,128)} %param.11) | copy-start | bytes 1572868
  21.1 32.3 %copy-start.5 = (s32[64,64]{1,0:T(8,128)S(1)}, s32[64,64]{1,0:T(8,128)}, u32[]{:S(2)}) copy-start(s32[64,64]{1,0:T(8,128)} %starts.1) | copy-start | bytes 49156
  21.2 32.3 %all-to-all-start = ((f32[64,16,128]{2,1,0:T(8,128)}), f32[64,16,128]{2,1,0:T(8,128)S(1)}, u32[]{:S(2)}, u32[]{:S(2)}) async-start(f32[64,16,128]{2,1,0:T(8,128)} %bitcast.3), calls=%async_computation | async-start | bytes 1048576 | tf_op jit(solution)/shard_map/all_to_all | solution.py:516
  35.9 9.8 %collective-permute-start.3 = (f32[4,8,2048]{2,1,0:T(8,128)S(1)}, f32[4,8,2048]{2,1,0:T(8,128)S(1)}, u32[]{:S(2)}, u32[]{:S(2)}) collective-permute-start(f32[4,8,2048]{2,1,0:T(8,128)S(1)} %pad_maximum_fusion), channel_id=1, source_target_pairs={{1,0},{2,1},{3,2},{5,4},{6,5},{7,6},{9,8},{10,9},{11,10},{13,12},{... | collective-permute-start | bytes 786440 | tf_op jit(solution)/shard_map/ppermute | solution.py:493
  38.6 8.4 %collective-permute-start.4 = (f32[4,8,2048]{2,1,0:T(8,128)S(1)}, f32[4,8,2048]{2,1,0:T(8,128)S(1)}, u32[]{:S(2)}, u32[]{:S(2)}) collective-permute-start(f32[4,8,2048]{2,1,0:T(8,128)S(1)} %pad_maximum_fusion.1), channel_id=1, source_target_pairs={{0,1},{1,2},{2,3},{4,5},{5,6},{6,7},{8,9},{9,10},{10,11},{12,13},{... | collective-permute-start | bytes 786440 | tf_op jit(solution)/shard_map/ppermute | solution.py:494
  47.0 0.7 copy-start.6
  54.8 30.1 %copy-start.7 = (f32[4,8,2048]{2,1,0:T(8,128)S(1)}, f32[4,8,2048]{2,1,0:T(8,128)}, u32[]{:S(2)}) copy-start(f32[4,8,2048]{2,1,0:T(8,128)} %copy-done.6) | copy-start | bytes 786436
  73.7 5.2 %collective-permute-start.6 = (bf16[1024,128]{1,0:T(8,128)(2,1)S(1)}, bf16[1024,128]{1,0:T(8,128)(2,1)S(1)}, u32[]{:S(2)}, u32[]{:S(2)}) collective-permute-start(bf16[1024,128]{1,0:T(8,128)(2,1)S(1)} %bitcast.34), channel_id=1, source_target_pairs={{0,2},{1,3},{2,0},{3,1},{4,6},{5,7},{6,4},{7,5},{8,10},{9,11},{10,... | collective-permute-start | bytes 786440 | tf_op jit(solution)/shard_map/ppermute | solution.py:528
  74.1 9.8 %collective-permute-start.5 = (bf16[1024,128]{1,0:T(8,128)(2,1)S(1)}, bf16[1024,128]{1,0:T(8,128)(2,1)S(1)}, u32[]{:S(2)}, u32[]{:S(2)}) collective-permute-start(bf16[1024,128]{1,0:T(8,128)(2,1)S(1)} %bitcast.35), channel_id=1, source_target_pairs={{0,1},{1,0},{2,3},{3,2},{4,5},{5,4},{6,7},{7,6},{8,9},{9,8},{10,11... | collective-permute-start | bytes 786440 | tf_op jit(solution)/shard_map/ppermute | solution.py:529
  79.0 6.0 %collective-permute-start.7 = (bf16[1024,128]{1,0:T(8,128)(2,1)S(1)}, bf16[1024,128]{1,0:T(8,128)(2,1)}, u32[]{:S(2)}, u32[]{:S(2)}) collective-permute-start(bf16[1024,128]{1,0:T(8,128)(2,1)S(1)} %collective-permute-done.6.b2), channel_id=1, source_target_pairs={{0,1},{1,0},{2,3},{3,2},{4,5},{5,4},{6,7},{7,6},{8,9},{9,8},{10,11... | collective-permute-start | bytes 786440 | tf_op jit(solution)/shard_map/ppermute | solution.py:530
  91.4 4.2 %collective-permute-start.8 = (bf16[88,2048]{1,0:T(8,128)(2,1)S(1)}, bf16[88,2048]{1,0:T(8,128)(2,1)S(1)}, u32[]{:S(2)}, u32[]{:S(2)}) collective-permute-start(bf16[88,2048]{1,0:T(8,128)(2,1)S(1)} %get-tuple-element.40), channel_id=1, source_target_pairs={{12,16},{28,32},{44,48},{60,64},{76,80},{92,96},{108,112},{124,128... | collective-permute-start | bytes 1081352 | tf_op jit(solution)/shard_map/ppermute | solution.py:559
  92.1 9.6 %collective-permute-start.9 = (bf16[88,2048]{1,0:T(8,128)(2,1)S(1)}, bf16[88,2048]{1,0:T(8,128)(2,1)S(1)}, u32[]{:S(2)}, u32[]{:S(2)}) collective-permute-start(bf16[88,2048]{1,0:T(8,128)(2,1)S(1)} %get-tuple-element.42), channel_id=1, source_target_pairs={{0,4},{4,8},{8,12},{16,20},{20,24},{24,28},{32,36},{36,40},{40,44}... | collective-permute-start | bytes 1081352 | tf_op jit(solution)/shard_map/ppermute | solution.py:560
  94.3 11.2 %collective-permute-start.10 = (bf16[88,2048]{1,0:T(8,128)(2,1)S(1)}, bf16[88,2048]{1,0:T(8,128)(2,1)S(1)}, u32[]{:S(2)}, u32[]{:S(2)}) collective-permute-start(bf16[88,2048]{1,0:T(8,128)(2,1)S(1)} %get-tuple-element.43), channel_id=1, source_target_pairs={{4,0},{8,4},{12,8},{20,16},{24,20},{28,24},{36,32},{40,36},{44,40}... | collective-permute-start | bytes 1081352 | tf_op jit(solution)/shard_map/ppermute | solution.py:561

commit v6 on v5

--- a/solution.py
+++ b/solution.py
@@ -89,7 +89,7 @@
 
 
 def project_kernel(
-    far, farnear, near, small, own, tiles, out, weights_out,
+    far, farnear, near, w_far, w_farnear, w_near, small, own, tiles, out, weights_out,
     own_here, sums, lhs, rhs, wide, acc, arrived,
 ):
     block = lax.axis_index("gy")
@@ -107,7 +107,7 @@
     )
     acc[...] = jnp.zeros_like(acc)
     sources = ((far, 2, inner), (farnear, 3, inner), (near, 1, slice(0, span)), (own_here, 0, slice(0, span)))
-    weight = [ref[:ROWS, ref.shape[1] - TILE :][:, :ANGLES] for ref in (far, farnear, near)]
+    weight = [ref[...] for ref in (w_far, w_farnear, w_near)]
     weight = pieces(jnp.concatenate([*weight, small[XT:]], axis=0).T, 3)
     row = iota((EXT, 1), 0)
     wanted = block * ROWS + row - jnp.where(row >= ROWS + HALO // 2, EXT, 0)
@@ -473,19 +473,20 @@
     kinds, bands = jnp.swapaxes(tile_kind, 0, 1), jnp.swapaxes(tile_band, 0, 1)
     small = jnp.concatenate([(kinds + NK * bands).astype(F32), weight], axis=0)
 
-    def outgoing(columns, weight_sent):
-        lanes = jnp.pad(weight_sent, ((0, PLANES * ROWS - ROWS), (0, TILE - ANGLES)))
-        return jnp.concatenate([columns, lanes], axis=1)
-
-    reach = REACH * TILE
-    to_chip = outgoing(jnp.where(block >= 2, flat[:, :reach], flat[:, WIDTH - reach :]), weight)
+    away = jnp.where(block >= 2, 0, (XT - REACH) * TILE)
+    to_chip = lax.dynamic_slice_in_dim(flat, away, REACH * TILE, axis=1)
     to_chip, flat_later, weight_later = lax.optimization_barrier((to_chip, flat, weight))
     far = lax.ppermute(to_chip, "gy", other_chip)
     beside = block ^ 1
     window = beside * 2 + jnp.where(beside >= 2, 2, 0)
     columns = lax.dynamic_slice_in_dim(flat_later, window * TILE, WINDOW * TILE, axis=1)
-    near = lax.ppermute(outgoing(columns, weight_later), "gy", other_core)
-    far, near, small = lax.optimization_barrier((far, near, small))
+    near = lax.ppermute(columns, "gy", other_core)
+    w_near, w_far, w_farnear = (
+        lax.ppermute(weight_later, "gy", [(i, i ^ flip) for i in range(blocks)]) for flip in (1, 2, 3)
+    )
+    far, near, small, w_near, w_far, w_farnear = lax.optimization_barrier(
+        (far, near, small, w_near, w_far, w_farnear)
+    )
     farnear = lax.ppermute(far, "gy", other_core)
     half = HALO // 2
     to_before = jnp.concatenate([volume[:, :half], col_norm[:, :half]], axis=1)
@@ -498,7 +499,7 @@
     slab_proj, weights = call(
         project_kernel,
         [((chunk, TILE), F32), ((EXT, ANGLES), F32)],
-        (far, farnear, near, small, flat, tiles),
+        (far, farnear, near, w_far, w_farnear, w_near, small, flat, tiles),
         [
             pltpu.VMEM((PLANES * ROWS, WINDOW * TILE), F32),
             pltpu.VMEM((rows, WINDOW * TILE), F32),

time: 173 us -> 177 us (1.023)
  local copies, waits for them, and re-layouts: 1.18 us -> 5.26 us
  waiting for transfers between devices: 29.9 us -> 31.9 us
    ppermute x1 -> x4, starting transfers between devices: 1.25 us -> 5.27 us  [the longest x3 4.68 us: per_device(): lax.ppermute(weight_later, 'gy', [(i, i ^ flip) for i in range(blocks)])]
    ppermute x1, waiting for transfers between devices: 4.37 us -> 7.74 us  [per_device(): far = lax.ppermute(to_chip, 'gy', other_chip)]
    ppermute x1, starting transfers between devices: 2.21 us -> 0.09 us  [per_device(): far = lax.ppermute(to_chip, 'gy', other_chip)]
    unnamed x23 -> x21, local copies, waits for them, and re-layouts: 1.05 us -> 3.1 us
    all_to_all x1, starting transfers between devices: 14.6 us -> 12.7 us  [per_device(): lax.all_to_all(chunks, 'gz', split_axis=0, concat_axis=0, tiled=True)]
  transfers between devices with their start and end apart: 12 -> 15, of which waited for: 10 -> 9; matrix products, arithmetic and copies ran while one was open for 0% -> 2% of each run, Pallas kernels for 0% -> 0%
where the time goes in v6:
time: 177 us; the launch traced here: 176 us
  blocking collectives  79.4 us (45%)
  starting transfers between devices  37.8 us (21%)
  waiting for transfers between devices  31.9 us (18%)
  Pallas kernels  19.5 us (11%)
  local copies, waits for them, and re-layouts  5.26 us (3%)
    all_to_all x3, blocking collectives, exchanged(): lax.all_to_all(parts, ('gz', 'gy'), split_axis=0, concat_axis=0, tiled=True)  60.4 us
    pallas_call x7, Pallas kernels, call(): pl.pallas_call(kernel, out_shape=shapes, in_specs=[VMEM] * (len(args) - f...  19.5 us
    all_to_all x1, blocking collectives, per_device(): held = lax.all_to_all(chunks, 'gz', split_axis=0, concat_axis=0, tiled=True)  18.9 us
    all_to_all x1, starting transfers between devices, per_device(): lax.all_to_all(chunks, 'gz', split_axis=0, concat_axis=0, tiled=True)  12.7 us
    ppermute x1, waiting for transfers between devices, per_device(): far = lax.ppermute(to_chip, 'gy', other_chip)  7.74 us
    ppermute x1, waiting for transfers between devices, per_device(): below = lax.ppermute(last, 'gz', within)  6.08 us
    all_to_all x1, waiting for transfers between devices, per_device(): lax.all_to_all(chunks, 'gz', split_axis=0, concat_axis=0, tiled=True)  5.46 us
    ppermute x1, starting transfers between devices, per_device(): held_farnear = lax.ppermute(held_far, 'gy', other_core)  4.69 us
  transfers between devices with their start and end apart: 15, of which 9 were waited for; matrix products, arithmetic and copies ran while one was open for 2% of the time, Pallas kernels for 0%

profile of v6, /device:TPU:1, one launch (start us, length us, event | category | flops | bytes accessed | tf_op | source)
XLA Modules:
  0.0 176.2 jit_solution(14669789324648256552)
XLA Ops:
  1.6 2.8 %collective-permute-start.4 = (f32[16,64]{1,0:T(8,128)}, f32[16,64]{1,0:T(8,128)S(1)}, u32[]{:S(2)}, u32[]{:S(2)}) collective-permute-start(f32[16,64]{1,0:T(8,128)} %bitcast.41), channel_id=1, source_target_pairs={{0,3},{1,2},{2,1},{3,0},{4,7},{5,6},{6,5},{7,4},{8,11},{9,10},{10,... | collective-permute-start | bytes 12296 | tf_op jit(solution)/shard_map/ppermute | solution.py:485
  4.4 1.9 %collective-permute-start.3 = (f32[16,64]{1,0:T(8,128)}, f32[16,64]{1,0:T(8,128)S(1)}, u32[]{:S(2)}, u32[]{:S(2)}) collective-permute-start(f32[16,64]{1,0:T(8,128)} %bitcast.42), channel_id=1, source_target_pairs={{0,2},{1,3},{2,0},{3,1},{4,6},{5,7},{6,4},{7,5},{8,10},{9,11},{10,... | collective-permute-start | bytes 12296 | tf_op jit(solution)/shard_map/ppermute | solution.py:485
  9.5 7.7 %collective-permute-done.far = f32[64,1280]{1,0:T(8,128)S(1)} collective-permute-done((f32[64,1280]{1,0:T(8,128)S(1)}, f32[64,1280]{1,0:T(8,128)S(1)}, u32[]{:S(2)}, u32[]{:S(2)}) %collective-permute-start) | collective-permute-done | bytes 327712 | tf_op jit(solution)/shard_map/ppermute | solution.py:479
  21.4 5.6 %shard_map.104 = (f32[1024,128]{1,0:T(8,128)}, f32[24,64]{1,0:T(8,128)S(1)}) custom-call(f32[64,1280]{1,0:T(8,128)S(1)} %collective-permute-done.far, f32[64,1280]{1,0:T(8,128)S(1)} %collective-permute-done.5.farnear, f32[64,1024]{1,0:T(8,128)S(1)} %collective-permute-done.1.near, f32[16,64]{1,0:T(8,128)S(1)} %collective-permute-done.3.w_far, ...), custom_call_target="tpu_custom_call" | custom-call | flops 2147483648 | bytes 2516992 | tf_op jit(solution)/shard_map/pallas_call | solution.py:452
  27.1 12.7 %all-to-all-start = ((f32[64,16,128]{2,1,0:T(8,128)}), f32[64,16,128]{2,1,0:T(8,128)S(1)}, u32[]{:S(2)}, u32[]{:S(2)}) async-start(f32[64,16,128]{2,1,0:T(8,128)} %bitcast.3), calls=%async_computation | async-start | bytes 1048576 | tf_op jit(solution)/shard_map/all_to_all | solution.py:517
  40.0 2.7 %collective-permute-start.6 = (f32[4,8,2048]{2,1,0:T(8,128)S(1)}, f32[4,8,2048]{2,1,0:T(8,128)S(1)}, u32[]{:S(2)}, u32[]{:S(2)}) collective-permute-start(f32[4,8,2048]{2,1,0:T(8,128)S(1)} %pad_maximum_fusion), channel_id=1, source_target_pairs={{1,0},{2,1},{3,2},{5,4},{6,5},{7,6},{9,8},{10,9},{11,10},{13,12},{... | collective-permute-start | bytes 786440 | tf_op jit(solution)/shard_map/ppermute | solution.py:494
  42.8 3.0 %collective-permute-start.7 = (f32[4,8,2048]{2,1,0:T(8,128)S(1)}, f32[4,8,2048]{2,1,0:T(8,128)S(1)}, u32[]{:S(2)}, u32[]{:S(2)}) collective-permute-start(f32[4,8,2048]{2,1,0:T(8,128)S(1)} %pad_maximum_fusion.1), channel_id=1, source_target_pairs={{0,1},{1,2},{2,3},{4,5},{5,6},{6,7},{8,9},{9,10},{10,11},{12,13},{... | collective-permute-start | bytes 786440 | tf_op jit(solution)/shard_map/ppermute | solution.py:495
  45.8 4.0 %collective-permute-done.6.after = f32[4,8,2048]{2,1,0:T(8,128)S(1)} collective-permute-done((f32[4,8,2048]{2,1,0:T(8,128)S(1)}, f32[4,8,2048]{2,1,0:T(8,128)S(1)}, u32[]{:S(2)}, u32[]{:S(2)}) %collective-permute-start.6) | collective-permute-done | bytes 262176 | tf_op jit(solution)/shard_map/ppermute | solution.py:494
  49.9 1.5 collective-permute-done.7.before
  52.1 5.5 %all-to-all-done = f32[64,16,128]{2,1,0:T(8,128)S(1)} async-done(((f32[64,16,128]{2,1,0:T(8,128)}), f32[64,16,128]{2,1,0:T(8,128)S(1)}, u32[]{:S(2)}, u32[]{:S(2)}) %all-to-all-start) | async-done | bytes 524320 | tf_op jit(solution)/shard_map/all_to_all | solution.py:517
  57.6 1.3 shard_map.105
  58.9 18.9 %all_to_all.43 = bf16[64,16,128]{2,1,0:T(8,128)(2,1)S(1)} all-to-all(bf16[64,16,128]{2,1,0:T(8,128)(2,1)S(1)} %bitcast.37), channel_id=1, replica_groups=mesh['gz'=64,'gy'=4] {'gz'}, dimensions={0} | all-to-all | bytes 524288 | tf_op jit(solution)/shard_map/all_to_all | solution.py:527
  78.2 3.8 %collective-permute-start.8 = (bf16[1024,128]{1,0:T(8,128)(2,1)S(1)}, bf16[1024,128]{1,0:T(8,128)(2,1)S(1)}, u32[]{:S(2)}, u32[]{:S(2)}) collective-permute-start(bf16[1024,128]{1,0:T(8,128)(2,1)S(1)} %bitcast.35), channel_id=1, source_target_pairs={{0,1},{1,0},{2,3},{3,2},{4,5},{5,4},{6,7},{7,6},{8,9},{9,8},{10,11... | collective-permute-start | bytes 786440 | tf_op jit(solution)/shard_map/ppermute | solution.py:530
  83.0 4.7 %collective-permute-start.10 = (bf16[1024,128]{1,0:T(8,128)(2,1)S(1)}, bf16[1024,128]{1,0:T(8,128)(2,1)}, u32[]{:S(2)}, u32[]{:S(2)}) collective-permute-start(bf16[1024,128]{1,0:T(8,128)(2,1)S(1)} %collective-permute-done.9.b2), channel_id=1, source_target_pairs={{0,1},{1,0},{2,3},{3,2},{4,5},{5,4},{6,7},{7,6},{8,9},{9,8},{10,11... | collective-permute-start | bytes 786440 | tf_op jit(solution)/shard_map/ppermute | solution.py:531
  89.0 6.4 %shard_map.106 = (f32[4,24,2048]{2,1,0:T(8,128)S(1)}, bf16[88,2048]{1,0:T(8,128)(2,1)S(1)}, bf16[88,2048]{1,0:T(8,128)(2,1)S(1)}, bf16[88,2048]{1,0:T(8,128)(2,1)S(1)}, f32[8,128]{1,0:T(8,128)S(1)}) custom-call(bf16[1024,128]{1,0:T(8,128)(2,1)S(1)} %bitcast.36, bf16[1024,128]{1,0:T(8,128)(2,1)S(1)} %collective-permute-done.8.b1, ...), custom_call_target="tpu_custom_call" | custom-call | flops 2147483648 | bytes 5031936 | tf_op jit(solution)/shard_map/pallas_call | solution.py:452
  96.2 2.2 %collective-permute-start.12 = (bf16[88,2048]{1,0:T(8,128)(2,1)S(1)}, bf16[88,2048]{1,0:T(8,128)(2,1)S(1)}, u32[]{:S(2)}, u32[]{:S(2)}) collective-permute-start(bf16[88,2048]{1,0:T(8,128)(2,1)S(1)} %get-tuple-element.48), channel_id=1, source_target_pairs={{0,4},{4,8},{8,12},{16,20},{20,24},{24,28},{32,36},{36,40},{40,44}... | collective-permute-start | bytes 1081352 | tf_op jit(solution)/shard_map/ppermute | solution.py:561
  98.4 1.3 collective-permute-start.13
  99.7 6.1 %collective-permute-done.12.below = bf16[88,2048]{1,0:T(8,128)(2,1)S(1)} collective-permute-done((bf16[88,2048]{1,0:T(8,128)(2,1)S(1)}, bf16[88,2048]{1,0:T(8,128)(2,1)S(1)}, u32[]{:S(2)}, u32[]{:S(2)}) %collective-permute-start.12) | collective-permute-done | bytes 360480 | tf_op jit(solution)/shard_map/ppermute | solution.py:561
  105.8 3.8 %collective-permute-done.13.above = bf16[88,2048]{1,0:T(8,128)(2,1)S(1)} collective-permute-done((bf16[88,2048]{1,0:T(8,128)(2,1)S(1)}, bf16[88,2048]{1,0:T(8,128)(2,1)S(1)}, u32[]{:S(2)}, u32[]{:S(2)}) %collective-permute-start.13) | collective-permute-done | bytes 360480 | tf_op jit(solution)/shard_map/ppermute | solution.py:562
  110.7 23.6 %all_to_all.44 = f32[256,1,128]{2,1,0:T(1,128)S(1)} all-to-all(f32[256,1,128]{2,1,0:T(1,128)S(1)} %bitcast.40), channel_id=1, replica_groups=mesh['gz'=64,'gy'=4] {'gz','gy'}, dimensions={0} | all-to-all | bytes 262144 | tf_op jit(solution)/shard_map/all_to_all | solution.py:565
  134.3 2.3 %shard_map.108 = (f32[8,24,2048]{2,1,0:T(8,128)S(1)}, f32[4,24,2048]{2,1,0:T(8,128)S(1)}, f32[256,128]{1,0:T(8,128)S(1)}) custom-call(f32[256,128]{1,0:T(8,128)S(1)} %bitcast.30, f32[8,128]{1,0:T(8,128)S(1)} %get-tuple-element.50.moved, f32[4,24,2048]{2,1,0:T(8,128)S(1)} %get-tuple-element.47.f, bf16[88,2048]{1,0:T(8,128)(2,1)S(1)} %collective-permute-done.12.below, ...), custom_call_target="tpu_custom_call" | custom-call | flops 23592960 | bytes 5279744 | tf_op jit(solution)/shard_map/pallas_call | solution.py:452
  136.7 18.4 %all_to_all.45 = f32[256,1,128]{2,1,0:T(1,128)S(1)} all-to-all(f32[256,1,128]{2,1,0:T(1,128)S(1)} %bitcast.38), channel_id=1, replica_groups=mesh['gz'=64,'gy'=4] {'gz','gy'}, dimensions={0} | all-to-all | bytes 262144 | tf_op jit(solution)/shard_map/all_to_all | solution.py:565
  155.1 1.7 shard_map.109
  156.8 18.4 %all_to_all.46 = f32[256,1,128]{2,1,0:T(1,128)S(1)} all-to-all(f32[256,1,128]{2,1,0:T(1,128)S(1)} %bitcast.39), channel_id=1, replica_groups=mesh['gz'=64,'gy'=4] {'gz','gy'}, dimensions={0} | all-to-all | bytes 262144 | tf_op jit(solution)/shard_map/all_to_all | solution.py:565
  (45 shorter events, 14.8 us)
Async XLA Ops:
  1.6 7.8 %collective-permute-start.4 = (f32[16,64]{1,0:T(8,128)}, f32[16,64]{1,0:T(8,128)S(1)}, u32[]{:S(2)}, u32[]{:S(2)}) collective-permute-start(f32[16,64]{1,0:T(8,128)} %bitcast.41), channel_id=1, source_target_pairs={{0,3},{1,2},{2,1},{3,0},{4,7},{5,6},{6,5},{7,4},{8,11},{9,10},{10,... | collective-permute-start | bytes 12296 | tf_op jit(solution)/shard_map/ppermute | solution.py:485
  4.4 5.1 %collective-permute-start.3 = (f32[16,64]{1,0:T(8,128)}, f32[16,64]{1,0:T(8,128)S(1)}, u32[]{:S(2)}, u32[]{:S(2)}) collective-permute-start(f32[16,64]{1,0:T(8,128)} %bitcast.42), channel_id=1, source_target_pairs={{0,2},{1,3},{2,0},{3,1},{4,6},{5,7},{6,4},{7,5},{8,10},{9,11},{10,... | collective-permute-start | bytes 12296 | tf_op jit(solution)/shard_map/ppermute | solution.py:485
  6.3 3.2 %collective-permute-start.2 = (f32[16,64]{1,0:T(8,128)}, f32[16,64]{1,0:T(8,128)S(1)}, u32[]{:S(2)}, u32[]{:S(2)}) collective-permute-start(f32[16,64]{1,0:T(8,128)} %bitcast.43), channel_id=1, source_target_pairs={{0,1},{1,0},{2,3},{3,2},{4,5},{5,4},{6,7},{7,6},{8,9},{9,8},{10,11... | collective-permute-start | bytes 12296 | tf_op jit(solution)/shard_map/ppermute | solution.py:485
  6.3 33.5 %copy-start.1 = (f32[4,16,2048]{2,1,0:T(8,128)S(1)}, f32[4,16,2048]{2,1,0:T(8,128)}, u32[]{:S(2)}) copy-start(f32[4,16,2048]{2,1,0:T(8,128)} %volume.1) | copy-start | bytes 1572868
  7.4 2.1 %collective-permute-start.1 = (f32[64,1024]{1,0:T(8,128)S(1)}, f32[64,1024]{1,0:T(8,128)S(1)}, u32[]{:S(2)}, u32[]{:S(2)}) collective-permute-start(f32[64,1024]{1,0:T(8,128)S(1)} %constant_dynamic-slice_fusion), channel_id=1, source_target_pairs={{0,1},{1,0},{2,3},{3,2},{4,5},{5,4},{6,7},{7,6},{8,9},{9,8},{10,11... | collective-permute-start | bytes 786440 | tf_op jit(solution)/shard_map/ppermute | solution.py:483
  8.0 9.3 %collective-permute-start = (f32[64,1280]{1,0:T(8,128)S(1)}, f32[64,1280]{1,0:T(8,128)S(1)}, u32[]{:S(2)}, u32[]{:S(2)}) collective-permute-start(f32[64,1280]{1,0:T(8,128)S(1)} %constant_dynamic-slice_fusion.1), channel_id=1, source_target_pairs={{0,2},{1,3},{2,0},{3,1},{4,6},{5,7},{6,4},{7,5},{8,10},{9,11},{10,... | collective-permute-start | bytes 983048 | tf_op jit(solution)/shard_map/ppermute | solution.py:479
  17.2 2.1 %collective-permute-start.5 = (f32[64,1280]{1,0:T(8,128)S(1)}, f32[64,1280]{1,0:T(8,128)S(1)}, u32[]{:S(2)}, u32[]{:S(2)}) collective-permute-start(f32[64,1280]{1,0:T(8,128)S(1)} %collective-permute-done.far), channel_id=1, source_target_pairs={{0,1},{1,0},{2,3},{3,2},{4,5},{5,4},{6,7},{7,6},{8,9},{9,8},{10,11... | collective-permute-start | bytes 983048 | tf_op jit(solution)/shard_map/ppermute | solution.py:490
  19.4 1.0 copy-start
  20.4 1.0 copy-start.4
  21.4 18.4 %copy-start.6 = (f32[4,16,2048]{2,1,0:T(8,128)S(1)}, f32[4,16,2048]{2,1,0:T(8,128)}, u32[]{:S(2)}) copy-start(f32[4,16,2048]{2,1,0:T(8,128)} %norm.1) | copy-start | bytes 1572868
  27.1 30.5 %copy-start.2 = (f32[1,256,512]{2,1,0:T(8,128)S(1)}, f32[1,256,512]{2,1,0:T(8,128)}, u32[]{:S(2)}) copy-start(f32[1,256,512]{2,1,0:T(8,128)} %param.10) | copy-start | bytes 1572868
  27.1 30.5 %copy-start.3 = (f32[1,256,512]{2,1,0:T(8,128)S(1)}, f32[1,256,512]{2,1,0:T(8,128)}, u32[]{:S(2)}) copy-start(f32[1,256,512]{2,1,0:T(8,128)} %param.11) | copy-start | bytes 1572868
  27.1 30.5 %copy-start.7 = (s32[64,64]{1,0:T(8,128)S(1)}, s32[64,64]{1,0:T(8,128)}, u32[]{:S(2)}) copy-start(s32[64,64]{1,0:T(8,128)} %starts.1) | copy-start | bytes 49156
  27.1 30.4 %all-to-all-start = ((f32[64,16,128]{2,1,0:T(8,128)}), f32[64,16,128]{2,1,0:T(8,128)S(1)}, u32[]{:S(2)}, u32[]{:S(2)}) async-start(f32[64,16,128]{2,1,0:T(8,128)} %bitcast.3), calls=%async_computation | async-start | bytes 1048576 | tf_op jit(solution)/shard_map/all_to_all | solution.py:517
  40.0 47.8 %copy-start.5 = (bf16[16,128,128]{2,1,0:T(8,128)(2,1)S(1)}, bf16[16,128,128]{2,1,0:T(8,128)(2,1)}, u32[]{:S(2)}) copy-start(bf16[16,128,128]{2,1,0:T(8,128)(2,1)} %tiles.1) | copy-start | bytes 1572868
  40.0 9.8 %collective-permute-start.6 = (f32[4,8,2048]{2,1,0:T(8,128)S(1)}, f32[4,8,2048]{2,1,0:T(8,128)S(1)}, u32[]{:S(2)}, u32[]{:S(2)}) collective-permute-start(f32[4,8,2048]{2,1,0:T(8,128)S(1)} %pad_maximum_fusion), channel_id=1, source_target_pairs={{1,0},{2,1},{3,2},{5,4},{6,5},{7,6},{9,8},{10,9},{11,10},{13,12},{... | collective-permute-start | bytes 786440 | tf_op jit(solution)/shard_map/ppermute | solution.py:494
  42.8 8.6 %collective-permute-start.7 = (f32[4,8,2048]{2,1,0:T(8,128)S(1)}, f32[4,8,2048]{2,1,0:T(8,128)S(1)}, u32[]{:S(2)}, u32[]{:S(2)}) collective-permute-start(f32[4,8,2048]{2,1,0:T(8,128)S(1)} %pad_maximum_fusion.1), channel_id=1, source_target_pairs={{0,1},{1,2},{2,3},{4,5},{5,6},{6,7},{8,9},{9,10},{10,11},{12,13},{... | collective-permute-start | bytes 786440 | tf_op jit(solution)/shard_map/ppermute | solution.py:495
  58.9 30.2 %copy-start.9 = (f32[4,8,2048]{2,1,0:T(8,128)S(1)}, f32[4,8,2048]{2,1,0:T(8,128)}, u32[]{:S(2)}) copy-start(f32[4,8,2048]{2,1,0:T(8,128)} %copy-done.8) | copy-start | bytes 786436
  77.8 5.2 %collective-permute-start.9 = (bf16[1024,128]{1,0:T(8,128)(2,1)S(1)}, bf16[1024,128]{1,0:T(8,128)(2,1)S(1)}, u32[]{:S(2)}, u32[]{:S(2)}) collective-permute-start(bf16[1024,128]{1,0:T(8,128)(2,1)S(1)} %bitcast.34), channel_id=1, source_target_pairs={{0,2},{1,3},{2,0},{3,1},{4,6},{5,7},{6,4},{7,5},{8,10},{9,11},{10,... | collective-permute-start | bytes 786440 | tf_op jit(solution)/shard_map/ppermute | solution.py:529
  78.2 9.8 %collective-permute-start.8 = (bf16[1024,128]{1,0:T(8,128)(2,1)S(1)}, bf16[1024,128]{1,0:T(8,128)(2,1)S(1)}, u32[]{:S(2)}, u32[]{:S(2)}) collective-permute-start(bf16[1024,128]{1,0:T(8,128)(2,1)S(1)} %bitcast.35), channel_id=1, source_target_pairs={{0,1},{1,0},{2,3},{3,2},{4,5},{5,4},{6,7},{7,6},{8,9},{9,8},{10,11... | collective-permute-start | bytes 786440 | tf_op jit(solution)/shard_map/ppermute | solution.py:530
  83.0 6.0 %collective-permute-start.10 = (bf16[1024,128]{1,0:T(8,128)(2,1)S(1)}, bf16[1024,128]{1,0:T(8,128)(2,1)}, u32[]{:S(2)}, u32[]{:S(2)}) collective-permute-start(bf16[1024,128]{1,0:T(8,128)(2,1)S(1)} %collective-permute-done.9.b2), channel_id=1, source_target_pairs={{0,1},{1,0},{2,3},{3,2},{4,5},{5,4},{6,7},{7,6},{8,9},{9,8},{10,11... | collective-permute-start | bytes 786440 | tf_op jit(solution)/shard_map/ppermute | solution.py:531
  95.5 4.2 %collective-permute-start.11 = (bf16[88,2048]{1,0:T(8,128)(2,1)S(1)}, bf16[88,2048]{1,0:T(8,128)(2,1)S(1)}, u32[]{:S(2)}, u32[]{:S(2)}) collective-permute-start(bf16[88,2048]{1,0:T(8,128)(2,1)S(1)} %get-tuple-element.46), channel_id=1, source_target_pairs={{12,16},{28,32},{44,48},{60,64},{76,80},{92,96},{108,112},{124,128... | collective-permute-start | bytes 1081352 | tf_op jit(solution)/shard_map/ppermute | solution.py:560
  96.2 9.6 %collective-permute-start.12 = (bf16[88,2048]{1,0:T(8,128)(2,1)S(1)}, bf16[88,2048]{1,0:T(8,128)(2,1)S(1)}, u32[]{:S(2)}, u32[]{:S(2)}) collective-permute-start(bf16[88,2048]{1,0:T(8,128)(2,1)S(1)} %get-tuple-element.48), channel_id=1, source_target_pairs={{0,4},{4,8},{8,12},{16,20},{20,24},{24,28},{32,36},{36,40},{40,44}... | collective-permute-start | bytes 1081352 | tf_op jit(solution)/shard_map/ppermute | solution.py:561
  98.4 11.2 %collective-permute-start.13 = (bf16[88,2048]{1,0:T(8,128)(2,1)S(1)}, bf16[88,2048]{1,0:T(8,128)(2,1)S(1)}, u32[]{:S(2)}, u32[]{:S(2)}) collective-permute-start(bf16[88,2048]{1,0:T(8,128)(2,1)S(1)} %get-tuple-element.49), channel_id=1, source_target_pairs={{4,0},{8,4},{12,8},{20,16},{24,20},{28,24},{36,32},{40,36},{44,40}... | collective-permute-start | bytes 1081352 | tf_op jit(solution)/shard_map/ppermute | solution.py:562
  (1 other events, 0.7 us)
